TPU v7x, 32 devices: a whole 2x2x4 slice. The times are simulated.
32 devices in a mesh: parts: 2 (over y), db: 4 (over z), blk: 4 (over x, core).
Axes of the slice: x: 2, y: 2, z: 4, core: 2. Of those that a mesh axis runs over, the one named last changes fastest.
Arguments:
- queries: bfloat16 [8192, 768], P(('parts', 'db', 'blk')), parts along dimension 0, may hold values from -6 to 6
- projection: bfloat16 [768, 768], replicated, may hold values from -0.21875 to 0.21875
- vectors: bfloat16 [768, 32768], P(None, ('parts', 'db', 'blk')), parts along dimension 1, may hold values from -0.21875 to 0.21875
- bins: int32 [32768], P(('parts', 'db', 'blk')), parts along dimension 0, may hold values from 0 to 127, as said below
- routes: int32 [8192, 1], P(('parts', 'db', 'blk')), parts along dimension 0, may hold values from 0 to 3; in each aligned block of 256 rows (0 to 255, 256 to 511, ...) at most 128 rows name the same one
Outputs:
- best: float32 [8192, 128], P(('parts', 'db', 'blk')), parts along dimension 0
There are 2 independent parts, one for each index of `parts`. A program takes and returns all parts, laid end to end along the dimension named above; an argument that names none is the same for every part. Nothing has to cross between parts.
Inputs may be any that keep to these rules, and one draw needn't show every extreme that they name: Within every aligned block of 1024 entries each of the 128 bins occurs exactly 1024 // 128 times. `routes`: within every aligned block of 256 rows no group is named by more than 128 rows; in every draw some block names some group exactly 128 times.
All inputs are finite; a program needn't handle non-finite values.
Results may differ from a plain program's by a relative error of at most 0.0014.
Values may be sent and summed in bfloat16 or wider, within the bound.
No kernel may reach another device: no remote copies, remote signals or barrier semaphores. Data moves between devices by JAX's collectives and lax.ppermute only.
A program may use at most 64 MiB of HBM per device.

v0:
```python
import jax
import jax.numpy as jnp
from jax import lax
from jax.sharding import PartitionSpec as P

BINS = 128


logit_scale = 10.0


def binned_max(query_rows, columns):
    scores = jnp.dot(query_rows, columns, preferred_element_type=jnp.float32)
    return jnp.max(scores.reshape(query_rows.shape[0], -1, BINS), axis=1)


def per_device(queries, projection, vectors, bins, routes):
    groups = lax.axis_size("db")
    requests = queries.shape[0]
    capacity = 2 * requests // groups
    slab_width = vectors.shape[1]
    per_bin = slab_width // BINS
    projected = jnp.dot(queries, projection, preferred_element_type=jnp.float32)
    normed = (
        projected * lax.rsqrt(jnp.sum(projected * projected, axis=1, keepdims=True) + 1e-06)
    ).astype(jnp.bfloat16)
    target = routes[:, 0]
    one_hot = (target[:, None] == jnp.arange(groups, dtype=jnp.int32)[None, :]).astype(jnp.int32)
    slot_index = jnp.sum((jnp.cumsum(one_hot, axis=0) - one_hot) * one_hot, axis=1)
    position = target * capacity + slot_index
    chooser = (jnp.arange(groups * capacity, dtype=jnp.int32)[:, None] == position[None, :]).astype(
        jnp.bfloat16
    )
    outgoing = jnp.dot(chooser, normed, preferred_element_type=jnp.float32).astype(jnp.bfloat16)
    arrived = lax.all_to_all(outgoing, "db", split_axis=0, concat_axis=0, tiled=True)
    ordering = jnp.argsort(bins, stable=True).reshape(BINS, per_bin).T.reshape(-1)
    sorted_slab = jnp.take(vectors, ordering, axis=1)
    maxima = binned_max(arrived, lax.all_gather(sorted_slab, "blk", axis=1, tiled=True))
    answers = lax.all_to_all(logit_scale * maxima, "db", split_axis=0, concat_axis=0, tiled=True)
    return jnp.take(answers, position, axis=0)


def solution(mesh):
    in_specs = (
        P(("parts", "db", "blk"), None),
        P(),
        P(None, ("parts", "db", "blk")),
        P(("parts", "db", "blk")),
        P(("parts", "db", "blk"), None),
    )
    out_specs = P(("parts", "db", "blk"), None)
    return jax.shard_map(
        per_device, mesh=mesh, in_specs=in_specs, out_specs=out_specs, check_vma=False
    )
```

profile of v0, /device:TPU:0, one launch (start us, length us, event | category | flops | bytes accessed | tf_op | source)
XLA Modules:
  0.0 99.5 jit_solution(16236672829381784357)
XLA Ops:
  6.5 0.0 copy-start
  6.5 0.0 all-gather.2.cloned.1.call-start
  6.5 5.1 %sort.17 = (s32[1024]{0:T(1024)}, s32[1024]{0:T(1024)S(1)}) sort(s32[1024]{0:T(1024)} %param.8, s32[1024]{0:T(1024)S(1)} %iota.16), dimensions={0}, to_apply=%region_4.5 | sort | flops 10240 | bytes 16384 | tf_op jit(solution)/shard_map/jit(argsort)/sort | solution.py:36
  11.7 0.1 reshape.88
  11.9 1.7 %copy.13 = bf16[768,1024]{0,1:T(8,128)(2,1)S(1)} copy(bf16[768,1024]{1,0:T(8,128)(2,1)} %param.7) | data formatting | bytes 3145728 | tf_op args[2]
  13.6 5.2 %gather_fusion = bf16[1024,768]{1,0:T(8,128)(2,1)} fusion(bf16[768,1024]{0,1:T(8,128)(2,1)S(1)} %copy.13, s32[1024]{0:T(1024)S(1)} %broadcast_clamp_fusion), kind=kCustom, calls=%fused_computation | custom fusion | bytes 3149824 | tf_op jit(solution)/shard_map/jit(_take)/gather | solution.py:37
  18.8 2.8 %select_bitcast_fusion = bf16[768,1024]{0,1:T(8,128)(2,1)} fusion(bf16[1024,768]{1,0:T(8,128)(2,1)} %gather_fusion, pred[1024]{0:T(1024)(128)(4,1)S(1)} %compare_and_fusion), kind=kLoop, calls=%fused_computation.3 | loop fusion | flops 786432 | bytes 3146752 | tf_op jit(solution)/shard_map/jit(_take)/select_n | solution.py:37
  21.6 0.0 copy-start.2
  21.6 0.0 copy-start.1
  21.6 0.0 all-gather.2.cloned.1.call-update
  21.6 0.7 copy-done.2
  22.3 1.2 %reduce-window.6 = s32[4,2,128]{2,1,0:T(2,128)S(1)} reduce-window(s32[4,2,128]{2,1,0:T(2,128)S(1)} %compare_convert_fusion, s32[]{:T(128)} %constant.23.clone.1), window={size=1x1x128 pad=0_0x0_0x127_0}, to_apply=%region_0.0 | reduce-window | flops 130048 | bytes 8196 | tf_op jit(solution)/shard_map/reduce-window
  23.5 0.1 slice.12
  23.6 0.1 copy.9
  23.7 0.1 copy.10
  23.8 0.1 add_bitcast_fusion
  23.9 0.0 copy-done
  23.9 0.0 copy-done.1
  23.9 0.6 multiply_reduce_fusion
  24.5 0.5 convolution_convert_fusion
  25.0 26.2 %all_to_all.21 = bf16[4,128,768]{2,1,0:T(8,128)(2,1)S(1)} all-to-all(bf16[4,128,768]{2,1,0:T(8,128)(2,1)S(1)} %bitcast.46), channel_id=1, replica_groups=mesh['parts'=2,'db'=4,'blk'=4] {'db'}, dimensions={0} | all-to-all | bytes 1572864 | tf_op jit(solution)/shard_map/all_to_all | solution.py:35
  51.2 19.7 %all-gather.2.cloned.1.call-done = bf16[768,4096]{0,1:T(8,128)(2,1)} async-done(((bf16[768,1024]{0,1:T(8,128)(2,1)}), bf16[768,4096]{0,1:T(8,128)(2,1)}) %all-gather.2.cloned.1.call-update) | async-done | bytes 6291472 | tf_op jit(solution)/shard_map/all_gather | solution.py:38
  70.9 5.7 %convolution_reduce_fusion = f32[512,128]{1,0:T(8,128)S(1)} fusion(bf16[512,768,1]{1,0,2:T(8,128)(2,1)S(1)} %bitcast.47, bf16[32,128,768]{2,1,0:T(8,128)(2,1)} %bitcast.57), kind=kOutput, calls=%fused_computation.2 | convolution fusion | flops 3223257088 | bytes 7340032 | tf_op jit(solution)/shard_map/dot_general | solution.py:13
  76.5 0.7 broadcast_multiply_fusion
  77.3 4.6 %all-to-all-start.1 = ((f32[4,128,128]{2,1,0:T(8,128)}), f32[4,128,128]{2,1,0:T(8,128)S(1)}, u32[]{:S(2)}, u32[]{:S(2)}) async-start(f32[4,128,128]{2,1,0:T(8,128)} %bitcast.15), calls=%async_computation.1 | async-start | bytes 524288 | tf_op jit(solution)/shard_map/all_to_all | solution.py:39
  81.9 9.3 %all-to-all-done.1 = f32[4,128,128]{2,1,0:T(8,128)S(1)} async-done(((f32[4,128,128]{2,1,0:T(8,128)}), f32[4,128,128]{2,1,0:T(8,128)S(1)}, u32[]{:S(2)}, u32[]{:S(2)}) %all-to-all-start.1) | async-done | bytes 262176 | tf_op jit(solution)/shard_map/all_to_all | solution.py:39
  91.2 0.7 gather_fusion.1
  91.9 0.8 broadcast_select_fusion
  (13 shorter events, 0.2 us)
Async XLA Ops:
  6.5 17.4 %copy-start = (bf16[768,768]{1,0:T(8,128)(2,1)S(1)}, bf16[768,768]{1,0:T(8,128)(2,1)}, u32[]{:S(2)}) copy-start(bf16[768,768]{1,0:T(8,128)(2,1)} %param.6) | copy-start | bytes 3538948
  6.5 64.3 %all-gather.2.cloned.1.call-start = ((), (), s32[]{:S(2)}) async-start(), calls=%async_computation.2 | async-start | bytes 7864320 | tf_op jit(solution)/shard_map/all_gather | solution.py:38
  21.6 0.7 copy-start.2
  21.6 2.3 %copy-start.1 = (bf16[256,768]{1,0:T(8,128)(2,1)S(1)}, bf16[256,768]{1,0:T(8,128)(2,1)}, u32[]{:S(2)}) copy-start(bf16[256,768]{1,0:T(8,128)(2,1)} %param.5) | copy-start | bytes 1179652
  77.3 13.9 %all-to-all-start.1 = ((f32[4,128,128]{2,1,0:T(8,128)}), f32[4,128,128]{2,1,0:T(8,128)S(1)}, u32[]{:S(2)}, u32[]{:S(2)}) async-start(f32[4,128,128]{2,1,0:T(8,128)} %bitcast.15), calls=%async_computation.1 | async-start | bytes 524288 | tf_op jit(solution)/shard_map/all_to_all | solution.py:39
Sparse Core Ops, SparseCore 0:
  21.8 49.0 all-gather.1
where the time goes:
time: 99.8 us; the launch traced here: 99.5 us
  waiting for transfers between devices  29 us (29%)
  blocking collectives  26.2 us (26%)
  between operations  13.5 us (14%)
  other arithmetic  10.8 us (11%)
  local copies, waits for them, and re-layouts  8.74 us (9%)
  matrix products  6.68 us (7%)
  starting transfers between devices  4.6 us (5%)
    all_to_all x1, blocking collectives, per_device(): lax.all_to_all(outgoing, 'db', split_axis=0, concat_axis=0, tiled=True)  26.2 us
    all_gather x1, waiting for transfers between devices, per_device(): lax.all_gather(sorted_slab, 'blk', axis=1, tiled=True)  19.7 us
    all_to_all x1, waiting for transfers between devices, per_device(): lax.all_to_all(logit_scale * maxima, 'db', split_axis=0, concat_axis=0, t...  9.28 us
    dot_general x1, matrix products, binned_max(): scores = jnp.dot(query_rows, columns, preferred_element_type=jnp.float32)  5.67 us
    gather x1, local copies, waits for them, and re-layouts, per_device(): sorted_slab = jnp.take(vectors, ordering, axis=1)  5.23 us
    sort x1, other arithmetic, per_device(): jnp.argsort(bins, stable=True).reshape(BINS, per_bin).T.reshape(-1)  5.15 us
    all_to_all x1, starting transfers between devices, per_device(): lax.all_to_all(logit_scale * maxima, 'db', split_axis=0, concat_axis=0, t...  4.6 us
    select_n x2, other arithmetic, per_device(): sorted_slab = jnp.take(vectors, ordering, axis=1)  2.8 us
  transfers between devices with their start and end apart: 2, of which 2 were waited for; matrix products, arithmetic and copies ran while one was open for 3% of the time, Pallas kernels for 0%

commit v1 on v0

--- a/solution.py
+++ b/solution.py
@@ -1,12 +1,194 @@
+import functools
+
 import jax
 import jax.numpy as jnp
 from jax import lax
+from jax.experimental import pallas as pl
+from jax.experimental.pallas import tpu as pltpu
 from jax.sharding import PartitionSpec as P
 
 BINS = 128
-
-
 logit_scale = 10.0
+VMEM_LIMIT = 48 * 2**20
+
+
+def params():
+    return pltpu.CompilerParams(vmem_limit_bytes=VMEM_LIMIT)
+
+
+def cost(flops, bytes_accessed):
+    return pl.CostEstimate(flops=flops, bytes_accessed=bytes_accessed, transcendentals=0)
+
+
+def ranks(member):
+    count = member.shape[1]
+    row = lax.broadcasted_iota(jnp.int32, (count, count), 0)
+    column = lax.broadcasted_iota(jnp.int32, (count, count), 1)
+    earlier = jnp.where(row < column, 1.0, 0.0).astype(jnp.bfloat16)
+    seen = jnp.dot(member.astype(jnp.bfloat16), earlier, preferred_element_type=jnp.float32)
+    return jnp.sum(seen * member, axis=0, keepdims=True).astype(jnp.int32)
+
+
+def prepare_kernel(groups, capacity, me_ref, queries_ref, projection_ref, routes_ref, position_ref, *piece_refs):
+    requests = queries_ref.shape[0]
+    distance = jnp.bitwise_xor(routes_ref[...], me_ref[0, 0])
+    classes = lax.broadcasted_iota(jnp.int32, (-(-groups // 8) * 8, requests), 0)
+    member = jnp.where(classes == distance, 1.0, 0.0)
+    position = distance * capacity + ranks(member)
+    position_ref[...] = position
+    projected = jnp.dot(queries_ref[...], projection_ref[...], preferred_element_type=jnp.float32)
+    normed = (
+        projected * lax.rsqrt(jnp.sum(projected * projected, axis=1, keepdims=True) + 1e-06)
+    ).astype(jnp.bfloat16)
+    slots = lax.broadcasted_iota(jnp.int32, (groups * capacity, requests), 0)
+    chooser = jnp.where(slots == position, 1.0, 0.0).astype(jnp.bfloat16)
+    outgoing = jnp.dot(chooser, normed, preferred_element_type=jnp.float32).astype(jnp.bfloat16)
+    start = 0
+    for ref in piece_refs:
+        ref[...] = outgoing[start : start + ref.shape[0]]
+        start += ref.shape[0]
+
+
+def prepare(me, queries, projection, routes, groups, capacity, sizes):
+    requests, width = queries.shape
+    return pl.pallas_call(
+        functools.partial(prepare_kernel, groups, capacity),
+        out_shape=[jax.ShapeDtypeStruct((1, requests), jnp.int32)]
+        + [jax.ShapeDtypeStruct((size, width), jnp.bfloat16) for size in sizes],
+        in_specs=[pl.BlockSpec(memory_space=pltpu.SMEM)] + [pl.BlockSpec(memory_space=pltpu.VMEM)] * 3,
+        compiler_params=params(),
+        cost_estimate=cost(2 * requests * width * (width + groups * capacity), 3 * width * width),
+        name="prepare",
+    )(me.reshape(1, 1), queries, projection, routes.reshape(1, requests))
+
+
+def sort_kernel(bins_ref, vectors_ref, sorted_ref):
+    bins = bins_ref[...]
+    width = bins.shape[1]
+    classes = lax.broadcasted_iota(jnp.int32, (BINS, width), 0)
+    member = jnp.where(classes == bins, 1.0, 0.0)
+    position = ranks(member) * BINS + bins
+    places = lax.broadcasted_iota(jnp.int32, (width, width), 0)
+    chooser = jnp.where(places == position, 1.0, 0.0).astype(jnp.bfloat16)
+    sorted_ref[...] = lax.dot_general(
+        vectors_ref[...], chooser, (((1,), (1,)), ((), ())), preferred_element_type=jnp.float32
+    ).astype(jnp.bfloat16)
+
+
+def sort_slab(bins, vectors):
+    depth, width = vectors.shape
+    return pl.pallas_call(
+        sort_kernel,
+        out_shape=jax.ShapeDtypeStruct(vectors.shape, jnp.bfloat16),
+        in_specs=[pl.BlockSpec(memory_space=pltpu.VMEM)] * 2,
+        compiler_params=params(),
+        cost_estimate=cost(2 * width * width * (depth + BINS), 4 * depth * width),
+        name="sort_slab",
+    )(bins.reshape(1, width), vectors)
+
+
+def score_kernel(pieces, *refs):
+    piece_refs, slab_refs, out_refs = refs[:pieces], refs[pieces:-pieces], refs[-pieces:]
+    rows = jnp.concatenate([ref[...] for ref in piece_refs], axis=0)
+    best = None
+    step = 2 * BINS
+    for slab_ref in slab_refs:
+        for start in range(0, slab_ref.shape[1], step):
+            scores = jnp.dot(rows, slab_ref[:, start : start + step], preferred_element_type=jnp.float32)
+            for first in range(0, step, BINS):
+                part = scores[:, first : first + BINS]
+                best = part if best is None else jnp.maximum(best, part)
+    start = 0
+    for ref in out_refs:
+        ref[...] = best[start : start + ref.shape[0]]
+        start += ref.shape[0]
+
+
+def score(pieces, slabs):
+    rows = sum(piece.shape[0] for piece in pieces)
+    columns = sum(slab.shape[1] for slab in slabs)
+    width = slabs[0].shape[0]
+    return pl.pallas_call(
+        functools.partial(score_kernel, len(pieces)),
+        out_shape=[jax.ShapeDtypeStruct((piece.shape[0], BINS), jnp.float32) for piece in pieces],
+        in_specs=[pl.BlockSpec(memory_space=pltpu.VMEM)] * (len(pieces) + len(slabs)),
+        compiler_params=params(),
+        cost_estimate=cost(2 * rows * columns * width, 2 * width * (rows + columns)),
+        name="score",
+    )(*pieces, *slabs)
+
+
+def select_kernel(position_ref, *refs):
+    *answer_refs, out_ref = refs
+    half = len(answer_refs) // 2
+    answers = jnp.concatenate(
+        [jnp.maximum(a[...], b[...]) for a, b in zip(answer_refs[:half], answer_refs[half:])], axis=0
+    )
+    high = answers.astype(jnp.bfloat16)
+    rest = answers - high.astype(jnp.float32)
+    middle = rest.astype(jnp.bfloat16)
+    low = (rest - middle.astype(jnp.float32)).astype(jnp.bfloat16)
+    parts = jnp.concatenate([high, middle, low], axis=1)
+    position = position_ref[...]
+    slots = lax.broadcasted_iota(jnp.int32, (answers.shape[0], position.shape[1]), 0)
+    chooser = jnp.where(slots == position, 1.0, 0.0).astype(jnp.bfloat16)
+    chosen = lax.dot_general(chooser, parts, (((0,), (0,)), ((), ())), preferred_element_type=jnp.float32)
+    total = (chosen[:, :BINS] + chosen[:, BINS : 2 * BINS]) + chosen[:, 2 * BINS :]
+    out_ref[...] = logit_scale * total
+
+
+def select(position, first, second):
+    requests = position.shape[1]
+    slots = sum(a.shape[0] for a in first)
+    return pl.pallas_call(
+        select_kernel,
+        out_shape=jax.ShapeDtypeStruct((requests, BINS), jnp.float32),
+        in_specs=[pl.BlockSpec(memory_space=pltpu.VMEM)] * (1 + len(first) + len(second)),
+        compiler_params=params(),
+        cost_estimate=cost(6 * requests * slots * BINS, 8 * slots * BINS),
+        name="select",
+    )(position, *first, *second)
+
+
+def device_paired(queries, projection, vectors, bins, routes):
+    groups, slabs = lax.axis_size("db"), lax.axis_size("blk")
+    requests = queries.shape[0]
+    capacity = 2 * requests // groups
+    me = lax.axis_index("db")
+
+    def along_db(value, distance):
+        return lax.ppermute(value, "db", [(i, i ^ distance) for i in range(groups)])
+
+    def along_blk(value, distance):
+        return lax.ppermute(value, "blk", [(i, i ^ distance) for i in range(slabs)])
+
+    def along_both(value, distance, distance_blk):
+        pairs = [
+            (i * slabs + j, (i ^ distance) * slabs + (j ^ distance_blk))
+            for i in range(groups)
+            for j in range(slabs)
+        ]
+        return lax.ppermute(value, ("db", "blk"), pairs)
+
+    position, *pieces = prepare(me, queries, projection, routes, groups, capacity, [capacity] * groups)
+    order = [3, 1, 2]
+    arrived = {0: pieces[0]}
+    for distance in order:
+        arrived[distance] = along_db(pieces[distance], distance)
+    own_slab = sort_slab(bins, vectors)
+    both_slabs = (own_slab, along_blk(own_slab, 1))
+    first, second = {}, {}
+    for distance in [0, 1, 3, 2]:
+        partner = along_blk(arrived[distance], 2)
+        here, there = score([arrived[distance], partner], both_slabs)
+        if distance:
+            first[distance] = along_db(here, distance)
+            second[distance] = along_both(there, distance, 2)
+        else:
+            first[distance] = here
+            second[distance] = along_blk(there, 2)
+    ids = range(groups)
+    return select(position, [first[k] for k in ids], [second[k] for k in ids])
 
 
 def binned_max(query_rows, columns):
@@ -14,7 +196,7 @@
     return jnp.max(scores.reshape(query_rows.shape[0], -1, BINS), axis=1)
 
 
-def per_device(queries, projection, vectors, bins, routes):
+def device_gathered(queries, projection, vectors, bins, routes):
     groups = lax.axis_size("db")
     requests = queries.shape[0]
     capacity = 2 * requests // groups
@@ -41,6 +223,7 @@
 
 
 def solution(mesh):
+    paired = mesh.shape["db"] == 4 and mesh.shape["blk"] == 4
     in_specs = (
         P(("parts", "db", "blk"), None),
         P(),
@@ -50,5 +233,9 @@
     )
     out_specs = P(("parts", "db", "blk"), None)
     return jax.shard_map(
-        per_device, mesh=mesh, in_specs=in_specs, out_specs=out_specs, check_vma=False
-    )
+        device_paired if paired else device_gathered,
+        mesh=mesh,
+        in_specs=in_specs,
+        out_specs=out_specs,
+        check_vma=False,
+    )

time: 99.8 us -> 56.4 us (0.57)
  blocking collectives: 26.2 us -> 0 us
  starting transfers between devices: 4.6 us -> 24.8 us
  between operations: 13.5 us -> 0.07 us
  other arithmetic: 10.8 us -> 0 us
  waiting for transfers between devices: 29 us -> 19.8 us
  Pallas kernels: 0 us -> 8.19 us
  matrix products: 6.68 us -> 0 us
  local copies, waits for them, and re-layouts: 8.74 us -> 3.37 us
    all_to_all x1 -> x0, blocking collectives: 26.2 us -> none  [per_device(): lax.all_to_all(outgoing, 'db', split_axis=0, concat_axis=0, tiled=True)]
    ppermute x0 -> x15, starting transfers between devices: none -> 24.8 us  [the longest x6 12.6 us: along_db(): return lax.ppermute(value, 'db', [(i, i ^ distance) for i in range(groups)])]
    ppermute x0 -> x15, waiting for transfers between devices: none -> 19.8 us  [the longest x6 16.2 us: along_db(): return lax.ppermute(value, 'db', [(i, i ^ distance) for i in range(groups)])]
    all_gather x1 -> x0, waiting for transfers between devices: 19.7 us -> none  [per_device(): lax.all_gather(sorted_slab, 'blk', axis=1, tiled=True)]
    all_to_all x1 -> x0, waiting for transfers between devices: 9.28 us -> none  [per_device(): lax.all_to_all(logit_scale * maxima, 'db', split_axis=0, concat_axis=0, t...]
    pallas_call x0 -> x7, Pallas kernels: none -> 8.19 us  [the longest x4 3.97 us: score(): pl.pallas_call(functools.partial(score_kernel, len(pieces)), out_shape=[j...]
    dot_general x3 -> x0, matrix products: 6.68 us -> none  [the longest x1 5.67 us: binned_max(): scores = jnp.dot(query_rows, columns, preferred_element_type=jnp.float32)]
    gather x2 -> x0, local copies, waits for them, and re-layouts: 5.96 us -> none  [the longest x1 5.23 us: per_device(): sorted_slab = jnp.take(vectors, ordering, axis=1)]
  transfers between devices with their start and end apart: 2 -> 15, of which waited for: 2 -> 7; matrix products, arithmetic and copies ran while one was open for 3% -> 0% of each run, Pallas kernels for 0% -> 9%
where the time goes in v1:
time: 56.4 us; the launch traced here: 56.2 us
  starting transfers between devices  24.8 us (44%)
  waiting for transfers between devices  19.8 us (35%)
  Pallas kernels  8.19 us (15%)
  local copies, waits for them, and re-layouts  3.37 us (6%)
    ppermute x6, waiting for transfers between devices, along_db(): return lax.ppermute(value, 'db', [(i, i ^ distance) for i in range(groups)])  16.2 us
    ppermute x6, starting transfers between devices, along_db(): return lax.ppermute(value, 'db', [(i, i ^ distance) for i in range(groups)])  12.6 us
    ppermute x6, starting transfers between devices, along_blk(): return lax.ppermute(value, 'blk', [(i, i ^ distance) for i in range(slabs)])  6.22 us
    ppermute x3, starting transfers between devices, along_both(): return lax.ppermute(value, ('db', 'blk'), pairs)  5.96 us
    pallas_call x4, Pallas kernels, score(): pl.pallas_call(functools.partial(score_kernel, len(pieces)), out_shape=[j...  3.97 us
    unnamed x10, local copies, waits for them, and re-layouts  3.37 us
    ppermute x6, waiting for transfers between devices, along_blk(): return lax.ppermute(value, 'blk', [(i, i ^ distance) for i in range(slabs)])  2.47 us
    pallas_call x1, Pallas kernels, sort_slab(): pl.pallas_call(sort_kernel, out_shape=jax.ShapeDtypeStruct(vectors.shape,...  2.15 us
  transfers between devices with their start and end apart: 15, of which 7 were waited for; matrix products, arithmetic and copies ran while one was open for 0% of the time, Pallas kernels for 9%

profile of v1, /device:TPU:0, one launch (start us, length us, event | category | flops | bytes accessed | tf_op | source)
XLA Modules:
  0.0 56.2 jit_solution(17156742665202813416)
XLA Ops:
  0.0 0.0 copy-start
  0.0 1.4 %copy-done = bf16[768,1024]{1,0:T(8,128)(2,1)S(1)} copy-done((bf16[768,1024]{1,0:T(8,128)(2,1)S(1)}, bf16[768,1024]{1,0:T(8,128)(2,1)}, u32[]{:S(2)}) %copy-start) | copy-done | bytes 1572888
  1.4 0.0 copy-start.3
  1.4 0.7 %copy-done.3 = s32[1024]{0:T(1024)S(1)} copy-done((s32[1024]{0:T(1024)S(1)}, s32[1024]{0:T(1024)}, u32[]{:S(2)}) %copy-start.3) | copy-done | bytes 4120
  2.1 0.0 copy-start.2
  2.1 0.0 copy-start.4
  2.1 2.2 %sort_slab.1.refs_2_ = bf16[768,1024]{1,0:T(8,128)(2,1)S(1)} custom-call(s32[1,1024]{1,0:T(1,128)S(1)} %bitcast.3, bf16[768,1024]{1,0:T(8,128)(2,1)S(1)} %copy-done), custom_call_target="tpu_custom_call" | custom-call | flops 1879048192 | bytes 3145728 | tf_op jit(solution)/shard_map/sort_slab/pallas_call | solution.py:80
  4.3 0.5 collective-permute-start.1
  4.8 0.0 copy-done.2
  4.8 0.0 copy-done.4
  4.8 0.0 copy-start.1
  4.8 1.3 %copy-done.1 = bf16[768,768]{1,0:T(8,128)(2,1)S(1)} copy-done((bf16[768,768]{1,0:T(8,128)(2,1)S(1)}, bf16[768,768]{1,0:T(8,128)(2,1)}, u32[]{:S(2)}) %copy-start.1) | copy-done | bytes 1179672
  6.1 1.1 %prepare.1 = (s32[1,256]{1,0:T(1,128)S(1)}, bf16[128,768]{1,0:T(8,128)(2,1)S(1)}, bf16[128,768]{1,0:T(8,128)(2,1)S(1)}, bf16[128,768]{1,0:T(8,128)(2,1)S(1)}, bf16[128,768]{1,0:T(8,128)(2,1)S(1)}) custom-call(s32[1,1]{1,0:T(1,128)} %bitcast.me_ref, bf16[256,768]{1,0:T(8,128)(2,1)S(1)} %copy-done.2, bf16[768,768]{1,0:T(8,128)(2,1)S(1)} %copy-done.1, ...), custom_call_target="tpu_custom_call" | custom-call | flops 503316480 | bytes 1769472 | tf_op jit(solution)/shard_map/prepare/pallas_call | solution.py:54
  7.2 4.7 %collective-permute-start.8 = (bf16[128,768]{1,0:T(8,128)(2,1)S(1)}, bf16[128,768]{1,0:T(8,128)(2,1)S(1)}, u32[]{:S(2)}, u32[]{:S(2)}) collective-permute-start(bf16[128,768]{1,0:T(8,128)(2,1)S(1)} %get-tuple-element.25), channel_id=1, source_target_pairs={{0,12},{4,8},{8,4},{12,0},{1,13},{5,9},{9,5},{13,1},{2,14},{6,10},... | collective-permute-start | bytes 589832 | tf_op jit(solution)/shard_map/ppermute | solution.py:160
  11.9 0.0 collective-permute-start.5
  11.9 0.6 %collective-permute-start.2 = (bf16[128,768]{1,0:T(8,128)(2,1)S(1)}, bf16[128,768]{1,0:T(8,128)(2,1)S(1)}, u32[]{:S(2)}, u32[]{:S(2)}) collective-permute-start(bf16[128,768]{1,0:T(8,128)(2,1)S(1)} %get-tuple-element.21), channel_id=1, source_target_pairs={{0,4},{4,0},{8,12},{12,8},{1,5},{5,1},{9,13},{13,9},{2,6},{6,2},{1... | collective-permute-start | bytes 589832 | tf_op jit(solution)/shard_map/ppermute | solution.py:160
  12.5 5.3 %collective-permute-done.8.refs_0_ = bf16[128,768]{1,0:T(8,128)(2,1)S(1)} collective-permute-done((bf16[128,768]{1,0:T(8,128)(2,1)S(1)}, bf16[128,768]{1,0:T(8,128)(2,1)S(1)}, u32[]{:S(2)}, u32[]{:S(2)}) %collective-permute-start.8) | collective-permute-done | bytes 196640 | tf_op jit(solution)/shard_map/ppermute | solution.py:160
  17.8 1.6 %collective-permute-start.9 = (bf16[128,768]{1,0:T(8,128)(2,1)S(1)}, bf16[128,768]{1,0:T(8,128)(2,1)S(1)}, u32[]{:S(2)}, u32[]{:S(2)}) collective-permute-start(bf16[128,768]{1,0:T(8,128)(2,1)S(1)} %collective-permute-done.8.refs_0_), channel_id=1, source_target_pairs={{0,2},{1,3},{2,0},{3,1},{4,6},{5,7},{6,4},{7,5},{8,10},{9,11},{10,... | collective-permute-start | bytes 589832 | tf_op jit(solution)/shard_map/ppermute | solution.py:163
  19.4 9.8 %collective-permute-done.5.refs_0_ = bf16[128,768]{1,0:T(8,128)(2,1)S(1)} collective-permute-done((bf16[128,768]{1,0:T(8,128)(2,1)S(1)}, bf16[128,768]{1,0:T(8,128)(2,1)S(1)}, u32[]{:S(2)}, u32[]{:S(2)}) %collective-permute-start.5) | collective-permute-done | bytes 196640 | tf_op jit(solution)/shard_map/ppermute | solution.py:160
  29.2 1.5 %collective-permute-start.6 = (bf16[128,768]{1,0:T(8,128)(2,1)S(1)}, bf16[128,768]{1,0:T(8,128)(2,1)S(1)}, u32[]{:S(2)}, u32[]{:S(2)}) collective-permute-start(bf16[128,768]{1,0:T(8,128)(2,1)S(1)} %collective-permute-done.5.refs_0_), channel_id=1, source_target_pairs={{0,2},{1,3},{2,0},{3,1},{4,6},{5,7},{6,4},{7,5},{8,10},{9,11},{10,... | collective-permute-start | bytes 589832 | tf_op jit(solution)/shard_map/ppermute | solution.py:163
  30.7 0.0 collective-permute-done.2.refs_0_
  30.7 0.5 collective-permute-start.3
  31.2 1.5 %collective-permute-start = (bf16[128,768]{1,0:T(8,128)(2,1)S(1)}, bf16[128,768]{1,0:T(8,128)(2,1)S(1)}, u32[]{:S(2)}, u32[]{:S(2)}) collective-permute-start(bf16[128,768]{1,0:T(8,128)(2,1)S(1)} %get-tuple-element.19.refs_0_), channel_id=1, source_target_pairs={{0,2},{1,3},{2,0},{3,1},{4,6},{5,7},{6,4},{7,5},{8,10},{9,11},{10,... | collective-permute-start | bytes 589832 | tf_op jit(solution)/shard_map/ppermute | solution.py:163
  32.7 0.0 collective-permute-done.9.refs_1_
  32.7 0.0 collective-permute-done.1.refs_3_
  32.7 1.0 %score.7 = (f32[128,128]{1,0:T(8,128)S(1)}, f32[128,128]{1,0:T(8,128)S(1)}) custom-call(bf16[128,768]{1,0:T(8,128)(2,1)S(1)} %collective-permute-done.8.refs_0_, bf16[128,768]{1,0:T(8,128)(2,1)S(1)} %collective-permute-done.9.refs_1_, bf16[768,1024]{1,0:T(8,128)(2,1)S(1)} %sort_slab.1.refs_2_, bf16[768,1024]{1,0:T(8,128)(2,1)S(1)} %collective-permute-done.1.refs_3_), custom_call_target="tpu_custom_call" | custom-call | flops 805306368 | bytes 3538944 | tf_op jit(solution)/shard_map/score/pallas_call | solution.py:111
  33.7 2.5 %collective-permute-start.10 = (f32[128,128]{1,0:T(8,128)S(1)}, f32[128,128]{1,0:T(8,128)S(1)}, u32[]{:S(2)}, u32[]{:S(2)}) collective-permute-start(f32[128,128]{1,0:T(8,128)S(1)} %get-tuple-element.26), channel_id=1, source_target_pairs={{0,12},{4,8},{8,4},{12,0},{1,13},{5,9},{9,5},{13,1},{2,14},{6,10},... | collective-permute-start | bytes 196616 | tf_op jit(solution)/shard_map/ppermute | solution.py:160
  36.2 1.3 %collective-permute-start.14 = (f32[128,128]{1,0:T(8,128)S(1)}, f32[128,128]{1,0:T(8,128)S(1)}, u32[]{:S(2)}, u32[]{:S(2)}) collective-permute-start(f32[128,128]{1,0:T(8,128)S(1)} %get-tuple-element.30), channel_id=1, source_target_pairs={{0,14},{1,15},{2,12},{3,13},{4,10},{5,11},{6,8},{7,9},{8,6},{9,7},... | collective-permute-start | bytes 196616 | tf_op jit(solution)/shard_map/ppermute | solution.py:171
  37.5 0.0 collective-permute-done.6.refs_1_
  37.5 1.0 %score.6 = (f32[128,128]{1,0:T(8,128)S(1)}, f32[128,128]{1,0:T(8,128)S(1)}) custom-call(bf16[128,768]{1,0:T(8,128)(2,1)S(1)} %collective-permute-done.5.refs_0_, bf16[128,768]{1,0:T(8,128)(2,1)S(1)} %collective-permute-done.6.refs_1_, bf16[768,1024]{1,0:T(8,128)(2,1)S(1)} %sort_slab.1.refs_2_, bf16[768,1024]{1,0:T(8,128)(2,1)S(1)} %collective-permute-done.1.refs_3_), custom_call_target="tpu_custom_call" | custom-call | flops 805306368 | bytes 3538944 | tf_op jit(solution)/shard_map/score/pallas_call | solution.py:111
  38.6 3.1 %collective-permute-start.13 = (f32[128,128]{1,0:T(8,128)S(1)}, f32[128,128]{1,0:T(8,128)S(1)}, u32[]{:S(2)}, u32[]{:S(2)}) collective-permute-start(f32[128,128]{1,0:T(8,128)S(1)} %get-tuple-element.29), channel_id=1, source_target_pairs={{0,10},{1,11},{2,8},{3,9},{4,14},{5,15},{6,12},{7,13},{8,2},{9,3},... | collective-permute-start | bytes 196616 | tf_op jit(solution)/shard_map/ppermute | solution.py:171
  41.7 0.2 collective-permute-done.3.refs_1_
  41.9 3.2 %collective-permute-start.7 = (f32[128,128]{1,0:T(8,128)S(1)}, f32[128,128]{1,0:T(8,128)S(1)}, u32[]{:S(2)}, u32[]{:S(2)}) collective-permute-start(f32[128,128]{1,0:T(8,128)S(1)} %get-tuple-element.24), channel_id=1, source_target_pairs={{0,8},{4,12},{8,0},{12,4},{1,9},{5,13},{9,1},{13,5},{2,10},{6,14},... | collective-permute-start | bytes 196616 | tf_op jit(solution)/shard_map/ppermute | solution.py:160
  45.1 1.0 %score.5 = (f32[128,128]{1,0:T(8,128)S(1)}, f32[128,128]{1,0:T(8,128)S(1)}) custom-call(bf16[128,768]{1,0:T(8,128)(2,1)S(1)} %collective-permute-done.2.refs_0_, bf16[128,768]{1,0:T(8,128)(2,1)S(1)} %collective-permute-done.3.refs_1_, bf16[768,1024]{1,0:T(8,128)(2,1)S(1)} %sort_slab.1.refs_2_, bf16[768,1024]{1,0:T(8,128)(2,1)S(1)} %collective-permute-done.1.refs_3_), custom_call_target="tpu_custom_call" | custom-call | flops 805306368 | bytes 3538944 | tf_op jit(solution)/shard_map/score/pallas_call | solution.py:111
  46.1 0.8 %collective-permute-done.refs_1_ = bf16[128,768]{1,0:T(8,128)(2,1)S(1)} collective-permute-done((bf16[128,768]{1,0:T(8,128)(2,1)S(1)}, bf16[128,768]{1,0:T(8,128)(2,1)S(1)}, u32[]{:S(2)}, u32[]{:S(2)}) %collective-permute-start) | collective-permute-done | bytes 196640 | tf_op jit(solution)/shard_map/ppermute | solution.py:163
  46.9 1.5 %collective-permute-start.12 = (f32[128,128]{1,0:T(8,128)S(1)}, f32[128,128]{1,0:T(8,128)S(1)}, u32[]{:S(2)}, u32[]{:S(2)}) collective-permute-start(f32[128,128]{1,0:T(8,128)S(1)} %get-tuple-element.28), channel_id=1, source_target_pairs={{0,6},{1,7},{2,4},{3,5},{4,2},{5,3},{6,0},{7,1},{8,14},{9,15},{10,... | collective-permute-start | bytes 196616 | tf_op jit(solution)/shard_map/ppermute | solution.py:171
  48.4 1.0 %score.4 = (f32[128,128]{1,0:T(8,128)S(1)}, f32[128,128]{1,0:T(8,128)S(1)}) custom-call(bf16[128,768]{1,0:T(8,128)(2,1)S(1)} %get-tuple-element.19.refs_0_, bf16[128,768]{1,0:T(8,128)(2,1)S(1)} %collective-permute-done.refs_1_, bf16[768,1024]{1,0:T(8,128)(2,1)S(1)} %sort_slab.1.refs_2_, bf16[768,1024]{1,0:T(8,128)(2,1)S(1)} %collective-permute-done.1.refs_3_), custom_call_target="tpu_custom_call" | custom-call | flops 805306368 | bytes 3538944 | tf_op jit(solution)/shard_map/score/pallas_call | solution.py:111
  49.4 0.0 collective-permute-done.10.refs_3_
  49.4 1.5 %collective-permute-start.4 = (f32[128,128]{1,0:T(8,128)S(1)}, f32[128,128]{1,0:T(8,128)S(1)}, u32[]{:S(2)}, u32[]{:S(2)}) collective-permute-start(f32[128,128]{1,0:T(8,128)S(1)} %get-tuple-element.22), channel_id=1, source_target_pairs={{0,4},{4,0},{8,12},{12,8},{1,5},{5,1},{9,13},{13,9},{2,6},{6,2},{1... | collective-permute-start | bytes 196616 | tf_op jit(solution)/shard_map/ppermute | solution.py:160
  50.9 0.0 collective-permute-done.14.refs_7_
  50.9 0.5 collective-permute-start.11
  51.5 0.0 collective-permute-done.13.refs_6_
  51.5 0.0 collective-permute-done.7.refs_2_
  51.5 1.1 %collective-permute-done.12.refs_5_ = f32[128,128]{1,0:T(8,128)S(1)} collective-permute-done((f32[128,128]{1,0:T(8,128)S(1)}, f32[128,128]{1,0:T(8,128)S(1)}, u32[]{:S(2)}, u32[]{:S(2)}) %collective-permute-start.12) | collective-permute-done | bytes 65568 | tf_op jit(solution)/shard_map/ppermute | solution.py:171
  52.5 1.2 %collective-permute-done.4.refs_1_ = f32[128,128]{1,0:T(8,128)S(1)} collective-permute-done((f32[128,128]{1,0:T(8,128)S(1)}, f32[128,128]{1,0:T(8,128)S(1)}, u32[]{:S(2)}, u32[]{:S(2)}) %collective-permute-start.4) | collective-permute-done | bytes 65568 | tf_op jit(solution)/shard_map/ppermute | solution.py:160
  53.7 1.5 %collective-permute-done.11.refs_4_ = f32[128,128]{1,0:T(8,128)S(1)} collective-permute-done((f32[128,128]{1,0:T(8,128)S(1)}, f32[128,128]{1,0:T(8,128)S(1)}, u32[]{:S(2)}, u32[]{:S(2)}) %collective-permute-start.11) | collective-permute-done | bytes 65568 | tf_op jit(solution)/shard_map/ppermute | solution.py:163
  55.2 1.0 %select.1 = f32[256,128]{1,0:T(8,128)} custom-call(s32[1,256]{1,0:T(1,128)S(1)} %get-tuple-element.18.position_ref, f32[128,128]{1,0:T(8,128)S(1)} %get-tuple-element.20.refs_0_, f32[128,128]{1,0:T(8,128)S(1)} %collective-permute-done.4.refs_1_, f32[128,128]{1,0:T(8,128)S(1)} %collective-permute-done.7.refs_2_, ...), custom_call_target="tpu_custom_call" | custom-call | flops 100663296 | bytes 524288 | tf_op jit(solution)/shard_map/select/pallas_call | solution.py:143
Async XLA Ops:
  0.0 1.4 %copy-start = (bf16[768,1024]{1,0:T(8,128)(2,1)S(1)}, bf16[768,1024]{1,0:T(8,128)(2,1)}, u32[]{:S(2)}) copy-start(bf16[768,1024]{1,0:T(8,128)(2,1)} %vectors_ref.1) | copy-start | bytes 4718596
  1.4 0.7 %copy-start.3 = (s32[1024]{0:T(1024)S(1)}, s32[1024]{0:T(1024)}, u32[]{:S(2)}) copy-start(s32[1024]{0:T(1024)} %param.8) | copy-start | bytes 12292
  2.1 2.7 %copy-start.2 = (bf16[256,768]{1,0:T(8,128)(2,1)S(1)}, bf16[256,768]{1,0:T(8,128)(2,1)}, u32[]{:S(2)}) copy-start(bf16[256,768]{1,0:T(8,128)(2,1)} %queries_ref.1) | copy-start | bytes 1179652
  2.1 2.7 %copy-start.4 = (s32[256,1]{0,1:T(1,128)S(1)}, s32[256,1]{0,1:T(1,128)}, u32[]{:S(2)}) copy-start(s32[256,1]{0,1:T(1,128)} %param.9) | copy-start | bytes 3076
  4.3 28.4 %collective-permute-start.1 = (bf16[768,1024]{1,0:T(8,128)(2,1)S(1)}, bf16[768,1024]{1,0:T(8,128)(2,1)S(1)}, u32[]{:S(2)}, u32[]{:S(2)}) collective-permute-start(bf16[768,1024]{1,0:T(8,128)(2,1)S(1)} %sort_slab.1.refs_2_), channel_id=1, source_target_pairs={{0,1},{1,0},{2,3},{3,2},{4,5},{5,4},{6,7},{7,6},{8,9},{9,8},{10,11... | collective-permute-start | bytes 4718600 | tf_op jit(solution)/shard_map/ppermute | solution.py:163
  4.8 1.3 %copy-start.1 = (bf16[768,768]{1,0:T(8,128)(2,1)S(1)}, bf16[768,768]{1,0:T(8,128)(2,1)}, u32[]{:S(2)}) copy-start(bf16[768,768]{1,0:T(8,128)(2,1)} %projection_ref.1) | copy-start | bytes 3538948
  7.2 10.6 %collective-permute-start.8 = (bf16[128,768]{1,0:T(8,128)(2,1)S(1)}, bf16[128,768]{1,0:T(8,128)(2,1)S(1)}, u32[]{:S(2)}, u32[]{:S(2)}) collective-permute-start(bf16[128,768]{1,0:T(8,128)(2,1)S(1)} %get-tuple-element.25), channel_id=1, source_target_pairs={{0,12},{4,8},{8,4},{12,0},{1,13},{5,9},{9,5},{13,1},{2,14},{6,10},... | collective-permute-start | bytes 589832 | tf_op jit(solution)/shard_map/ppermute | solution.py:160
  11.9 17.3 %collective-permute-start.5 = (bf16[128,768]{1,0:T(8,128)(2,1)S(1)}, bf16[128,768]{1,0:T(8,128)(2,1)S(1)}, u32[]{:S(2)}, u32[]{:S(2)}) collective-permute-start(bf16[128,768]{1,0:T(8,128)(2,1)S(1)} %get-tuple-element.23), channel_id=1, source_target_pairs={{0,8},{4,12},{8,0},{12,4},{1,9},{5,13},{9,1},{13,5},{2,10},{6,14},... | collective-permute-start | bytes 589832 | tf_op jit(solution)/shard_map/ppermute | solution.py:160
  11.9 18.8 %collective-permute-start.2 = (bf16[128,768]{1,0:T(8,128)(2,1)S(1)}, bf16[128,768]{1,0:T(8,128)(2,1)S(1)}, u32[]{:S(2)}, u32[]{:S(2)}) collective-permute-start(bf16[128,768]{1,0:T(8,128)(2,1)S(1)} %get-tuple-element.21), channel_id=1, source_target_pairs={{0,4},{4,0},{8,12},{12,8},{1,5},{5,1},{9,13},{13,9},{2,6},{6,2},{1... | collective-permute-start | bytes 589832 | tf_op jit(solution)/shard_map/ppermute | solution.py:160
  17.8 14.9 %collective-permute-start.9 = (bf16[128,768]{1,0:T(8,128)(2,1)S(1)}, bf16[128,768]{1,0:T(8,128)(2,1)S(1)}, u32[]{:S(2)}, u32[]{:S(2)}) collective-permute-start(bf16[128,768]{1,0:T(8,128)(2,1)S(1)} %collective-permute-done.8.refs_0_), channel_id=1, source_target_pairs={{0,2},{1,3},{2,0},{3,1},{4,6},{5,7},{6,4},{7,5},{8,10},{9,11},{10,... | collective-permute-start | bytes 589832 | tf_op jit(solution)/shard_map/ppermute | solution.py:163
  29.2 8.4 %collective-permute-start.6 = (bf16[128,768]{1,0:T(8,128)(2,1)S(1)}, bf16[128,768]{1,0:T(8,128)(2,1)S(1)}, u32[]{:S(2)}, u32[]{:S(2)}) collective-permute-start(bf16[128,768]{1,0:T(8,128)(2,1)S(1)} %collective-permute-done.5.refs_0_), channel_id=1, source_target_pairs={{0,2},{1,3},{2,0},{3,1},{4,6},{5,7},{6,4},{7,5},{8,10},{9,11},{10,... | collective-permute-start | bytes 589832 | tf_op jit(solution)/shard_map/ppermute | solution.py:163
  30.7 11.2 %collective-permute-start.3 = (bf16[128,768]{1,0:T(8,128)(2,1)S(1)}, bf16[128,768]{1,0:T(8,128)(2,1)S(1)}, u32[]{:S(2)}, u32[]{:S(2)}) collective-permute-start(bf16[128,768]{1,0:T(8,128)(2,1)S(1)} %collective-permute-done.2.refs_0_), channel_id=1, source_target_pairs={{0,2},{1,3},{2,0},{3,1},{4,6},{5,7},{6,4},{7,5},{8,10},{9,11},{10,... | collective-permute-start | bytes 589832 | tf_op jit(solution)/shard_map/ppermute | solution.py:163
  31.2 15.7 %collective-permute-start = (bf16[128,768]{1,0:T(8,128)(2,1)S(1)}, bf16[128,768]{1,0:T(8,128)(2,1)S(1)}, u32[]{:S(2)}, u32[]{:S(2)}) collective-permute-start(bf16[128,768]{1,0:T(8,128)(2,1)S(1)} %get-tuple-element.19.refs_0_), channel_id=1, source_target_pairs={{0,2},{1,3},{2,0},{3,1},{4,6},{5,7},{6,4},{7,5},{8,10},{9,11},{10,... | collective-permute-start | bytes 589832 | tf_op jit(solution)/shard_map/ppermute | solution.py:163
  33.7 15.7 %collective-permute-start.10 = (f32[128,128]{1,0:T(8,128)S(1)}, f32[128,128]{1,0:T(8,128)S(1)}, u32[]{:S(2)}, u32[]{:S(2)}) collective-permute-start(f32[128,128]{1,0:T(8,128)S(1)} %get-tuple-element.26), channel_id=1, source_target_pairs={{0,12},{4,8},{8,4},{12,0},{1,13},{5,9},{9,5},{13,1},{2,14},{6,10},... | collective-permute-start | bytes 196616 | tf_op jit(solution)/shard_map/ppermute | solution.py:160
  36.2 14.7 %collective-permute-start.14 = (f32[128,128]{1,0:T(8,128)S(1)}, f32[128,128]{1,0:T(8,128)S(1)}, u32[]{:S(2)}, u32[]{:S(2)}) collective-permute-start(f32[128,128]{1,0:T(8,128)S(1)} %get-tuple-element.30), channel_id=1, source_target_pairs={{0,14},{1,15},{2,12},{3,13},{4,10},{5,11},{6,8},{7,9},{8,6},{9,7},... | collective-permute-start | bytes 196616 | tf_op jit(solution)/shard_map/ppermute | solution.py:171
  38.6 12.9 %collective-permute-start.13 = (f32[128,128]{1,0:T(8,128)S(1)}, f32[128,128]{1,0:T(8,128)S(1)}, u32[]{:S(2)}, u32[]{:S(2)}) collective-permute-start(f32[128,128]{1,0:T(8,128)S(1)} %get-tuple-element.29), channel_id=1, source_target_pairs={{0,10},{1,11},{2,8},{3,9},{4,14},{5,15},{6,12},{7,13},{8,2},{9,3},... | collective-permute-start | bytes 196616 | tf_op jit(solution)/shard_map/ppermute | solution.py:171
  41.9 9.6 %collective-permute-start.7 = (f32[128,128]{1,0:T(8,128)S(1)}, f32[128,128]{1,0:T(8,128)S(1)}, u32[]{:S(2)}, u32[]{:S(2)}) collective-permute-start(f32[128,128]{1,0:T(8,128)S(1)} %get-tuple-element.24), channel_id=1, source_target_pairs={{0,8},{4,12},{8,0},{12,4},{1,9},{5,13},{9,1},{13,5},{2,10},{6,14},... | collective-permute-start | bytes 196616 | tf_op jit(solution)/shard_map/ppermute | solution.py:160
  46.9 5.6 %collective-permute-start.12 = (f32[128,128]{1,0:T(8,128)S(1)}, f32[128,128]{1,0:T(8,128)S(1)}, u32[]{:S(2)}, u32[]{:S(2)}) collective-permute-start(f32[128,128]{1,0:T(8,128)S(1)} %get-tuple-element.28), channel_id=1, source_target_pairs={{0,6},{1,7},{2,4},{3,5},{4,2},{5,3},{6,0},{7,1},{8,14},{9,15},{10,... | collective-permute-start | bytes 196616 | tf_op jit(solution)/shard_map/ppermute | solution.py:171
  49.4 4.3 %collective-permute-start.4 = (f32[128,128]{1,0:T(8,128)S(1)}, f32[128,128]{1,0:T(8,128)S(1)}, u32[]{:S(2)}, u32[]{:S(2)}) collective-permute-start(f32[128,128]{1,0:T(8,128)S(1)} %get-tuple-element.22), channel_id=1, source_target_pairs={{0,4},{4,0},{8,12},{12,8},{1,5},{5,1},{9,13},{13,9},{2,6},{6,2},{1... | collective-permute-start | bytes 196616 | tf_op jit(solution)/shard_map/ppermute | solution.py:160
  50.9 4.3 %collective-permute-start.11 = (f32[128,128]{1,0:T(8,128)S(1)}, f32[128,128]{1,0:T(8,128)S(1)}, u32[]{:S(2)}, u32[]{:S(2)}) collective-permute-start(f32[128,128]{1,0:T(8,128)S(1)} %get-tuple-element.27), channel_id=1, source_target_pairs={{0,2},{1,3},{2,0},{3,1},{4,6},{5,7},{6,4},{7,5},{8,10},{9,11},{10,... | collective-permute-start | bytes 196616 | tf_op jit(solution)/shard_map/ppermute | solution.py:163

commit v2 on v1

--- a/solution.py
+++ b/solution.py
@@ -9,6 +9,9 @@
 
 BINS = 128
 logit_scale = 10.0
+ORDER = (3, 1, 2)
+PREP_LIMIT = 63 * 2**20
+NO_COST = pl.CostEstimate(flops=0, bytes_accessed=0, transcendentals=0)
 VMEM_LIMIT = 48 * 2**20
 
 
@@ -29,19 +32,41 @@
     return jnp.sum(seen * member, axis=0, keepdims=True).astype(jnp.int32)
 
 
-def prepare_kernel(groups, capacity, me_ref, queries_ref, projection_ref, routes_ref, position_ref, *piece_refs):
+def prepare_kernel(
+    groups,
+    capacity,
+    sizes,
+    queries_hbm,
+    projection_hbm,
+    routes_hbm,
+    position_ref,
+    *refs,
+):
+    piece_refs = refs[: len(sizes)]
+    queries_ref, projection_ref, routes_ref, sems = refs[len(sizes) :]
+    copies = [
+        pltpu.make_async_copy(routes_hbm, routes_ref, sems.at[0]),
+        pltpu.make_async_copy(projection_hbm, projection_ref, sems.at[1]),
+        pltpu.make_async_copy(queries_hbm, queries_ref, sems.at[2]),
+    ]
+    for copy in copies:
+        copy.start()
     requests = queries_ref.shape[0]
-    distance = jnp.bitwise_xor(routes_ref[...], me_ref[0, 0])
+    me = lax.axis_index("db")
+    copies[0].wait()
+    distance = jnp.bitwise_xor(routes_ref[...], me)
     classes = lax.broadcasted_iota(jnp.int32, (-(-groups // 8) * 8, requests), 0)
     member = jnp.where(classes == distance, 1.0, 0.0)
     position = distance * capacity + ranks(member)
     position_ref[...] = position
+    slots = lax.broadcasted_iota(jnp.int32, (groups * capacity, requests), 0)
+    chooser = jnp.where(slots == position, 1.0, 0.0).astype(jnp.bfloat16)
+    copies[1].wait()
+    copies[2].wait()
     projected = jnp.dot(queries_ref[...], projection_ref[...], preferred_element_type=jnp.float32)
     normed = (
         projected * lax.rsqrt(jnp.sum(projected * projected, axis=1, keepdims=True) + 1e-06)
     ).astype(jnp.bfloat16)
-    slots = lax.broadcasted_iota(jnp.int32, (groups * capacity, requests), 0)
-    chooser = jnp.where(slots == position, 1.0, 0.0).astype(jnp.bfloat16)
     outgoing = jnp.dot(chooser, normed, preferred_element_type=jnp.float32).astype(jnp.bfloat16)
     start = 0
     for ref in piece_refs:
@@ -49,45 +74,81 @@
         start += ref.shape[0]
 
 
-def prepare(me, queries, projection, routes, groups, capacity, sizes):
+def prepare(queries, projection, routes, groups, capacity, sizes):
     requests, width = queries.shape
     return pl.pallas_call(
-        functools.partial(prepare_kernel, groups, capacity),
+        functools.partial(prepare_kernel, groups, capacity, sizes),
         out_shape=[jax.ShapeDtypeStruct((1, requests), jnp.int32)]
         + [jax.ShapeDtypeStruct((size, width), jnp.bfloat16) for size in sizes],
-        in_specs=[pl.BlockSpec(memory_space=pltpu.SMEM)] + [pl.BlockSpec(memory_space=pltpu.VMEM)] * 3,
-        compiler_params=params(),
+        in_specs=[pl.BlockSpec(memory_space=pltpu.HBM)] * 3,
+        scratch_shapes=[
+            pltpu.VMEM(queries.shape, queries.dtype),
+            pltpu.VMEM(projection.shape, projection.dtype),
+            pltpu.VMEM((1, requests), jnp.int32),
+            pltpu.SemaphoreType.DMA((3,)),
+        ],
+        compiler_params=pltpu.CompilerParams(vmem_limit_bytes=PREP_LIMIT),
         cost_estimate=cost(2 * requests * width * (width + groups * capacity), 3 * width * width),
         name="prepare",
-    )(me.reshape(1, 1), queries, projection, routes.reshape(1, requests))
-
-
-def sort_kernel(bins_ref, vectors_ref, sorted_ref):
-    bins = bins_ref[...]
-    width = bins.shape[1]
-    classes = lax.broadcasted_iota(jnp.int32, (BINS, width), 0)
-    member = jnp.where(classes == bins, 1.0, 0.0)
-    position = ranks(member) * BINS + bins
-    places = lax.broadcasted_iota(jnp.int32, (width, width), 0)
-    chooser = jnp.where(places == position, 1.0, 0.0).astype(jnp.bfloat16)
-    sorted_ref[...] = lax.dot_general(
-        vectors_ref[...], chooser, (((1,), (1,)), ((), ())), preferred_element_type=jnp.float32
-    ).astype(jnp.bfloat16)
-
-
-def sort_slab(bins, vectors):
-    depth, width = vectors.shape
+    )(queries, projection, routes.reshape(1, requests))
+
+
+def gate_kernel(value_ref, *refs):
+    pass
+
+
+def gate(value, *after):
+    return pl.pallas_call(
+        gate_kernel,
+        out_shape=jax.ShapeDtypeStruct(value.shape, value.dtype),
+        in_specs=[pl.BlockSpec(memory_space=pltpu.VMEM)] + [pl.BlockSpec(memory_space=pl.ANY)] * len(after),
+        out_specs=pl.BlockSpec(memory_space=pltpu.VMEM),
+        input_output_aliases={0: 0},
+        compiler_params=params(),
+        cost_estimate=NO_COST,
+        name="gate",
+    )(value, *after)
+
+
+def sort_kernel(after_ref, *refs):
+    slabs = len(refs) // 3
+    row = lax.broadcasted_iota(jnp.int32, (BINS, BINS), 0)
+    column = lax.broadcasted_iota(jnp.int32, (BINS, BINS), 1)
+    earlier = jnp.where(row < column, 1.0, 0.0).astype(jnp.bfloat16)
+    for bins_ref, slab_ref, sorted_ref in zip(refs[:slabs], refs[slabs : 2 * slabs], refs[2 * slabs :]):
+        width = bins_ref.shape[1]
+        places = lax.broadcasted_iota(jnp.int32, (width, BINS), 0)
+        before = jnp.zeros((BINS, 1), jnp.float32)
+        choosers = []
+        for start in range(0, width, BINS):
+            bins = bins_ref[:, start : start + BINS]
+            member = jnp.where(row == bins, 1.0, 0.0)
+            seen = before + jnp.dot(member.astype(jnp.bfloat16), earlier, preferred_element_type=jnp.float32)
+            before += jnp.sum(member, axis=1, keepdims=True)
+            rank = jnp.sum(seen * member, axis=0, keepdims=True).astype(jnp.int32)
+            choosers.append(jnp.where(places == rank * BINS + bins, 1.0, 0.0).astype(jnp.bfloat16))
+        sorted_ref[...] = lax.dot_general(
+            slab_ref[...],
+            jnp.concatenate(choosers, axis=1),
+            (((1,), (1,)), ((), ())),
+            preferred_element_type=jnp.float32,
+        ).astype(jnp.bfloat16)
+
+
+def sort_slabs(after, bins, slabs):
+    depth, width = slabs[0].shape
     return pl.pallas_call(
         sort_kernel,
-        out_shape=jax.ShapeDtypeStruct(vectors.shape, jnp.bfloat16),
-        in_specs=[pl.BlockSpec(memory_space=pltpu.VMEM)] * 2,
+        out_shape=[jax.ShapeDtypeStruct(slab.shape, jnp.bfloat16) for slab in slabs],
+        in_specs=[pl.BlockSpec(memory_space=pl.ANY)] + [pl.BlockSpec(memory_space=pltpu.VMEM)] * (2 * len(slabs)),
         compiler_params=params(),
-        cost_estimate=cost(2 * width * width * (depth + BINS), 4 * depth * width),
-        name="sort_slab",
-    )(bins.reshape(1, width), vectors)
-
-
-def score_kernel(pieces, *refs):
+        cost_estimate=NO_COST,
+        name="sort_slabs",
+    )(after, *[row.reshape(1, width) for row in bins], *slabs)
+
+
+def score_kernel(afters, pieces, *refs):
+    refs = refs[afters:]
     piece_refs, slab_refs, out_refs = refs[:pieces], refs[pieces:-pieces], refs[-pieces:]
     rows = jnp.concatenate([ref[...] for ref in piece_refs], axis=0)
     best = None
@@ -104,18 +165,19 @@
         start += ref.shape[0]
 
 
-def score(pieces, slabs):
+def score(after, pieces, slabs):
     rows = sum(piece.shape[0] for piece in pieces)
     columns = sum(slab.shape[1] for slab in slabs)
     width = slabs[0].shape[0]
     return pl.pallas_call(
-        functools.partial(score_kernel, len(pieces)),
+        functools.partial(score_kernel, len(after), len(pieces)),
         out_shape=[jax.ShapeDtypeStruct((piece.shape[0], BINS), jnp.float32) for piece in pieces],
-        in_specs=[pl.BlockSpec(memory_space=pltpu.VMEM)] * (len(pieces) + len(slabs)),
+        in_specs=[pl.BlockSpec(memory_space=pl.ANY)] * len(after)
+        + [pl.BlockSpec(memory_space=pltpu.VMEM)] * (len(pieces) + len(slabs)),
         compiler_params=params(),
         cost_estimate=cost(2 * rows * columns * width, 2 * width * (rows + columns)),
         name="score",
-    )(*pieces, *slabs)
+    )(*after, *pieces, *slabs)
 
 
 def select_kernel(position_ref, *refs):
@@ -154,7 +216,6 @@
     groups, slabs = lax.axis_size("db"), lax.axis_size("blk")
     requests = queries.shape[0]
     capacity = 2 * requests // groups
-    me = lax.axis_index("db")
 
     def along_db(value, distance):
         return lax.ppermute(value, "db", [(i, i ^ distance) for i in range(groups)])
@@ -170,23 +231,32 @@
         ]
         return lax.ppermute(value, ("db", "blk"), pairs)
 
-    position, *pieces = prepare(me, queries, projection, routes, groups, capacity, [capacity] * groups)
-    order = [3, 1, 2]
-    arrived = {0: pieces[0]}
-    for distance in order:
-        arrived[distance] = along_db(pieces[distance], distance)
-    own_slab = sort_slab(bins, vectors)
-    both_slabs = (own_slab, along_blk(own_slab, 1))
+    order = ORDER
+    position, *pieces = prepare(queries, projection, routes, groups, capacity, [capacity] * groups)
+    arrived, partner, results = {0: pieces[0]}, {}, {}
+    for k in order:
+        arrived[k] = along_db(pieces[k], k)
+    partner[0] = along_blk(arrived[0], 2)
+    slabs_here = sort_slabs(position, [bins, along_blk(bins, 1)], [vectors, along_blk(vectors, 1)])
+
     first, second = {}, {}
-    for distance in [0, 1, 3, 2]:
-        partner = along_blk(arrived[distance], 2)
-        here, there = score([arrived[distance], partner], both_slabs)
-        if distance:
-            first[distance] = along_db(here, distance)
-            second[distance] = along_both(there, distance, 2)
-        else:
-            first[distance] = here
-            second[distance] = along_blk(there, 2)
+
+    def scores(k, *after):
+        here, there = score(after, [arrived[k], partner[k]], slabs_here)
+        results[k] = there
+        first[k] = along_db(here, k) if k else here
+        second[k] = along_both(there, k, 2) if k else along_blk(there, 2)
+
+    a, b, c = order
+    arrived[a] = gate(arrived[a], slabs_here[0])
+    partner[a] = along_blk(arrived[a], 2)
+    scores(0, arrived[a])
+    arrived[b] = gate(arrived[b], second[0])
+    partner[b] = along_blk(arrived[b], 2)
+    partner[c] = along_blk(arrived[c], 2)
+    scores(a, results[0])
+    scores(b, results[a])
+    scores(c, results[b], first[a])
     ids = range(groups)
     return select(position, [first[k] for k in ids], [second[k] for k in ids])
 

time: 56.4 us -> 50.3 us (0.89)
  waiting for transfers between devices: 19.8 us -> 11.1 us
  Pallas kernels: 8.19 us -> 13.7 us
  starting transfers between devices: 24.8 us -> 22.7 us
  local copies, waits for them, and re-layouts: 3.37 us -> 2.53 us
    ppermute x6, waiting for transfers between devices: 16.2 us -> 0.5 us  [along_db(): return lax.ppermute(value, 'db', [(i, i ^ distance) for i in range(groups)])]
    pallas_call x6 -> x8, Pallas kernels: 7.19 us -> 12.7 us  [the longest x1 5.31 us: sort_slabs(): pl.pallas_call(sort_kernel, out_shape=[jax.ShapeDtypeStruct(slab.shape, j...]
    ppermute x6 -> x7, waiting for transfers between devices: 2.47 us -> 7.53 us  [along_blk(): return lax.ppermute(value, 'blk', [(i, i ^ distance) for i in range(slabs)])]
    ppermute x3, starting transfers between devices: 5.96 us -> 3.03 us  [along_both(): return lax.ppermute(value, ('db', 'blk'), pairs)]
    ppermute x3, waiting for transfers between devices: 1.06 us -> 3.04 us  [along_both(): return lax.ppermute(value, ('db', 'blk'), pairs)]
    ppermute x6, starting transfers between devices: 12.6 us -> 14 us  [along_db(): return lax.ppermute(value, 'db', [(i, i ^ distance) for i in range(groups)])]
    unnamed x10 -> x8, local copies, waits for them, and re-layouts: 3.37 us -> 2.53 us
    ppermute x6 -> x7, starting transfers between devices: 6.22 us -> 5.69 us  [along_blk(): return lax.ppermute(value, 'blk', [(i, i ^ distance) for i in range(slabs)])]
  transfers between devices with their start and end apart: 15 -> 16, of which waited for: 7 -> 6; matrix products, arithmetic and copies ran while one was open for 0% -> 0% of each run, Pallas kernels for 9% -> 25%
where the time goes in v2:
time: 50.3 us; the launch traced here: 50.1 us
  starting transfers between devices  22.7 us (45%)
  Pallas kernels  13.7 us (27%)
  waiting for transfers between devices  11.1 us (22%)
  local copies, waits for them, and re-layouts  2.53 us (5%)
    ppermute x6, starting transfers between devices, along_db(): return lax.ppermute(value, 'db', [(i, i ^ distance) for i in range(groups)])  14 us
    ppermute x7, waiting for transfers between devices, along_blk(): return lax.ppermute(value, 'blk', [(i, i ^ distance) for i in range(slabs)])  7.53 us
    ppermute x7, starting transfers between devices, along_blk(): return lax.ppermute(value, 'blk', [(i, i ^ distance) for i in range(slabs)])  5.69 us
    pallas_call x1, Pallas kernels, sort_slabs(): pl.pallas_call(sort_kernel, out_shape=[jax.ShapeDtypeStruct(slab.shape, j...  5.31 us
    pallas_call x4, Pallas kernels, score(): pl.pallas_call(functools.partial(score_kernel, len(after), len(pieces)),...  4.02 us
    pallas_call x1, Pallas kernels, prepare(): pl.pallas_call(functools.partial(prepare_kernel, groups, capacity, sizes)...  3.33 us
    ppermute x3, waiting for transfers between devices, along_both(): return lax.ppermute(value, ('db', 'blk'), pairs)  3.04 us
    ppermute x3, starting transfers between devices, along_both(): return lax.ppermute(value, ('db', 'blk'), pairs)  3.03 us
  transfers between devices with their start and end apart: 16, of which 6 were waited for; matrix products, arithmetic and copies ran while one was open for 0% of the time, Pallas kernels for 25%

profile of v2, /device:TPU:0, one launch (start us, length us, event | category | flops | bytes accessed | tf_op | source)
XLA Modules:
  0.0 50.1 jit_solution(8442988771946957053)
XLA Ops:
  0.0 0.0 copy-start.2
  0.0 0.5 collective-permute-start.2
  0.5 3.3 %prepare.1 = (s32[1,256]{1,0:T(1,128)}, bf16[128,768]{1,0:T(8,128)(2,1)}, bf16[128,768]{1,0:T(8,128)(2,1)}, bf16[128,768]{1,0:T(8,128)(2,1)}, bf16[128,768]{1,0:T(8,128)(2,1)}) custom-call(bf16[256,768]{1,0:T(8,128)(2,1)} %queries_hbm.1, bf16[768,768]{1,0:T(8,128)(2,1)} %projection_hbm.1, s32[1,256]{1,0:T(1,128)} %bitcast.5), custom_call_target="tpu_custom_call" | custom-call | flops 503316480 | bytes 1769472 | tf_op jit(solution)/shard_map/prepare/pallas_call | solution.py:79
  3.8 4.7 %collective-permute-start = (bf16[128,768]{1,0:T(8,128)(2,1)}, bf16[128,768]{1,0:T(8,128)(2,1)S(1)}, u32[]{:S(2)}, u32[]{:S(2)}) collective-permute-start(bf16[128,768]{1,0:T(8,128)(2,1)} %get-tuple-element.21), channel_id=1, source_target_pairs={{0,12},{4,8},{8,4},{12,0},{1,13},{5,9},{9,5},{13,1},{2,14},{6,10},... | collective-permute-start | bytes 589832 | tf_op jit(solution)/shard_map/ppermute | solution.py:221
  8.5 1.5 %collective-permute-start.3 = (bf16[128,768]{1,0:T(8,128)(2,1)}, bf16[128,768]{1,0:T(8,128)(2,1)S(1)}, u32[]{:S(2)}, u32[]{:S(2)}) collective-permute-start(bf16[128,768]{1,0:T(8,128)(2,1)} %get-tuple-element.23.refs_1_), channel_id=1, source_target_pairs={{0,2},{1,3},{2,0},{3,1},{4,6},{5,7},{6,4},{7,5},{8,10},{9,11},{10,... | collective-permute-start | bytes 589832 | tf_op jit(solution)/shard_map/ppermute | solution.py:224
  10.0 0.0 collective-permute-start.5
  10.0 0.0 copy-done.2
  10.0 0.0 collective-permute-start.1
  10.0 1.2 %collective-permute-done.1 = s32[1024]{0:T(1024)S(1)} collective-permute-done((s32[1024]{0:T(1024)S(1)}, s32[1024]{0:T(1024)S(1)}, u32[]{:S(2)}, u32[]{:S(2)}) %collective-permute-start.1) | collective-permute-done | bytes 4128 | tf_op jit(solution)/shard_map/ppermute | solution.py:224
  11.1 0.8 %collective-permute-start.10 = (bf16[128,768]{1,0:T(8,128)(2,1)}, bf16[128,768]{1,0:T(8,128)(2,1)S(1)}, u32[]{:S(2)}, u32[]{:S(2)}) collective-permute-start(bf16[128,768]{1,0:T(8,128)(2,1)} %get-tuple-element.32), channel_id=1, source_target_pairs={{0,8},{4,12},{8,0},{12,4},{1,9},{5,13},{9,1},{13,5},{2,10},{6,14},... | collective-permute-start | bytes 589832 | tf_op jit(solution)/shard_map/ppermute | solution.py:221
  11.9 0.0 collective-permute-done.2.refs_3_
  11.9 0.0 copy-start
  11.9 1.4 %copy-done = bf16[768,1024]{1,0:T(8,128)(2,1)S(1)} copy-done((bf16[768,1024]{1,0:T(8,128)(2,1)S(1)}, bf16[768,1024]{1,0:T(8,128)(2,1)}, u32[]{:S(2)}) %copy-start) | copy-done | bytes 1572888
  13.3 0.0 copy-start.3
  13.3 0.7 %copy-done.3 = s32[1,256]{1,0:T(1,128)S(1)} copy-done((s32[1,256]{1,0:T(1,128)S(1)}, s32[1,256]{1,0:T(1,128)}, u32[]{:S(2)}) %copy-start.3) | copy-done | bytes 1048
  14.0 5.3 %sort_slabs.1 = (bf16[768,1024]{1,0:T(8,128)(2,1)S(1)}, bf16[768,1024]{1,0:T(8,128)(2,1)S(1)}) custom-call(s32[1,256]{1,0:T(1,128)S(1)} %copy-done.3, s32[1,1024]{1,0:T(1,128)S(1)} %bitcast.3, s32[1,1024]{1,0:T(1,128)S(1)} %bitcast.4, bf16[768,1024]{1,0:T(8,128)(2,1)S(1)} %copy-done, bf16[768,1024]{1,0:T(8,128)(2,1)} %collective-permute-done.2.refs_3_), custom_call_target="tpu_custom_call" | custom-call | tf_op jit(solution)/shard_map/sort_slabs/pallas_call | solution.py:140
  19.3 0.0 copy-start.1
  19.3 0.0 collective-permute-done.value_ref
  19.4 0.5 collective-permute-start.4
  19.8 0.0 collective-permute-done.3.refs_2_
  19.8 0.4 copy-done.1
  20.3 1.0 %score.4 = (f32[128,128]{1,0:T(8,128)S(1)}, f32[128,128]{1,0:T(8,128)S(1)}) custom-call(bf16[128,768]{1,0:T(8,128)(2,1)S(1)} %gate.2.refs_0_.refs_1_, bf16[128,768]{1,0:T(8,128)(2,1)S(1)} %copy-done.1, bf16[128,768]{1,0:T(8,128)(2,1)S(1)} %collective-permute-done.3.refs_2_, bf16[768,1024]{1,0:T(8,128)(2,1)S(1)} %get-tuple-element.22.refs_0_.refs_3_.refs_4_, ...), custom_call_target="tpu_custom_call" | custom-call | flops 805306368 | bytes 3538944 | tf_op jit(solution)/shard_map/score/pallas_call | solution.py:172
  21.3 1.3 %collective-permute-start.6 = (f32[128,128]{1,0:T(8,128)S(1)}, f32[128,128]{1,0:T(8,128)S(1)}, u32[]{:S(2)}, u32[]{:S(2)}) collective-permute-start(f32[128,128]{1,0:T(8,128)S(1)} %get-tuple-element.26.refs_0_), channel_id=1, source_target_pairs={{0,2},{1,3},{2,0},{3,1},{4,6},{5,7},{6,4},{7,5},{8,10},{9,11},{10,... | collective-permute-start | bytes 196616 | tf_op jit(solution)/shard_map/ppermute | solution.py:224
  22.5 0.0 collective-permute-done.5.value_ref
  22.5 5.0 %collective-permute-done.6.refs_0_.refs_4_ = f32[128,128]{1,0:T(8,128)S(1)} collective-permute-done((f32[128,128]{1,0:T(8,128)S(1)}, f32[128,128]{1,0:T(8,128)S(1)}, u32[]{:S(2)}, u32[]{:S(2)}) %collective-permute-start.6) | collective-permute-done | bytes 65568 | tf_op jit(solution)/shard_map/ppermute | solution.py:224
  27.5 0.4 collective-permute-start.7
  27.9 0.0 collective-permute-done.10.refs_2_
  27.9 1.6 %collective-permute-start.11 = (bf16[128,768]{1,0:T(8,128)(2,1)S(1)}, bf16[128,768]{1,0:T(8,128)(2,1)S(1)}, u32[]{:S(2)}, u32[]{:S(2)}) collective-permute-start(bf16[128,768]{1,0:T(8,128)(2,1)S(1)} %collective-permute-done.10.refs_2_), channel_id=1, source_target_pairs={{0,2},{1,3},{2,0},{3,1},{4,6},{5,7},{6,4},{7,5},{8,10},{9,11},{10,... | collective-permute-start | bytes 589832 | tf_op jit(solution)/shard_map/ppermute | solution.py:224
  29.6 0.0 collective-permute-done.4.refs_2_
  29.6 1.0 %score.5 = (f32[128,128]{1,0:T(8,128)S(1)}, f32[128,128]{1,0:T(8,128)S(1)}) custom-call(f32[128,128]{1,0:T(8,128)S(1)} %get-tuple-element.26.refs_0_, bf16[128,768]{1,0:T(8,128)(2,1)S(1)} %gate.2.refs_0_.refs_1_, bf16[128,768]{1,0:T(8,128)(2,1)S(1)} %collective-permute-done.4.refs_2_, bf16[768,1024]{1,0:T(8,128)(2,1)S(1)} %get-tuple-element.22.refs_0_.refs_3_.refs_4_, ...), custom_call_target="tpu_custom_call" | custom-call | flops 805306368 | bytes 3538944 | tf_op jit(solution)/shard_map/score/pallas_call | solution.py:172
  30.6 3.7 %collective-permute-start.9 = (f32[128,128]{1,0:T(8,128)S(1)}, f32[128,128]{1,0:T(8,128)S(1)}, u32[]{:S(2)}, u32[]{:S(2)}) collective-permute-start(f32[128,128]{1,0:T(8,128)S(1)} %get-tuple-element.31), channel_id=1, source_target_pairs={{0,12},{4,8},{8,4},{12,0},{1,13},{5,9},{9,5},{13,1},{2,14},{6,10},... | collective-permute-start | bytes 196616 | tf_op jit(solution)/shard_map/ppermute | solution.py:221
  34.2 0.1 collective-permute-start.15
  34.3 1.1 %collective-permute-done.7.refs_2_ = bf16[128,768]{1,0:T(8,128)(2,1)S(1)} collective-permute-done((bf16[128,768]{1,0:T(8,128)(2,1)S(1)}, bf16[128,768]{1,0:T(8,128)(2,1)S(1)}, u32[]{:S(2)}, u32[]{:S(2)}) %collective-permute-start.7) | collective-permute-done | bytes 196640 | tf_op jit(solution)/shard_map/ppermute | solution.py:224
  35.4 1.0 %score.6 = (f32[128,128]{1,0:T(8,128)S(1)}, f32[128,128]{1,0:T(8,128)S(1)}) custom-call(f32[128,128]{1,0:T(8,128)S(1)} %get-tuple-element.27.refs_0_, bf16[128,768]{1,0:T(8,128)(2,1)S(1)} %gate.3.refs_1_, bf16[128,768]{1,0:T(8,128)(2,1)S(1)} %collective-permute-done.7.refs_2_, bf16[768,1024]{1,0:T(8,128)(2,1)S(1)} %get-tuple-element.22.refs_0_.refs_3_.refs_4_, ...), custom_call_target="tpu_custom_call" | custom-call | flops 805306368 | bytes 3538944 | tf_op jit(solution)/shard_map/score/pallas_call | solution.py:172
  36.4 2.3 %collective-permute-start.13 = (f32[128,128]{1,0:T(8,128)S(1)}, f32[128,128]{1,0:T(8,128)S(1)}, u32[]{:S(2)}, u32[]{:S(2)}) collective-permute-start(f32[128,128]{1,0:T(8,128)S(1)} %get-tuple-element.30.refs_0_), channel_id=1, source_target_pairs={{0,6},{1,7},{2,4},{3,5},{4,2},{5,3},{6,0},{7,1},{8,14},{9,15},{10,... | collective-permute-start | bytes 196616 | tf_op jit(solution)/shard_map/ppermute | solution.py:232
  38.6 0.3 collective-permute-done.11.refs_3_
  39.0 0.0 collective-permute-done.9.refs_1_.refs_3_
  39.0 1.0 %score.7 = (f32[128,128]{1,0:T(8,128)S(1)}, f32[128,128]{1,0:T(8,128)S(1)}) custom-call(f32[128,128]{1,0:T(8,128)S(1)} %get-tuple-element.30.refs_0_, f32[128,128]{1,0:T(8,128)S(1)} %collective-permute-done.9.refs_1_.refs_3_, bf16[128,768]{1,0:T(8,128)(2,1)S(1)} %collective-permute-done.10.refs_2_, bf16[128,768]{1,0:T(8,128)(2,1)S(1)} %collective-permute-done.11.refs_3_, ...), custom_call_target="tpu_custom_call" | custom-call | flops 805306368 | bytes 3538944 | tf_op jit(solution)/shard_map/score/pallas_call | solution.py:172
  40.0 2.9 %collective-permute-start.12 = (f32[128,128]{1,0:T(8,128)S(1)}, f32[128,128]{1,0:T(8,128)S(1)}, u32[]{:S(2)}, u32[]{:S(2)}) collective-permute-start(f32[128,128]{1,0:T(8,128)S(1)} %get-tuple-element.33), channel_id=1, source_target_pairs={{0,8},{4,12},{8,0},{12,4},{1,9},{5,13},{9,1},{13,5},{2,10},{6,14},... | collective-permute-start | bytes 196616 | tf_op jit(solution)/shard_map/ppermute | solution.py:221
  42.9 0.7 %collective-permute-start.14 = (f32[128,128]{1,0:T(8,128)S(1)}, f32[128,128]{1,0:T(8,128)S(1)}, u32[]{:S(2)}, u32[]{:S(2)}) collective-permute-start(f32[128,128]{1,0:T(8,128)S(1)} %get-tuple-element.34), channel_id=1, source_target_pairs={{0,10},{1,11},{2,8},{3,9},{4,14},{5,15},{6,12},{7,13},{8,2},{9,3},... | collective-permute-start | bytes 196616 | tf_op jit(solution)/shard_map/ppermute | solution.py:232
  43.6 2.0 %collective-permute-start.8 = (f32[128,128]{1,0:T(8,128)S(1)}, f32[128,128]{1,0:T(8,128)S(1)}, u32[]{:S(2)}, u32[]{:S(2)}) collective-permute-start(f32[128,128]{1,0:T(8,128)S(1)} %get-tuple-element.29), channel_id=1, source_target_pairs={{0,4},{4,0},{8,12},{12,8},{1,5},{5,1},{9,13},{13,9},{2,6},{6,2},{1... | collective-permute-start | bytes 196616 | tf_op jit(solution)/shard_map/ppermute | solution.py:221
  45.5 0.0 collective-permute-done.15.refs_7_
  45.5 0.5 collective-permute-done.12.refs_2_
  46.0 3.0 %collective-permute-done.14.refs_6_ = f32[128,128]{1,0:T(8,128)S(1)} collective-permute-done((f32[128,128]{1,0:T(8,128)S(1)}, f32[128,128]{1,0:T(8,128)S(1)}, u32[]{:S(2)}, u32[]{:S(2)}) %collective-permute-start.14) | collective-permute-done | bytes 65568 | tf_op jit(solution)/shard_map/ppermute | solution.py:232
  49.1 0.0 collective-permute-done.13.refs_5_
  49.1 0.0 collective-permute-done.8.refs_1_
  49.1 1.0 %select.1 = f32[256,128]{1,0:T(8,128)} custom-call(s32[1,256]{1,0:T(1,128)S(1)} %copy-done.3, f32[128,128]{1,0:T(8,128)S(1)} %get-tuple-element.25.refs_0_, f32[128,128]{1,0:T(8,128)S(1)} %collective-permute-done.8.refs_1_, f32[128,128]{1,0:T(8,128)S(1)} %collective-permute-done.12.refs_2_, f32[128,128]{1,0:T(8,128)S(1)} %collective-permute-done.9.refs_1_.refs_3_, ...), custom_call_target="tpu_custom_call" | custom-call | flops 100663296 | bytes 524288 | tf_op jit(solution)/shard_map/select/pallas_call | solution.py:205
  (2 shorter events, 0.0 us)
Async XLA Ops:
  0.0 10.0 %copy-start.2 = (s32[1024]{0:T(1024)S(1)}, s32[1024]{0:T(1024)}, u32[]{:S(2)}) copy-start(s32[1024]{0:T(1024)} %param.8) | copy-start | bytes 12292
  0.0 11.9 %collective-permute-start.2 = (bf16[768,1024]{1,0:T(8,128)(2,1)}, bf16[768,1024]{1,0:T(8,128)(2,1)}, u32[]{:S(2)}, u32[]{:S(2)}) collective-permute-start(bf16[768,1024]{1,0:T(8,128)(2,1)} %refs_2_.1), channel_id=1, source_target_pairs={{0,1},{1,0},{2,3},{3,2},{4,5},{5,4},{6,7},{7,6},{8,9},{9,8},{10,11... | collective-permute-start | bytes 4718600 | tf_op jit(solution)/shard_map/ppermute | solution.py:224
  3.8 15.5 %collective-permute-start = (bf16[128,768]{1,0:T(8,128)(2,1)}, bf16[128,768]{1,0:T(8,128)(2,1)S(1)}, u32[]{:S(2)}, u32[]{:S(2)}) collective-permute-start(bf16[128,768]{1,0:T(8,128)(2,1)} %get-tuple-element.21), channel_id=1, source_target_pairs={{0,12},{4,8},{8,4},{12,0},{1,13},{5,9},{9,5},{13,1},{2,14},{6,10},... | collective-permute-start | bytes 589832 | tf_op jit(solution)/shard_map/ppermute | solution.py:221
  8.5 11.3 %collective-permute-start.3 = (bf16[128,768]{1,0:T(8,128)(2,1)}, bf16[128,768]{1,0:T(8,128)(2,1)S(1)}, u32[]{:S(2)}, u32[]{:S(2)}) collective-permute-start(bf16[128,768]{1,0:T(8,128)(2,1)} %get-tuple-element.23.refs_1_), channel_id=1, source_target_pairs={{0,2},{1,3},{2,0},{3,1},{4,6},{5,7},{6,4},{7,5},{8,10},{9,11},{10,... | collective-permute-start | bytes 589832 | tf_op jit(solution)/shard_map/ppermute | solution.py:224
  10.0 12.6 %collective-permute-start.5 = (bf16[128,768]{1,0:T(8,128)(2,1)}, bf16[128,768]{1,0:T(8,128)(2,1)S(1)}, u32[]{:S(2)}, u32[]{:S(2)}) collective-permute-start(bf16[128,768]{1,0:T(8,128)(2,1)} %get-tuple-element.28), channel_id=1, source_target_pairs={{0,4},{4,0},{8,12},{12,8},{1,5},{5,1},{9,13},{13,9},{2,6},{6,2},{1... | collective-permute-start | bytes 589832 | tf_op jit(solution)/shard_map/ppermute | solution.py:221
  10.0 1.2 %collective-permute-start.1 = (s32[1024]{0:T(1024)S(1)}, s32[1024]{0:T(1024)S(1)}, u32[]{:S(2)}, u32[]{:S(2)}) collective-permute-start(s32[1024]{0:T(1024)S(1)} %copy-done.2), channel_id=1, source_target_pairs={{0,1},{1,0},{2,3},{3,2},{4,5},{5,4},{6,7},{7,6},{8,9},{9,8},{10,11... | collective-permute-start | bytes 12296 | tf_op jit(solution)/shard_map/ppermute | solution.py:224
  11.1 16.8 %collective-permute-start.10 = (bf16[128,768]{1,0:T(8,128)(2,1)}, bf16[128,768]{1,0:T(8,128)(2,1)S(1)}, u32[]{:S(2)}, u32[]{:S(2)}) collective-permute-start(bf16[128,768]{1,0:T(8,128)(2,1)} %get-tuple-element.32), channel_id=1, source_target_pairs={{0,8},{4,12},{8,0},{12,4},{1,9},{5,13},{9,1},{13,5},{2,10},{6,14},... | collective-permute-start | bytes 589832 | tf_op jit(solution)/shard_map/ppermute | solution.py:221
  11.9 1.4 %copy-start = (bf16[768,1024]{1,0:T(8,128)(2,1)S(1)}, bf16[768,1024]{1,0:T(8,128)(2,1)}, u32[]{:S(2)}) copy-start(bf16[768,1024]{1,0:T(8,128)(2,1)} %refs_2_.1) | copy-start | bytes 4718596
  13.3 0.7 %copy-start.3 = (s32[1,256]{1,0:T(1,128)S(1)}, s32[1,256]{1,0:T(1,128)}, u32[]{:S(2)}) copy-start(s32[1,256]{1,0:T(1,128)} %get-tuple-element.20.after_ref.position_ref) | copy-start | bytes 3076
  19.3 0.9 %copy-start.1 = (bf16[128,768]{1,0:T(8,128)(2,1)S(1)}, bf16[128,768]{1,0:T(8,128)(2,1)}, u32[]{:S(2)}) copy-start(bf16[128,768]{1,0:T(8,128)(2,1)} %get-tuple-element.23.refs_1_) | copy-start | bytes 589828
  19.4 10.2 %collective-permute-start.4 = (bf16[128,768]{1,0:T(8,128)(2,1)S(1)}, bf16[128,768]{1,0:T(8,128)(2,1)S(1)}, u32[]{:S(2)}, u32[]{:S(2)}) collective-permute-start(bf16[128,768]{1,0:T(8,128)(2,1)S(1)} %gate.2.refs_0_.refs_1_), channel_id=1, source_target_pairs={{0,2},{1,3},{2,0},{3,1},{4,6},{5,7},{6,4},{7,5},{8,10},{9,11},{10,... | collective-permute-start | bytes 589832 | tf_op jit(solution)/shard_map/ppermute | solution.py:224
  21.3 6.3 %collective-permute-start.6 = (f32[128,128]{1,0:T(8,128)S(1)}, f32[128,128]{1,0:T(8,128)S(1)}, u32[]{:S(2)}, u32[]{:S(2)}) collective-permute-start(f32[128,128]{1,0:T(8,128)S(1)} %get-tuple-element.26.refs_0_), channel_id=1, source_target_pairs={{0,2},{1,3},{2,0},{3,1},{4,6},{5,7},{6,4},{7,5},{8,10},{9,11},{10,... | collective-permute-start | bytes 196616 | tf_op jit(solution)/shard_map/ppermute | solution.py:224
  27.5 7.8 %collective-permute-start.7 = (bf16[128,768]{1,0:T(8,128)(2,1)S(1)}, bf16[128,768]{1,0:T(8,128)(2,1)S(1)}, u32[]{:S(2)}, u32[]{:S(2)}) collective-permute-start(bf16[128,768]{1,0:T(8,128)(2,1)S(1)} %gate.3.refs_1_), channel_id=1, source_target_pairs={{0,2},{1,3},{2,0},{3,1},{4,6},{5,7},{6,4},{7,5},{8,10},{9,11},{10,... | collective-permute-start | bytes 589832 | tf_op jit(solution)/shard_map/ppermute | solution.py:224
  27.9 11.0 %collective-permute-start.11 = (bf16[128,768]{1,0:T(8,128)(2,1)S(1)}, bf16[128,768]{1,0:T(8,128)(2,1)S(1)}, u32[]{:S(2)}, u32[]{:S(2)}) collective-permute-start(bf16[128,768]{1,0:T(8,128)(2,1)S(1)} %collective-permute-done.10.refs_2_), channel_id=1, source_target_pairs={{0,2},{1,3},{2,0},{3,1},{4,6},{5,7},{6,4},{7,5},{8,10},{9,11},{10,... | collective-permute-start | bytes 589832 | tf_op jit(solution)/shard_map/ppermute | solution.py:224
  30.6 8.4 %collective-permute-start.9 = (f32[128,128]{1,0:T(8,128)S(1)}, f32[128,128]{1,0:T(8,128)S(1)}, u32[]{:S(2)}, u32[]{:S(2)}) collective-permute-start(f32[128,128]{1,0:T(8,128)S(1)} %get-tuple-element.31), channel_id=1, source_target_pairs={{0,12},{4,8},{8,4},{12,0},{1,13},{5,9},{9,5},{13,1},{2,14},{6,10},... | collective-permute-start | bytes 196616 | tf_op jit(solution)/shard_map/ppermute | solution.py:221
  34.2 11.3 %collective-permute-start.15 = (f32[128,128]{1,0:T(8,128)S(1)}, f32[128,128]{1,0:T(8,128)S(1)}, u32[]{:S(2)}, u32[]{:S(2)}) collective-permute-start(f32[128,128]{1,0:T(8,128)S(1)} %get-tuple-element.27.refs_0_), channel_id=1, source_target_pairs={{0,14},{1,15},{2,12},{3,13},{4,10},{5,11},{6,8},{7,9},{8,6},{9,7},... | collective-permute-start | bytes 196616 | tf_op jit(solution)/shard_map/ppermute | solution.py:232
  36.4 12.7 %collective-permute-start.13 = (f32[128,128]{1,0:T(8,128)S(1)}, f32[128,128]{1,0:T(8,128)S(1)}, u32[]{:S(2)}, u32[]{:S(2)}) collective-permute-start(f32[128,128]{1,0:T(8,128)S(1)} %get-tuple-element.30.refs_0_), channel_id=1, source_target_pairs={{0,6},{1,7},{2,4},{3,5},{4,2},{5,3},{6,0},{7,1},{8,14},{9,15},{10,... | collective-permute-start | bytes 196616 | tf_op jit(solution)/shard_map/ppermute | solution.py:232
  40.0 6.0 %collective-permute-start.12 = (f32[128,128]{1,0:T(8,128)S(1)}, f32[128,128]{1,0:T(8,128)S(1)}, u32[]{:S(2)}, u32[]{:S(2)}) collective-permute-start(f32[128,128]{1,0:T(8,128)S(1)} %get-tuple-element.33), channel_id=1, source_target_pairs={{0,8},{4,12},{8,0},{12,4},{1,9},{5,13},{9,1},{13,5},{2,10},{6,14},... | collective-permute-start | bytes 196616 | tf_op jit(solution)/shard_map/ppermute | solution.py:221
  42.9 6.2 %collective-permute-start.14 = (f32[128,128]{1,0:T(8,128)S(1)}, f32[128,128]{1,0:T(8,128)S(1)}, u32[]{:S(2)}, u32[]{:S(2)}) collective-permute-start(f32[128,128]{1,0:T(8,128)S(1)} %get-tuple-element.34), channel_id=1, source_target_pairs={{0,10},{1,11},{2,8},{3,9},{4,14},{5,15},{6,12},{7,13},{8,2},{9,3},... | collective-permute-start | bytes 196616 | tf_op jit(solution)/shard_map/ppermute | solution.py:232
  43.6 5.5 %collective-permute-start.8 = (f32[128,128]{1,0:T(8,128)S(1)}, f32[128,128]{1,0:T(8,128)S(1)}, u32[]{:S(2)}, u32[]{:S(2)}) collective-permute-start(f32[128,128]{1,0:T(8,128)S(1)} %get-tuple-element.29), channel_id=1, source_target_pairs={{0,4},{4,0},{8,12},{12,8},{1,5},{5,1},{9,13},{13,9},{2,6},{6,2},{1... | collective-permute-start | bytes 196616 | tf_op jit(solution)/shard_map/ppermute | solution.py:221

commit v3 on v1

v3 whole, which is shorter than its diff:
```python
import functools

import jax
import jax.numpy as jnp
from jax import lax
from jax.experimental import pallas as pl
from jax.experimental.pallas import tpu as pltpu
from jax.sharding import PartitionSpec as P

BINS = 128
logit_scale = 10.0
MIB = 2**20


def params(limit=48):
    return pltpu.CompilerParams(vmem_limit_bytes=limit * MIB)


def us(time):
    return pl.CostEstimate(flops=int(time * 10**9), bytes_accessed=0, transcendentals=0)


def ranks(member):
    count = member.shape[1]
    row = lax.broadcasted_iota(jnp.int32, (count, count), 0)
    column = lax.broadcasted_iota(jnp.int32, (count, count), 1)
    earlier = jnp.where(row < column, 1.0, 0.0).astype(jnp.bfloat16)
    seen = jnp.dot(member.astype(jnp.bfloat16), earlier, preferred_element_type=jnp.float32)
    return jnp.sum(seen * member, axis=0, keepdims=True).astype(jnp.int32)


def sorted_columns(bins_row, slab):
    row = lax.broadcasted_iota(jnp.int32, (BINS, BINS), 0)
    column = lax.broadcasted_iota(jnp.int32, (BINS, BINS), 1)
    earlier = jnp.where(row < column, 1.0, 0.0).astype(jnp.bfloat16)
    width = bins_row.shape[1]
    places = lax.broadcasted_iota(jnp.int32, (width, BINS), 0)
    before = jnp.zeros((BINS, 1), jnp.float32)
    choosers = []
    for start in range(0, width, BINS):
        bins = bins_row[:, start : start + BINS]
        member = jnp.where(row == bins, 1.0, 0.0)
        seen = before + jnp.dot(member.astype(jnp.bfloat16), earlier, preferred_element_type=jnp.float32)
        before += jnp.sum(member, axis=1, keepdims=True)
        rank = jnp.sum(seen * member, axis=0, keepdims=True).astype(jnp.int32)
        choosers.append(jnp.where(places == rank * BINS + bins, 1.0, 0.0).astype(jnp.bfloat16))
    return lax.dot_general(
        slab, jnp.concatenate(choosers, axis=1), (((1,), (1,)), ((), ())), preferred_element_type=jnp.float32
    ).astype(jnp.bfloat16)


def projected_rows(queries, projection):
    projected = jnp.dot(queries, projection, preferred_element_type=jnp.float32)
    scale = lax.rsqrt(jnp.sum(projected * projected, axis=1, keepdims=True) + 1e-06)
    return (projected * scale).astype(jnp.bfloat16)


def prepare_kernel(groups, capacity, routes_hbm, queries_hbm, position_ref, *refs):
    piece_refs, (routes_ref, queries_ref, sems) = refs[:groups], refs[groups:]
    copies = [
        pltpu.make_async_copy(routes_hbm, routes_ref, sems.at[0]),
        pltpu.make_async_copy(queries_hbm, queries_ref, sems.at[1]),
    ]
    for copy in copies:
        copy.start()
    requests = queries_ref.shape[0]
    copies[0].wait()
    distance = jnp.bitwise_xor(routes_ref[...], lax.axis_index("db"))
    classes = lax.broadcasted_iota(jnp.int32, (-(-groups // 8) * 8, requests), 0)
    member = jnp.where(classes == distance, 1.0, 0.0)
    position = distance * capacity + ranks(member)
    position_ref[...] = position
    slots = lax.broadcasted_iota(jnp.int32, (groups * capacity, requests), 0)
    chooser = jnp.where(slots == position, 1.0, 0.0).astype(jnp.bfloat16)
    copies[1].wait()
    outgoing = jnp.dot(chooser, queries_ref[...], preferred_element_type=jnp.float32).astype(jnp.bfloat16)
    for i, ref in enumerate(piece_refs):
        ref[...] = outgoing[i * capacity : (i + 1) * capacity]


def prepare(queries, routes, groups, capacity):
    requests, width = queries.shape
    ins = [routes.reshape(1, requests), queries]
    return pl.pallas_call(
        functools.partial(prepare_kernel, groups, capacity),
        out_shape=[jax.ShapeDtypeStruct((1, requests), jnp.int32)]
        + [jax.ShapeDtypeStruct((capacity, width), jnp.bfloat16)] * groups,
        in_specs=[pl.BlockSpec(memory_space=pltpu.HBM)] * len(ins),
        scratch_shapes=[pltpu.VMEM(x.shape, x.dtype) for x in ins] + [pltpu.SemaphoreType.DMA((len(ins),))],
        compiler_params=params(63),
        cost_estimate=us(0),
        name="prepare",
    )(*ins)


def project_kernel(piece_ref, projection_ref, *refs):
    refs[-1][...] = projected_rows(piece_ref[...], projection_ref[...])


def project(piece, projection, *after):
    return pl.pallas_call(
        project_kernel,
        out_shape=jax.ShapeDtypeStruct(piece.shape, jnp.bfloat16),
        in_specs=[pl.BlockSpec(memory_space=pltpu.VMEM)] * 2 + [pl.BlockSpec(memory_space=pl.ANY)] * len(after),
        compiler_params=params(),
        cost_estimate=us(0),
        name="project",
    )(piece, projection, *after)


def sort_kernel(slabs, after_ref, *refs):
    for bins_ref, slab_ref, sorted_ref in zip(refs[:slabs], refs[slabs : 2 * slabs], refs[2 * slabs :]):
        sorted_ref[...] = sorted_columns(bins_ref[...], slab_ref[...])


def sort_slabs(after, bins, slabs):
    width = slabs[0].shape[1]
    return pl.pallas_call(
        functools.partial(sort_kernel, len(slabs)),
        out_shape=[jax.ShapeDtypeStruct(slab.shape, jnp.bfloat16) for slab in slabs],
        in_specs=[pl.BlockSpec(memory_space=pl.ANY)] + [pl.BlockSpec(memory_space=pltpu.VMEM)] * (2 * len(slabs)),
        compiler_params=params(),
        cost_estimate=us(0),
        name="sort_slabs",
    )(after, *[row.reshape(1, width) for row in bins], *slabs)


def score_kernel(afters, pieces, outs, *refs):
    refs = refs[afters:]
    piece_refs, slab_refs, out_refs = refs[:pieces], refs[pieces:-outs], refs[-outs:]
    rows = jnp.concatenate([ref[...] for ref in piece_refs], axis=0)
    best = None
    step = 2 * BINS
    for slab_ref in slab_refs:
        for start in range(0, slab_ref.shape[1], step):
            scores = jnp.dot(rows, slab_ref[:, start : start + step], preferred_element_type=jnp.float32)
            for first in range(0, step, BINS):
                part = scores[:, first : first + BINS]
                best = part if best is None else jnp.maximum(best, part)
    start = 0
    for ref in out_refs:
        ref[...] = best[start : start + ref.shape[0]]
        start += ref.shape[0]


def score(after, pieces, slabs, sizes):
    rows = sum(sizes)
    return pl.pallas_call(
        functools.partial(score_kernel, len(after), len(pieces), len(sizes)),
        out_shape=[jax.ShapeDtypeStruct((size, BINS), jnp.float32) for size in sizes],
        in_specs=[pl.BlockSpec(memory_space=pl.ANY)] * len(after)
        + [pl.BlockSpec(memory_space=pltpu.VMEM)] * (len(pieces) + len(slabs)),
        compiler_params=params(),
        cost_estimate=us(rows / 256),
        name="score",
    )(*after, *pieces, *slabs)


def select_kernel(pieces, position_ref, *refs):
    out_ref = refs[-1]
    answers = [jnp.maximum(a[...], b[...]) for a, b in zip(refs[:pieces], refs[pieces : 2 * pieces])]
    answers = jnp.concatenate(answers, axis=0)
    high = answers.astype(jnp.bfloat16)
    rest = answers - high.astype(jnp.float32)
    middle = rest.astype(jnp.bfloat16)
    low = (rest - middle.astype(jnp.float32)).astype(jnp.bfloat16)
    parts = jnp.concatenate([high, middle, low], axis=1)
    position = position_ref[...]
    slots = lax.broadcasted_iota(jnp.int32, (answers.shape[0], position.shape[1]), 0)
    chooser = jnp.where(slots == position, 1.0, 0.0).astype(jnp.bfloat16)
    chosen = lax.dot_general(chooser, parts, (((0,), (0,)), ((), ())), preferred_element_type=jnp.float32)
    out_ref[...] = logit_scale * ((chosen[:, :BINS] + chosen[:, BINS : 2 * BINS]) + chosen[:, 2 * BINS :])


def select(position, first, second):
    return pl.pallas_call(
        functools.partial(select_kernel, len(first)),
        out_shape=jax.ShapeDtypeStruct((position.shape[1], BINS), jnp.float32),
        in_specs=[pl.BlockSpec(memory_space=pltpu.VMEM)] * (1 + 2 * len(first)),
        compiler_params=params(),
        cost_estimate=us(0),
        name="select",
    )(position, *first, *second)


def device_paired(queries, projection, vectors, bins, routes):
    groups, slabs = lax.axis_size("db"), lax.axis_size("blk")
    requests = queries.shape[0]
    capacity = 2 * requests // groups

    def along_db(value, distance):
        return lax.ppermute(value, "db", [(i, i ^ distance) for i in range(groups)])

    def along_blk(value, distance):
        return lax.ppermute(value, "blk", [(i, i ^ distance) for i in range(slabs)])

    def along_both(value, distance, distance_blk):
        pairs = [
            (i * slabs + j, (i ^ distance) * slabs + (j ^ distance_blk))
            for i in range(groups)
            for j in range(slabs)
        ]
        return lax.ppermute(value, ("db", "blk"), pairs)

    position, *pieces = prepare(queries, routes, groups, capacity)
    arrived = {k: along_db(pieces[k], k) for k in (3, 1, 2)}
    slabs_here = sort_slabs(position, [bins, along_blk(bins, 1)], [vectors, along_blk(vectors, 1)])
    here = {0: project(pieces[0], projection)}
    for k in (3, 1, 2):
        here[k] = project(arrived[k], projection, slabs_here[0])
    partner = {k: along_blk(here[k], 2) for k in (0, 3, 1, 2)}
    first, second = {}, {}

    def scores(wave, *after):
        found = score(after, [here[k] for k in wave] + [partner[k] for k in wave], slabs_here, [capacity] * 2 * len(wave))
        for k, mine, theirs in zip(wave, found[: len(wave)], found[len(wave) :]):
            first[k] = along_db(mine, k) if k else mine
            second[k] = along_both(theirs, k, 2) if k else along_blk(theirs, 2)
        return found[-1]

    done = scores([3, 0])
    done = scores([1], done)
    scores([2], done, first[3], second[3], second[0])
    ids = range(groups)
    return select(position, [first[k] for k in ids], [second[k] for k in ids])


def binned_max(query_rows, columns):
    scores = jnp.dot(query_rows, columns, preferred_element_type=jnp.float32)
    return jnp.max(scores.reshape(query_rows.shape[0], -1, BINS), axis=1)


def device_gathered(queries, projection, vectors, bins, routes):
    groups = lax.axis_size("db")
    requests = queries.shape[0]
    capacity = 2 * requests // groups
    slab_width = vectors.shape[1]
    per_bin = slab_width // BINS
    projected = jnp.dot(queries, projection, preferred_element_type=jnp.float32)
    normed = (
        projected * lax.rsqrt(jnp.sum(projected * projected, axis=1, keepdims=True) + 1e-06)
    ).astype(jnp.bfloat16)
    target = routes[:, 0]
    one_hot = (target[:, None] == jnp.arange(groups, dtype=jnp.int32)[None, :]).astype(jnp.int32)
    slot_index = jnp.sum((jnp.cumsum(one_hot, axis=0) - one_hot) * one_hot, axis=1)
    position = target * capacity + slot_index
    chooser = (jnp.arange(groups * capacity, dtype=jnp.int32)[:, None] == position[None, :]).astype(
        jnp.bfloat16
    )
    outgoing = jnp.dot(chooser, normed, preferred_element_type=jnp.float32).astype(jnp.bfloat16)
    arrived = lax.all_to_all(outgoing, "db", split_axis=0, concat_axis=0, tiled=True)
    ordering = jnp.argsort(bins, stable=True).reshape(BINS, per_bin).T.reshape(-1)
    sorted_slab = jnp.take(vectors, ordering, axis=1)
    maxima = binned_max(arrived, lax.all_gather(sorted_slab, "blk", axis=1, tiled=True))
    answers = lax.all_to_all(logit_scale * maxima, "db", split_axis=0, concat_axis=0, tiled=True)
    return jnp.take(answers, position, axis=0)


def solution(mesh):
    paired = mesh.shape["db"] == 4 and mesh.shape["blk"] == 4
    in_specs = (
        P(("parts", "db", "blk"), None),
        P(),
        P(None, ("parts", "db", "blk")),
        P(("parts", "db", "blk")),
        P(("parts", "db", "blk"), None),
    )
    out_specs = P(("parts", "db", "blk"), None)
    return jax.shard_map(
        device_paired if paired else device_gathered,
        mesh=mesh,
        in_specs=in_specs,
        out_specs=out_specs,
        check_vma=False,
    )
```

time: 56.4 us -> 49.3 us (0.87)
  waiting for transfers between devices: 19.8 us -> 9.69 us
  Pallas kernels: 8.19 us -> 14.1 us
  starting transfers between devices: 24.8 us -> 23 us
  local copies, waits for them, and re-layouts: 3.37 us -> 2.22 us
    ppermute x6, waiting for transfers between devices: 16.2 us -> 5.15 us  [along_db(): return lax.ppermute(value, 'db', [(i, i ^ distance) for i in range(groups)])]
    pallas_call x6 -> x9, Pallas kernels: 7.12 us -> 11.9 us  [the longest x1 5.41 us: sort_slabs(): pl.pallas_call(functools.partial(sort_kernel, len(slabs)), out_shape=[jax...]
    ppermute x3, waiting for transfers between devices: 1.06 us -> 4.53 us  [along_both(): return lax.ppermute(value, ('db', 'blk'), pairs)]
    ppermute x6, starting transfers between devices: 12.6 us -> 10.1 us  [along_db(): return lax.ppermute(value, 'db', [(i, i ^ distance) for i in range(groups)])]
    ppermute x6 -> x7, waiting for transfers between devices: 2.47 us -> 0.02 us  [along_blk(): return lax.ppermute(value, 'blk', [(i, i ^ distance) for i in range(slabs)])]
    unnamed x10 -> x12, local copies, waits for them, and re-layouts: 3.37 us -> 2.22 us
    pallas_call x1, Pallas kernels: 1.07 us -> 2.19 us  [prepare(): pl.pallas_call(functools.partial(prepare_kernel, groups, capacity), out_s...]
    ppermute x6 -> x7, starting transfers between devices: 6.22 us -> 6.54 us  [along_blk(): return lax.ppermute(value, 'blk', [(i, i ^ distance) for i in range(slabs)])]
  transfers between devices with their start and end apart: 15 -> 16, of which waited for: 7 -> 4; matrix products, arithmetic and copies ran while one was open for 0% -> 0% of each run, Pallas kernels for 9% -> 27%
where the time goes in v3:
time: 49.3 us; the launch traced here: 49.1 us
  starting transfers between devices  23 us (47%)
  Pallas kernels  14.1 us (29%)
  waiting for transfers between devices  9.69 us (20%)
  local copies, waits for them, and re-layouts  2.22 us (5%)
    ppermute x6, starting transfers between devices, along_db(): return lax.ppermute(value, 'db', [(i, i ^ distance) for i in range(groups)])  10.1 us
    ppermute x7, starting transfers between devices, along_blk(): return lax.ppermute(value, 'blk', [(i, i ^ distance) for i in range(slabs)])  6.54 us
    ppermute x3, starting transfers between devices, along_both(): return lax.ppermute(value, ('db', 'blk'), pairs)  6.29 us
    pallas_call x1, Pallas kernels, sort_slabs(): pl.pallas_call(functools.partial(sort_kernel, len(slabs)), out_shape=[jax...  5.41 us
    ppermute x6, waiting for transfers between devices, along_db(): return lax.ppermute(value, 'db', [(i, i ^ distance) for i in range(groups)])  5.15 us
    ppermute x3, waiting for transfers between devices, along_both(): return lax.ppermute(value, ('db', 'blk'), pairs)  4.53 us
    pallas_call x3, Pallas kernels, score(): pl.pallas_call(functools.partial(score_kernel, len(after), len(pieces), l...  3.83 us
    unnamed x12, local copies, waits for them, and re-layouts  2.22 us
  transfers between devices with their start and end apart: 16, of which 4 were waited for; matrix products, arithmetic and copies ran while one was open for 0% of the time, Pallas kernels for 27%

profile of v3, /device:TPU:0, one launch (start us, length us, event | category | flops | bytes accessed | tf_op | source)
XLA Modules:
  0.0 49.1 jit_solution(1077878507324404137)
XLA Ops:
  0.0 0.5 collective-permute-start.2
  0.5 2.2 %prepare.1 = (s32[1,256]{1,0:T(1,128)}, bf16[128,768]{1,0:T(8,128)(2,1)}, bf16[128,768]{1,0:T(8,128)(2,1)}, bf16[128,768]{1,0:T(8,128)(2,1)}, bf16[128,768]{1,0:T(8,128)(2,1)}) custom-call(s32[1,256]{1,0:T(1,128)} %bitcast.5, bf16[256,768]{1,0:T(8,128)(2,1)} %queries_hbm.1), custom_call_target="tpu_custom_call" | custom-call | tf_op jit(solution)/shard_map/prepare/pallas_call | solution.py:84
  2.6 0.0 copy-start.5
  2.7 4.7 %collective-permute-start = (bf16[128,768]{1,0:T(8,128)(2,1)}, bf16[128,768]{1,0:T(8,128)(2,1)S(1)}, u32[]{:S(2)}, u32[]{:S(2)}) collective-permute-start(bf16[128,768]{1,0:T(8,128)(2,1)} %get-tuple-element.21), channel_id=1, source_target_pairs={{0,12},{4,8},{8,4},{12,0},{1,13},{5,9},{9,5},{13,1},{2,14},{6,10},... | collective-permute-start | bytes 589832 | tf_op jit(solution)/shard_map/ppermute | solution.py:192
  7.3 0.0 collective-permute-start.5
  7.3 0.2 collective-permute-start.1
  7.6 1.3 %copy-done = bf16[768,768]{1,0:T(8,128)(2,1)S(1)} copy-done((bf16[768,768]{1,0:T(8,128)(2,1)S(1)}, bf16[768,768]{1,0:T(8,128)(2,1)}, u32[]{:S(2)}) %copy-start) | copy-done | bytes 1179672
  8.8 0.9 %copy-done.3 = bf16[128,768]{1,0:T(8,128)(2,1)S(1)} copy-done((bf16[128,768]{1,0:T(8,128)(2,1)S(1)}, bf16[128,768]{1,0:T(8,128)(2,1)}, u32[]{:S(2)}) %copy-start.3) | copy-done | bytes 196632
  9.8 0.4 project.5.refs_1_
  10.2 1.6 %collective-permute-start.4 = (bf16[128,768]{1,0:T(8,128)(2,1)S(1)}, bf16[128,768]{1,0:T(8,128)(2,1)S(1)}, u32[]{:S(2)}, u32[]{:S(2)}) collective-permute-start(bf16[128,768]{1,0:T(8,128)(2,1)S(1)} %project.5.refs_1_), channel_id=1, source_target_pairs={{0,2},{1,3},{2,0},{3,1},{4,6},{5,7},{6,4},{7,5},{8,10},{9,11},{10,... | collective-permute-start | bytes 589832 | tf_op jit(solution)/shard_map/ppermute | solution.py:195
  11.7 0.0 collective-permute-done.1
  11.7 0.6 %collective-permute-start.11 = (bf16[128,768]{1,0:T(8,128)(2,1)}, bf16[128,768]{1,0:T(8,128)(2,1)S(1)}, u32[]{:S(2)}, u32[]{:S(2)}) collective-permute-start(bf16[128,768]{1,0:T(8,128)(2,1)} %get-tuple-element.32), channel_id=1, source_target_pairs={{0,8},{4,12},{8,0},{12,4},{1,9},{5,13},{9,1},{13,5},{2,10},{6,14},... | collective-permute-start | bytes 589832 | tf_op jit(solution)/shard_map/ppermute | solution.py:192
  12.4 0.0 collective-permute-done.2.refs_3_
  12.4 0.0 copy-done.4
  12.4 0.0 copy-done.5
  12.4 0.0 copy-start.1
  12.4 5.4 %sort_slabs.1 = (bf16[768,1024]{1,0:T(8,128)(2,1)S(1)}, bf16[768,1024]{1,0:T(8,128)(2,1)S(1)}) custom-call(s32[1,256]{1,0:T(1,128)S(1)} %copy-done.5, s32[1,1024]{1,0:T(1,128)S(1)} %bitcast.3, s32[1,1024]{1,0:T(1,128)S(1)} %bitcast.4, bf16[768,1024]{1,0:T(8,128)(2,1)S(1)} %copy-done.2, bf16[768,1024]{1,0:T(8,128)(2,1)} %collective-permute-done.2.refs_3_), custom_call_target="tpu_custom_call" | custom-call | tf_op jit(solution)/shard_map/sort_slabs/pallas_call | solution.py:118
  17.8 0.0 collective-permute-done.piece_ref
  17.9 0.4 project.4.refs_0_
  18.3 0.6 %collective-permute-start.3 = (bf16[128,768]{1,0:T(8,128)(2,1)S(1)}, bf16[128,768]{1,0:T(8,128)(2,1)S(1)}, u32[]{:S(2)}, u32[]{:S(2)}) collective-permute-start(bf16[128,768]{1,0:T(8,128)(2,1)S(1)} %project.4.refs_0_), channel_id=1, source_target_pairs={{0,2},{1,3},{2,0},{3,1},{4,6},{5,7},{6,4},{7,5},{8,10},{9,11},{10,... | collective-permute-start | bytes 589832 | tf_op jit(solution)/shard_map/ppermute | solution.py:195
  18.9 0.0 collective-permute-done.5.piece_ref
  18.9 0.4 project.6.refs_1_
  19.3 1.6 %collective-permute-start.6 = (bf16[128,768]{1,0:T(8,128)(2,1)S(1)}, bf16[128,768]{1,0:T(8,128)(2,1)S(1)}, u32[]{:S(2)}, u32[]{:S(2)}) collective-permute-start(bf16[128,768]{1,0:T(8,128)(2,1)S(1)} %project.6.refs_1_), channel_id=1, source_target_pairs={{0,2},{1,3},{2,0},{3,1},{4,6},{5,7},{6,4},{7,5},{8,10},{9,11},{10,... | collective-permute-start | bytes 589832 | tf_op jit(solution)/shard_map/ppermute | solution.py:195
  20.9 4.0 %collective-permute-done.11.piece_ref = bf16[128,768]{1,0:T(8,128)(2,1)S(1)} collective-permute-done((bf16[128,768]{1,0:T(8,128)(2,1)}, bf16[128,768]{1,0:T(8,128)(2,1)S(1)}, u32[]{:S(2)}, u32[]{:S(2)}) %collective-permute-start.11) | collective-permute-done | bytes 196640 | tf_op jit(solution)/shard_map/ppermute | solution.py:192
  24.9 0.4 project.7.refs_4_
  25.3 1.6 %collective-permute-start.12 = (bf16[128,768]{1,0:T(8,128)(2,1)S(1)}, bf16[128,768]{1,0:T(8,128)(2,1)S(1)}, u32[]{:S(2)}, u32[]{:S(2)}) collective-permute-start(bf16[128,768]{1,0:T(8,128)(2,1)S(1)} %project.7.refs_4_), channel_id=1, source_target_pairs={{0,2},{1,3},{2,0},{3,1},{4,6},{5,7},{6,4},{7,5},{8,10},{9,11},{10,... | collective-permute-start | bytes 589832 | tf_op jit(solution)/shard_map/ppermute | solution.py:195
  26.9 0.0 collective-permute-done.4.refs_3_
  26.9 0.0 collective-permute-done.3.refs_2_
  26.9 1.8 %score.3 = (f32[128,128]{1,0:T(8,128)S(1)}, f32[128,128]{1,0:T(8,128)S(1)}, f32[128,128]{1,0:T(8,128)S(1)}, f32[128,128]{1,0:T(8,128)S(1)}) custom-call(bf16[128,768]{1,0:T(8,128)(2,1)S(1)} %project.4.refs_0_, bf16[128,768]{1,0:T(8,128)(2,1)S(1)} %project.5.refs_1_, bf16[128,768]{1,0:T(8,128)(2,1)S(1)} %collective-permute-done.3.refs_2_, ...), custom_call_target="tpu_custom_call" | custom-call | flops 2000000000 | tf_op jit(solution)/shard_map/score/pallas_call | solution.py:148
  28.7 0.6 %collective-permute-start.10 = (f32[128,128]{1,0:T(8,128)S(1)}, f32[128,128]{1,0:T(8,128)S(1)}, u32[]{:S(2)}, u32[]{:S(2)}) collective-permute-start(f32[128,128]{1,0:T(8,128)S(1)} %get-tuple-element.26.refs_0_), channel_id=1, source_target_pairs={{0,2},{1,3},{2,0},{3,1},{4,6},{5,7},{6,4},{7,5},{8,10},{9,11},{10,... | collective-permute-start | bytes 196616 | tf_op jit(solution)/shard_map/ppermute | solution.py:195
  29.3 2.8 %collective-permute-start.8 = (f32[128,128]{1,0:T(8,128)S(1)}, f32[128,128]{1,0:T(8,128)S(1)}, u32[]{:S(2)}, u32[]{:S(2)}) collective-permute-start(f32[128,128]{1,0:T(8,128)S(1)} %get-tuple-element.30), channel_id=1, source_target_pairs={{0,12},{4,8},{8,4},{12,0},{1,13},{5,9},{9,5},{13,1},{2,14},{6,10},... | collective-permute-start | bytes 196616 | tf_op jit(solution)/shard_map/ppermute | solution.py:192
  32.1 2.0 %collective-permute-start.9 = (f32[128,128]{1,0:T(8,128)S(1)}, f32[128,128]{1,0:T(8,128)S(1)}, u32[]{:S(2)}, u32[]{:S(2)}) collective-permute-start(f32[128,128]{1,0:T(8,128)S(1)} %get-tuple-element.31), channel_id=1, source_target_pairs={{0,14},{1,15},{2,12},{3,13},{4,10},{5,11},{6,8},{7,9},{8,6},{9,7},... | collective-permute-start | bytes 196616 | tf_op jit(solution)/shard_map/ppermute | solution.py:203
  34.1 0.0 collective-permute-done.6.refs_2_
  34.1 1.0 %score.4 = (f32[128,128]{1,0:T(8,128)S(1)}, f32[128,128]{1,0:T(8,128)S(1)}) custom-call(f32[128,128]{1,0:T(8,128)S(1)} %get-tuple-element.26.refs_0_, bf16[128,768]{1,0:T(8,128)(2,1)S(1)} %project.6.refs_1_, bf16[128,768]{1,0:T(8,128)(2,1)S(1)} %collective-permute-done.6.refs_2_, bf16[768,1024]{1,0:T(8,128)(2,1)S(1)} %get-tuple-element.22.refs_0_.refs_4_.refs_3_.refs_6_, ...), custom_call_target="tpu_custom_call" | custom-call | flops 1000000000 | tf_op jit(solution)/shard_map/score/pallas_call | solution.py:148
  35.1 0.1 collective-permute-start.14
  35.2 0.0 collective-permute-done.12.refs_5_
  35.2 2.0 %collective-permute-start.7 = (f32[128,128]{1,0:T(8,128)S(1)}, f32[128,128]{1,0:T(8,128)S(1)}, u32[]{:S(2)}, u32[]{:S(2)}) collective-permute-start(f32[128,128]{1,0:T(8,128)S(1)} %get-tuple-element.28), channel_id=1, source_target_pairs={{0,4},{4,0},{8,12},{12,8},{1,5},{5,1},{9,13},{13,9},{2,6},{6,2},{1... | collective-permute-start | bytes 196616 | tf_op jit(solution)/shard_map/ppermute | solution.py:192
  37.2 0.0 collective-permute-done.10.refs_3_.refs_4_
  37.2 0.0 collective-permute-done.8.refs_1_.refs_3_
  37.2 2.0 %collective-permute-done.9.refs_2_.refs_7_ = f32[128,128]{1,0:T(8,128)S(1)} collective-permute-done((f32[128,128]{1,0:T(8,128)S(1)}, f32[128,128]{1,0:T(8,128)S(1)}, u32[]{:S(2)}, u32[]{:S(2)}) %collective-permute-start.9) | collective-permute-done | bytes 65568 | tf_op jit(solution)/shard_map/ppermute | solution.py:203
  39.2 1.0 %score.5 = (f32[128,128]{1,0:T(8,128)S(1)}, f32[128,128]{1,0:T(8,128)S(1)}) custom-call(f32[128,128]{1,0:T(8,128)S(1)} %get-tuple-element.29.refs_0_, f32[128,128]{1,0:T(8,128)S(1)} %collective-permute-done.8.refs_1_.refs_3_, f32[128,128]{1,0:T(8,128)S(1)} %collective-permute-done.9.refs_2_.refs_7_, f32[128,128]{1,0:T(8,128)S(1)} %collective-permute-done.10.refs_3_.refs_4_, ...), custom_call_target="tpu_custom_call" | custom-call | flops 1000000000 | tf_op jit(solution)/shard_map/score/pallas_call | solution.py:148
  40.2 0.1 collective-permute-start.13
  40.2 4.2 %collective-permute-start.15 = (f32[128,128]{1,0:T(8,128)S(1)}, f32[128,128]{1,0:T(8,128)S(1)}, u32[]{:S(2)}, u32[]{:S(2)}) collective-permute-start(f32[128,128]{1,0:T(8,128)S(1)} %get-tuple-element.34), channel_id=1, source_target_pairs={{0,10},{1,11},{2,8},{3,9},{4,14},{5,15},{6,12},{7,13},{8,2},{9,3},... | collective-permute-start | bytes 196616 | tf_op jit(solution)/shard_map/ppermute | solution.py:203
  44.5 0.0 collective-permute-done.14.refs_5_
  44.5 0.0 collective-permute-done.7.refs_1_
  44.5 1.1 %collective-permute-done.13.refs_2_ = f32[128,128]{1,0:T(8,128)S(1)} collective-permute-done((f32[128,128]{1,0:T(8,128)S(1)}, f32[128,128]{1,0:T(8,128)S(1)}, u32[]{:S(2)}, u32[]{:S(2)}) %collective-permute-start.13) | collective-permute-done | bytes 65568 | tf_op jit(solution)/shard_map/ppermute | solution.py:192
  45.6 2.5 %collective-permute-done.15.refs_6_ = f32[128,128]{1,0:T(8,128)S(1)} collective-permute-done((f32[128,128]{1,0:T(8,128)S(1)}, f32[128,128]{1,0:T(8,128)S(1)}, u32[]{:S(2)}, u32[]{:S(2)}) %collective-permute-start.15) | collective-permute-done | bytes 65568 | tf_op jit(solution)/shard_map/ppermute | solution.py:203
  48.1 1.0 %select.1 = f32[256,128]{1,0:T(8,128)} custom-call(s32[1,256]{1,0:T(1,128)S(1)} %copy-done.5, f32[128,128]{1,0:T(8,128)S(1)} %get-tuple-element.25.refs_0_, f32[128,128]{1,0:T(8,128)S(1)} %collective-permute-done.7.refs_1_, f32[128,128]{1,0:T(8,128)S(1)} %collective-permute-done.13.refs_2_, f32[128,128]{1,0:T(8,128)S(1)} %collective-permute-done.8.refs_1_.refs_3_, ...), custom_call_target="tpu_custom_call" | custom-call | tf_op jit(solution)/shard_map/select/pallas_call | solution.py:176
  (6 shorter events, 0.0 us)
Async XLA Ops:
  0.0 12.4 %copy-start.4 = (s32[1024]{0:T(1024)S(1)}, s32[1024]{0:T(1024)}, u32[]{:S(2)}) copy-start(s32[1024]{0:T(1024)} %param.8) | copy-start | bytes 12292
  0.0 12.4 %collective-permute-start.2 = (bf16[768,1024]{1,0:T(8,128)(2,1)}, bf16[768,1024]{1,0:T(8,128)(2,1)}, u32[]{:S(2)}, u32[]{:S(2)}) collective-permute-start(bf16[768,1024]{1,0:T(8,128)(2,1)} %refs_2_.1), channel_id=1, source_target_pairs={{0,1},{1,0},{2,3},{3,2},{4,5},{5,4},{6,7},{7,6},{8,9},{9,8},{10,11... | collective-permute-start | bytes 4718600 | tf_op jit(solution)/shard_map/ppermute | solution.py:195
  2.6 9.7 %copy-start.5 = (s32[1,256]{1,0:T(1,128)S(1)}, s32[1,256]{1,0:T(1,128)}, u32[]{:S(2)}) copy-start(s32[1,256]{1,0:T(1,128)} %get-tuple-element.20.after_ref.position_ref) | copy-start | bytes 3076
  2.7 15.2 %collective-permute-start = (bf16[128,768]{1,0:T(8,128)(2,1)}, bf16[128,768]{1,0:T(8,128)(2,1)S(1)}, u32[]{:S(2)}, u32[]{:S(2)}) collective-permute-start(bf16[128,768]{1,0:T(8,128)(2,1)} %get-tuple-element.21), channel_id=1, source_target_pairs={{0,12},{4,8},{8,4},{12,0},{1,13},{5,9},{9,5},{13,1},{2,14},{6,10},... | collective-permute-start | bytes 589832 | tf_op jit(solution)/shard_map/ppermute | solution.py:192
  7.3 11.5 %collective-permute-start.5 = (bf16[128,768]{1,0:T(8,128)(2,1)}, bf16[128,768]{1,0:T(8,128)(2,1)S(1)}, u32[]{:S(2)}, u32[]{:S(2)}) collective-permute-start(bf16[128,768]{1,0:T(8,128)(2,1)} %get-tuple-element.27), channel_id=1, source_target_pairs={{0,4},{4,0},{8,12},{12,8},{1,5},{5,1},{9,13},{13,9},{2,6},{6,2},{1... | collective-permute-start | bytes 589832 | tf_op jit(solution)/shard_map/ppermute | solution.py:192
  7.3 4.4 %collective-permute-start.1 = (s32[1024]{0:T(1024)}, s32[1024]{0:T(1024)S(1)}, u32[]{:S(2)}, u32[]{:S(2)}) collective-permute-start(s32[1024]{0:T(1024)} %param.8), channel_id=1, source_target_pairs={{0,1},{1,0},{2,3},{3,2},{4,5},{5,4},{6,7},{7,6},{8,9},{9,8},{10,11... | collective-permute-start | bytes 12296 | tf_op jit(solution)/shard_map/ppermute | solution.py:195
  7.6 1.3 %copy-start = (bf16[768,768]{1,0:T(8,128)(2,1)S(1)}, bf16[768,768]{1,0:T(8,128)(2,1)}, u32[]{:S(2)}) copy-start(bf16[768,768]{1,0:T(8,128)(2,1)} %projection_ref.7) | copy-start | bytes 3538948
  8.8 0.9 %copy-start.3 = (bf16[128,768]{1,0:T(8,128)(2,1)S(1)}, bf16[128,768]{1,0:T(8,128)(2,1)}, u32[]{:S(2)}) copy-start(bf16[128,768]{1,0:T(8,128)(2,1)} %get-tuple-element.23.piece_ref) | copy-start | bytes 589828
  9.8 2.6 %copy-start.2 = (bf16[768,1024]{1,0:T(8,128)(2,1)S(1)}, bf16[768,1024]{1,0:T(8,128)(2,1)}, u32[]{:S(2)}) copy-start(bf16[768,1024]{1,0:T(8,128)(2,1)} %refs_2_.1) | copy-start | bytes 4718596
  10.2 16.7 %collective-permute-start.4 = (bf16[128,768]{1,0:T(8,128)(2,1)S(1)}, bf16[128,768]{1,0:T(8,128)(2,1)S(1)}, u32[]{:S(2)}, u32[]{:S(2)}) collective-permute-start(bf16[128,768]{1,0:T(8,128)(2,1)S(1)} %project.5.refs_1_), channel_id=1, source_target_pairs={{0,2},{1,3},{2,0},{3,1},{4,6},{5,7},{6,4},{7,5},{8,10},{9,11},{10,... | collective-permute-start | bytes 589832 | tf_op jit(solution)/shard_map/ppermute | solution.py:195
  11.7 13.2 %collective-permute-start.11 = (bf16[128,768]{1,0:T(8,128)(2,1)}, bf16[128,768]{1,0:T(8,128)(2,1)S(1)}, u32[]{:S(2)}, u32[]{:S(2)}) collective-permute-start(bf16[128,768]{1,0:T(8,128)(2,1)} %get-tuple-element.32), channel_id=1, source_target_pairs={{0,8},{4,12},{8,0},{12,4},{1,9},{5,13},{9,1},{13,5},{2,10},{6,14},... | collective-permute-start | bytes 589832 | tf_op jit(solution)/shard_map/ppermute | solution.py:192
  12.4 5.4 %copy-start.1 = (bf16[768,768]{1,0:T(8,128)(2,1)S(1)}, bf16[768,768]{1,0:T(8,128)(2,1)}, u32[]{:S(2)}) copy-start(bf16[768,768]{1,0:T(8,128)(2,1)} %projection_ref.7) | copy-start | bytes 3538948
  18.3 8.6 %collective-permute-start.3 = (bf16[128,768]{1,0:T(8,128)(2,1)S(1)}, bf16[128,768]{1,0:T(8,128)(2,1)S(1)}, u32[]{:S(2)}, u32[]{:S(2)}) collective-permute-start(bf16[128,768]{1,0:T(8,128)(2,1)S(1)} %project.4.refs_0_), channel_id=1, source_target_pairs={{0,2},{1,3},{2,0},{3,1},{4,6},{5,7},{6,4},{7,5},{8,10},{9,11},{10,... | collective-permute-start | bytes 589832 | tf_op jit(solution)/shard_map/ppermute | solution.py:195
  19.3 14.8 %collective-permute-start.6 = (bf16[128,768]{1,0:T(8,128)(2,1)S(1)}, bf16[128,768]{1,0:T(8,128)(2,1)S(1)}, u32[]{:S(2)}, u32[]{:S(2)}) collective-permute-start(bf16[128,768]{1,0:T(8,128)(2,1)S(1)} %project.6.refs_1_), channel_id=1, source_target_pairs={{0,2},{1,3},{2,0},{3,1},{4,6},{5,7},{6,4},{7,5},{8,10},{9,11},{10,... | collective-permute-start | bytes 589832 | tf_op jit(solution)/shard_map/ppermute | solution.py:195
  25.3 9.8 %collective-permute-start.12 = (bf16[128,768]{1,0:T(8,128)(2,1)S(1)}, bf16[128,768]{1,0:T(8,128)(2,1)S(1)}, u32[]{:S(2)}, u32[]{:S(2)}) collective-permute-start(bf16[128,768]{1,0:T(8,128)(2,1)S(1)} %project.7.refs_4_), channel_id=1, source_target_pairs={{0,2},{1,3},{2,0},{3,1},{4,6},{5,7},{6,4},{7,5},{8,10},{9,11},{10,... | collective-permute-start | bytes 589832 | tf_op jit(solution)/shard_map/ppermute | solution.py:195
  28.7 8.4 %collective-permute-start.10 = (f32[128,128]{1,0:T(8,128)S(1)}, f32[128,128]{1,0:T(8,128)S(1)}, u32[]{:S(2)}, u32[]{:S(2)}) collective-permute-start(f32[128,128]{1,0:T(8,128)S(1)} %get-tuple-element.26.refs_0_), channel_id=1, source_target_pairs={{0,2},{1,3},{2,0},{3,1},{4,6},{5,7},{6,4},{7,5},{8,10},{9,11},{10,... | collective-permute-start | bytes 196616 | tf_op jit(solution)/shard_map/ppermute | solution.py:195
  29.3 7.8 %collective-permute-start.8 = (f32[128,128]{1,0:T(8,128)S(1)}, f32[128,128]{1,0:T(8,128)S(1)}, u32[]{:S(2)}, u32[]{:S(2)}) collective-permute-start(f32[128,128]{1,0:T(8,128)S(1)} %get-tuple-element.30), channel_id=1, source_target_pairs={{0,12},{4,8},{8,4},{12,0},{1,13},{5,9},{9,5},{13,1},{2,14},{6,10},... | collective-permute-start | bytes 196616 | tf_op jit(solution)/shard_map/ppermute | solution.py:192
  32.1 7.1 %collective-permute-start.9 = (f32[128,128]{1,0:T(8,128)S(1)}, f32[128,128]{1,0:T(8,128)S(1)}, u32[]{:S(2)}, u32[]{:S(2)}) collective-permute-start(f32[128,128]{1,0:T(8,128)S(1)} %get-tuple-element.31), channel_id=1, source_target_pairs={{0,14},{1,15},{2,12},{3,13},{4,10},{5,11},{6,8},{7,9},{8,6},{9,7},... | collective-permute-start | bytes 196616 | tf_op jit(solution)/shard_map/ppermute | solution.py:203
  35.1 9.4 %collective-permute-start.14 = (f32[128,128]{1,0:T(8,128)S(1)}, f32[128,128]{1,0:T(8,128)S(1)}, u32[]{:S(2)}, u32[]{:S(2)}) collective-permute-start(f32[128,128]{1,0:T(8,128)S(1)} %get-tuple-element.29.refs_0_), channel_id=1, source_target_pairs={{0,6},{1,7},{2,4},{3,5},{4,2},{5,3},{6,0},{7,1},{8,14},{9,15},{10,... | collective-permute-start | bytes 196616 | tf_op jit(solution)/shard_map/ppermute | solution.py:203
  35.2 9.3 %collective-permute-start.7 = (f32[128,128]{1,0:T(8,128)S(1)}, f32[128,128]{1,0:T(8,128)S(1)}, u32[]{:S(2)}, u32[]{:S(2)}) collective-permute-start(f32[128,128]{1,0:T(8,128)S(1)} %get-tuple-element.28), channel_id=1, source_target_pairs={{0,4},{4,0},{8,12},{12,8},{1,5},{5,1},{9,13},{13,9},{2,6},{6,2},{1... | collective-permute-start | bytes 196616 | tf_op jit(solution)/shard_map/ppermute | solution.py:192
  40.2 5.4 %collective-permute-start.13 = (f32[128,128]{1,0:T(8,128)S(1)}, f32[128,128]{1,0:T(8,128)S(1)}, u32[]{:S(2)}, u32[]{:S(2)}) collective-permute-start(f32[128,128]{1,0:T(8,128)S(1)} %get-tuple-element.33), channel_id=1, source_target_pairs={{0,8},{4,12},{8,0},{12,4},{1,9},{5,13},{9,1},{13,5},{2,10},{6,14},... | collective-permute-start | bytes 196616 | tf_op jit(solution)/shard_map/ppermute | solution.py:192
  40.2 7.9 %collective-permute-start.15 = (f32[128,128]{1,0:T(8,128)S(1)}, f32[128,128]{1,0:T(8,128)S(1)}, u32[]{:S(2)}, u32[]{:S(2)}) collective-permute-start(f32[128,128]{1,0:T(8,128)S(1)} %get-tuple-element.34), channel_id=1, source_target_pairs={{0,10},{1,11},{2,8},{3,9},{4,14},{5,15},{6,12},{7,13},{8,2},{9,3},... | collective-permute-start | bytes 196616 | tf_op jit(solution)/shard_map/ppermute | solution.py:203

commit v4 on v3

--- a/solution.py
+++ b/solution.py
@@ -108,26 +108,31 @@
     )(piece, projection, *after)
 
 
-def sort_kernel(slabs, after_ref, *refs):
-    for bins_ref, slab_ref, sorted_ref in zip(refs[:slabs], refs[slabs : 2 * slabs], refs[2 * slabs :]):
-        sorted_ref[...] = sorted_columns(bins_ref[...], slab_ref[...])
-
-
-def sort_slabs(after, bins, slabs):
-    width = slabs[0].shape[1]
-    return pl.pallas_call(
-        functools.partial(sort_kernel, len(slabs)),
-        out_shape=[jax.ShapeDtypeStruct(slab.shape, jnp.bfloat16) for slab in slabs],
-        in_specs=[pl.BlockSpec(memory_space=pl.ANY)] + [pl.BlockSpec(memory_space=pltpu.VMEM)] * (2 * len(slabs)),
+def sort_kernel(after_ref, bins_ref, slab_ref, other_bins_ref, other_hbm, sorted_ref, other_sorted_ref, other_ref, sem):
+    copy = pltpu.make_async_copy(other_hbm, other_ref, sem)
+    copy.start()
+    sorted_ref[...] = sorted_columns(bins_ref[...], slab_ref[...])
+    copy.wait()
+    other_sorted_ref[...] = sorted_columns(other_bins_ref[...], other_ref[...])
+
+
+def sort_slabs(after, bins, slab, other_bins, other_slab):
+    width = slab.shape[1]
+    vmem, hbm = pl.BlockSpec(memory_space=pltpu.VMEM), pl.BlockSpec(memory_space=pltpu.HBM)
+    return pl.pallas_call(
+        sort_kernel,
+        out_shape=[jax.ShapeDtypeStruct(slab.shape, jnp.bfloat16)] * 2,
+        in_specs=[pl.BlockSpec(memory_space=pl.ANY), vmem, vmem, vmem, hbm],
+        scratch_shapes=[pltpu.VMEM(slab.shape, slab.dtype), pltpu.SemaphoreType.DMA],
         compiler_params=params(),
         cost_estimate=us(0),
         name="sort_slabs",
-    )(after, *[row.reshape(1, width) for row in bins], *slabs)
-
-
-def score_kernel(afters, pieces, outs, *refs):
+    )(after, bins.reshape(1, width), slab, other_bins.reshape(1, width), other_slab)
+
+
+def score_kernel(afters, pieces, *refs):
     refs = refs[afters:]
-    piece_refs, slab_refs, out_refs = refs[:pieces], refs[pieces:-outs], refs[-outs:]
+    piece_refs, slab_refs, out_refs = refs[:pieces], refs[pieces : pieces + 2], refs[pieces + 2 :]
     rows = jnp.concatenate([ref[...] for ref in piece_refs], axis=0)
     best = None
     step = 2 * BINS
@@ -137,50 +142,59 @@
             for first in range(0, step, BINS):
                 part = scores[:, first : first + BINS]
                 best = part if best is None else jnp.maximum(best, part)
-    start = 0
-    for ref in out_refs:
-        ref[...] = best[start : start + ref.shape[0]]
-        start += ref.shape[0]
-
-
-def score(after, pieces, slabs, sizes):
-    rows = sum(sizes)
-    return pl.pallas_call(
-        functools.partial(score_kernel, len(after), len(pieces), len(sizes)),
-        out_shape=[jax.ShapeDtypeStruct((size, BINS), jnp.float32) for size in sizes],
+    count = best.shape[0] // len(out_refs)
+    for i, ref in enumerate(out_refs):
+        ref[...] = best[i * count : (i + 1) * count]
+
+
+def score(after, pieces, slabs):
+    return pl.pallas_call(
+        functools.partial(score_kernel, len(after), len(pieces)),
+        out_shape=[jax.ShapeDtypeStruct((piece.shape[0], BINS), jnp.float32) for piece in pieces],
         in_specs=[pl.BlockSpec(memory_space=pl.ANY)] * len(after)
         + [pl.BlockSpec(memory_space=pltpu.VMEM)] * (len(pieces) + len(slabs)),
         compiler_params=params(),
-        cost_estimate=us(rows / 256),
+        cost_estimate=us(0),
         name="score",
     )(*after, *pieces, *slabs)
 
 
-def select_kernel(pieces, position_ref, *refs):
-    out_ref = refs[-1]
-    answers = [jnp.maximum(a[...], b[...]) for a, b in zip(refs[:pieces], refs[pieces : 2 * pieces])]
-    answers = jnp.concatenate(answers, axis=0)
-    high = answers.astype(jnp.bfloat16)
-    rest = answers - high.astype(jnp.float32)
-    middle = rest.astype(jnp.bfloat16)
-    low = (rest - middle.astype(jnp.float32)).astype(jnp.bfloat16)
-    parts = jnp.concatenate([high, middle, low], axis=1)
+def select_kernel(distances, position_ref, *refs):
+    pieces = len(distances)
+    first_refs, second_refs, others, out_ref = refs[:pieces], refs[pieces : 2 * pieces], refs[2 * pieces : -1], refs[-1]
     position = position_ref[...]
-    slots = lax.broadcasted_iota(jnp.int32, (answers.shape[0], position.shape[1]), 0)
-    chooser = jnp.where(slots == position, 1.0, 0.0).astype(jnp.bfloat16)
-    chosen = lax.dot_general(chooser, parts, (((0,), (0,)), ((), ())), preferred_element_type=jnp.float32)
-    out_ref[...] = logit_scale * ((chosen[:, :BINS] + chosen[:, BINS : 2 * BINS]) + chosen[:, 2 * BINS :])
-
-
-def select(position, first, second):
-    return pl.pallas_call(
-        functools.partial(select_kernel, len(first)),
+    parts, choosers = [], []
+    for k, first_ref, second_ref in zip(distances, first_refs, second_refs):
+        values = jnp.maximum(first_ref[...], second_ref[...])
+        high = values.astype(jnp.bfloat16)
+        rest = values - high.astype(jnp.float32)
+        middle = rest.astype(jnp.bfloat16)
+        low = (rest - middle.astype(jnp.float32)).astype(jnp.bfloat16)
+        parts.append(jnp.concatenate([high, middle, low], axis=1))
+        slots = lax.broadcasted_iota(jnp.int32, (values.shape[0], position.shape[1]), 0)
+        choosers.append(jnp.where(slots + k * values.shape[0] == position, 1.0, 0.0).astype(jnp.bfloat16))
+    chosen = lax.dot_general(
+        jnp.concatenate(choosers, axis=0),
+        jnp.concatenate(parts, axis=0),
+        (((0,), (0,)), ((), ())),
+        preferred_element_type=jnp.float32,
+    )
+    total = logit_scale * ((chosen[:, :BINS] + chosen[:, BINS : 2 * BINS]) + chosen[:, 2 * BINS :])
+    for ref in others:
+        total += ref[...]
+    out_ref[...] = total
+
+
+def select(position, distances, answers, others, time):
+    flat = [answers[k][i] for i in (0, 1) for k in distances] + others
+    return pl.pallas_call(
+        functools.partial(select_kernel, distances),
         out_shape=jax.ShapeDtypeStruct((position.shape[1], BINS), jnp.float32),
-        in_specs=[pl.BlockSpec(memory_space=pltpu.VMEM)] * (1 + 2 * len(first)),
-        compiler_params=params(),
-        cost_estimate=us(0),
+        in_specs=[pl.BlockSpec(memory_space=pltpu.VMEM)] * (1 + len(flat)),
+        compiler_params=params(),
+        cost_estimate=us(time),
         name="select",
-    )(position, *first, *second)
+    )(position, *flat)
 
 
 def device_paired(queries, projection, vectors, bins, routes):
@@ -203,26 +217,26 @@
         return lax.ppermute(value, ("db", "blk"), pairs)
 
     position, *pieces = prepare(queries, routes, groups, capacity)
+    other_slab, other_bins = along_blk(vectors, 1), along_blk(bins, 1)
+    slabs_here = sort_slabs(position, bins, vectors, other_bins, other_slab)
     arrived = {k: along_db(pieces[k], k) for k in (3, 1, 2)}
-    slabs_here = sort_slabs(position, [bins, along_blk(bins, 1)], [vectors, along_blk(vectors, 1)])
-    here = {0: project(pieces[0], projection)}
-    for k in (3, 1, 2):
-        here[k] = project(arrived[k], projection, slabs_here[0])
-    partner = {k: along_blk(here[k], 2) for k in (0, 3, 1, 2)}
-    first, second = {}, {}
-
-    def scores(wave, *after):
-        found = score(after, [here[k] for k in wave] + [partner[k] for k in wave], slabs_here, [capacity] * 2 * len(wave))
+    here, partner = {}, {}
+    for k, piece, after in (
+        (0, pieces[0], [other_bins]),
+        (1, arrived[1], []),
+        (3, arrived[3], []),
+        (2, arrived[2], [slabs_here[0]]),
+    ):
+        here[k] = project(piece, projection, *after)
+        partner[k] = along_blk(here[k], 2)
+    answers, after = {}, []
+    for wave in ((3, 0), (1,), (2,)):
+        found = score(after, [here[k] for k in wave] + [partner[k] for k in wave], slabs_here)
         for k, mine, theirs in zip(wave, found[: len(wave)], found[len(wave) :]):
-            first[k] = along_db(mine, k) if k else mine
-            second[k] = along_both(theirs, k, 2) if k else along_blk(theirs, 2)
-        return found[-1]
-
-    done = scores([3, 0])
-    done = scores([1], done)
-    scores([2], done, first[3], second[3], second[0])
-    ids = range(groups)
-    return select(position, [first[k] for k in ids], [second[k] for k in ids])
+            answers[k] = (along_db(mine, k), along_both(theirs, k, 2)) if k else (mine, along_blk(theirs, 2))
+        after = found[-1:]
+    some = select(position, (3,), answers, [], 3)
+    return select(position, (0, 1, 2), answers, [some], 0)
 
 
 def binned_max(query_rows, columns):

time: 49.3 us -> 46.9 us (0.951)
  waiting for transfers between devices: 9.69 us -> 7.74 us
  Pallas kernels: 14.1 us -> 13.5 us
    ppermute x3, waiting for transfers between devices: 4.53 us -> 1.16 us  [along_both(): return lax.ppermute(value, ('db', 'blk'), pairs)]
    ppermute x3, starting transfers between devices: 6.29 us -> 4.15 us  [along_both(): return lax.ppermute(value, ('db', 'blk'), pairs)]
    ppermute x7, waiting for transfers between devices: 0.02 us -> 1.39 us  [along_blk(): return lax.ppermute(value, 'blk', [(i, i ^ distance) for i in range(slabs)])]
    ppermute x7, starting transfers between devices: 6.54 us -> 7.84 us  [along_blk(): return lax.ppermute(value, 'blk', [(i, i ^ distance) for i in range(slabs)])]
    ppermute x6, starting transfers between devices: 10.1 us -> 11.1 us  [along_db(): return lax.ppermute(value, 'db', [(i, i ^ distance) for i in range(groups)])]
    pallas_call x5 -> x6, Pallas kernels: 10.2 us -> 9.6 us  [the longest x1 4.55 us: sort_slabs(): pl.pallas_call(sort_kernel, out_shape=[jax.ShapeDtypeStruct(slab.shape, j...]
where the time goes in v4:
time: 46.9 us; the launch traced here: 46.7 us
  starting transfers between devices  23.1 us (49%)
  Pallas kernels  13.5 us (29%)
  waiting for transfers between devices  7.74 us (17%)
  local copies, waits for them, and re-layouts  2.22 us (5%)
    ppermute x6, starting transfers between devices, along_db(): return lax.ppermute(value, 'db', [(i, i ^ distance) for i in range(groups)])  11.1 us
    ppermute x7, starting transfers between devices, along_blk(): return lax.ppermute(value, 'blk', [(i, i ^ distance) for i in range(slabs)])  7.84 us
    ppermute x6, waiting for transfers between devices, along_db(): return lax.ppermute(value, 'db', [(i, i ^ distance) for i in range(groups)])  5.19 us
    pallas_call x1, Pallas kernels, sort_slabs(): pl.pallas_call(sort_kernel, out_shape=[jax.ShapeDtypeStruct(slab.shape, j...  4.55 us
    ppermute x3, starting transfers between devices, along_both(): return lax.ppermute(value, ('db', 'blk'), pairs)  4.15 us
    pallas_call x3, Pallas kernels, score(): pl.pallas_call(functools.partial(score_kernel, len(after), len(pieces)),...  3.83 us
    unnamed x12, local copies, waits for them, and re-layouts  2.22 us
    pallas_call x1, Pallas kernels, prepare(): pl.pallas_call(functools.partial(prepare_kernel, groups, capacity), out_s...  2.18 us
  transfers between devices with their start and end apart: 16, of which 4 were waited for; matrix products, arithmetic and copies ran while one was open for 0% of the time, Pallas kernels for 27%

profile of v4, /device:TPU:0, one launch (start us, length us, event | category | flops | bytes accessed | tf_op | source)
XLA Modules:
  0.0 46.7 jit_solution(3500524324748837749)
XLA Ops:
  0.0 0.5 collective-permute-start.4
  0.5 2.2 %prepare.1 = (s32[1,256]{1,0:T(1,128)}, bf16[128,768]{1,0:T(8,128)(2,1)}, bf16[128,768]{1,0:T(8,128)(2,1)}, bf16[128,768]{1,0:T(8,128)(2,1)}, bf16[128,768]{1,0:T(8,128)(2,1)}) custom-call(s32[1,256]{1,0:T(1,128)} %bitcast.5, bf16[256,768]{1,0:T(8,128)(2,1)} %queries_hbm.1), custom_call_target="tpu_custom_call" | custom-call | tf_op jit(solution)/shard_map/prepare/pallas_call | solution.py:84
  2.6 4.7 %collective-permute-start = (bf16[128,768]{1,0:T(8,128)(2,1)}, bf16[128,768]{1,0:T(8,128)(2,1)S(1)}, u32[]{:S(2)}, u32[]{:S(2)}) collective-permute-start(bf16[128,768]{1,0:T(8,128)(2,1)} %get-tuple-element.21), channel_id=1, source_target_pairs={{0,12},{4,8},{8,4},{12,0},{1,13},{5,9},{9,5},{13,1},{2,14},{6,10},... | collective-permute-start | bytes 589832 | tf_op jit(solution)/shard_map/ppermute | solution.py:206
  7.3 0.0 collective-permute-start.5
  7.3 0.6 %collective-permute-start.8 = (bf16[128,768]{1,0:T(8,128)(2,1)}, bf16[128,768]{1,0:T(8,128)(2,1)S(1)}, u32[]{:S(2)}, u32[]{:S(2)}) collective-permute-start(bf16[128,768]{1,0:T(8,128)(2,1)} %get-tuple-element.30), channel_id=1, source_target_pairs={{0,8},{4,12},{8,0},{12,4},{1,9},{5,13},{9,1},{13,5},{2,10},{6,14},... | collective-permute-start | bytes 589832 | tf_op jit(solution)/shard_map/ppermute | solution.py:206
  8.0 0.0 collective-permute-start.1
  8.0 1.4 %collective-permute-done.1.refs_0_ = s32[1024]{0:T(1024)S(1)} collective-permute-done((s32[1024]{0:T(1024)}, s32[1024]{0:T(1024)S(1)}, u32[]{:S(2)}, u32[]{:S(2)}) %collective-permute-start.1) | collective-permute-done | bytes 4128 | tf_op jit(solution)/shard_map/ppermute | solution.py:209
  9.3 1.3 %copy-done = bf16[768,768]{1,0:T(8,128)(2,1)S(1)} copy-done((bf16[768,768]{1,0:T(8,128)(2,1)S(1)}, bf16[768,768]{1,0:T(8,128)(2,1)}, u32[]{:S(2)}) %copy-start) | copy-done | bytes 1179672
  10.6 0.9 %copy-done.3 = bf16[128,768]{1,0:T(8,128)(2,1)S(1)} copy-done((bf16[128,768]{1,0:T(8,128)(2,1)S(1)}, bf16[128,768]{1,0:T(8,128)(2,1)}, u32[]{:S(2)}) %copy-start.3) | copy-done | bytes 196632
  11.5 0.4 project.5.refs_1_
  12.0 0.0 copy-start.2
  12.0 0.0 copy-start.4
  12.0 0.0 copy-start.5
  12.0 1.7 %collective-permute-start.3 = (bf16[128,768]{1,0:T(8,128)(2,1)S(1)}, bf16[128,768]{1,0:T(8,128)(2,1)S(1)}, u32[]{:S(2)}, u32[]{:S(2)}) collective-permute-start(bf16[128,768]{1,0:T(8,128)(2,1)S(1)} %project.5.refs_1_), channel_id=1, source_target_pairs={{0,2},{1,3},{2,0},{3,1},{4,6},{5,7},{6,4},{7,5},{8,10},{9,11},{10,... | collective-permute-start | bytes 589832 | tf_op jit(solution)/shard_map/ppermute | solution.py:209
  13.7 0.0 collective-permute-done.piece_ref
  13.7 0.4 project.4.refs_0_
  14.1 1.3 %collective-permute-start.2 = (bf16[128,768]{1,0:T(8,128)(2,1)S(1)}, bf16[128,768]{1,0:T(8,128)(2,1)S(1)}, u32[]{:S(2)}, u32[]{:S(2)}) collective-permute-start(bf16[128,768]{1,0:T(8,128)(2,1)S(1)} %project.4.refs_0_), channel_id=1, source_target_pairs={{0,2},{1,3},{2,0},{3,1},{4,6},{5,7},{6,4},{7,5},{8,10},{9,11},{10,... | collective-permute-start | bytes 589832 | tf_op jit(solution)/shard_map/ppermute | solution.py:209
  15.4 3.0 %collective-permute-done.5.piece_ref = bf16[128,768]{1,0:T(8,128)(2,1)S(1)} collective-permute-done((bf16[128,768]{1,0:T(8,128)(2,1)}, bf16[128,768]{1,0:T(8,128)(2,1)S(1)}, u32[]{:S(2)}, u32[]{:S(2)}) %collective-permute-start.5) | collective-permute-done | bytes 196640 | tf_op jit(solution)/shard_map/ppermute | solution.py:206
  18.4 0.4 project.6.refs_1_
  18.9 1.5 %collective-permute-start.6 = (bf16[128,768]{1,0:T(8,128)(2,1)S(1)}, bf16[128,768]{1,0:T(8,128)(2,1)S(1)}, u32[]{:S(2)}, u32[]{:S(2)}) collective-permute-start(bf16[128,768]{1,0:T(8,128)(2,1)S(1)} %project.6.refs_1_), channel_id=1, source_target_pairs={{0,2},{1,3},{2,0},{3,1},{4,6},{5,7},{6,4},{7,5},{8,10},{9,11},{10,... | collective-permute-start | bytes 589832 | tf_op jit(solution)/shard_map/ppermute | solution.py:209
  20.4 0.0 collective-permute-done.4.other_hbm
  20.4 4.6 %sort_slabs.1 = (bf16[768,1024]{1,0:T(8,128)(2,1)S(1)}, bf16[768,1024]{1,0:T(8,128)(2,1)S(1)}) custom-call(s32[1,256]{1,0:T(1,128)S(1)} %copy-done.5, s32[1,1024]{1,0:T(1,128)S(1)} %bitcast.4, bf16[768,1024]{1,0:T(8,128)(2,1)S(1)} %copy-done.2, s32[1,1024]{1,0:T(1,128)S(1)} %bitcast.3, bf16[768,1024]{1,0:T(8,128)(2,1)} %collective-permute-done.4.other_hbm), custom_call_target="tpu_custom_call" | custom-call | tf_op jit(solution)/shard_map/sort_slabs/pallas_call | solution.py:122
  25.0 0.0 collective-permute-done.8.piece_ref
  25.0 0.4 project.7.refs_1_
  25.4 1.4 %collective-permute-start.9 = (bf16[128,768]{1,0:T(8,128)(2,1)S(1)}, bf16[128,768]{1,0:T(8,128)(2,1)S(1)}, u32[]{:S(2)}, u32[]{:S(2)}) collective-permute-start(bf16[128,768]{1,0:T(8,128)(2,1)S(1)} %project.7.refs_1_), channel_id=1, source_target_pairs={{0,2},{1,3},{2,0},{3,1},{4,6},{5,7},{6,4},{7,5},{8,10},{9,11},{10,... | collective-permute-start | bytes 589832 | tf_op jit(solution)/shard_map/ppermute | solution.py:209
  26.9 0.0 collective-permute-done.3.refs_3_
  26.9 0.0 collective-permute-done.2.refs_2_
  26.9 1.8 %score.3 = (f32[128,128]{1,0:T(8,128)S(1)}, f32[128,128]{1,0:T(8,128)S(1)}, f32[128,128]{1,0:T(8,128)S(1)}, f32[128,128]{1,0:T(8,128)S(1)}) custom-call(bf16[128,768]{1,0:T(8,128)(2,1)S(1)} %project.4.refs_0_, bf16[128,768]{1,0:T(8,128)(2,1)S(1)} %project.5.refs_1_, bf16[128,768]{1,0:T(8,128)(2,1)S(1)} %collective-permute-done.2.refs_2_, ...), custom_call_target="tpu_custom_call" | custom-call | tf_op jit(solution)/shard_map/score/pallas_call | solution.py:151
  28.7 2.6 %collective-permute-start.14 = (f32[128,128]{1,0:T(8,128)S(1)}, f32[128,128]{1,0:T(8,128)S(1)}, u32[]{:S(2)}, u32[]{:S(2)}) collective-permute-start(f32[128,128]{1,0:T(8,128)S(1)} %get-tuple-element.33), channel_id=1, source_target_pairs={{0,12},{4,8},{8,4},{12,0},{1,13},{5,9},{9,5},{13,1},{2,14},{6,10},... | collective-permute-start | bytes 196616 | tf_op jit(solution)/shard_map/ppermute | solution.py:206
  31.3 1.4 %collective-permute-start.15 = (f32[128,128]{1,0:T(8,128)S(1)}, f32[128,128]{1,0:T(8,128)S(1)}, u32[]{:S(2)}, u32[]{:S(2)}) collective-permute-start(f32[128,128]{1,0:T(8,128)S(1)} %get-tuple-element.34), channel_id=1, source_target_pairs={{0,14},{1,15},{2,12},{3,13},{4,10},{5,11},{6,8},{7,9},{8,6},{9,7},... | collective-permute-start | bytes 196616 | tf_op jit(solution)/shard_map/ppermute | solution.py:217
  32.7 1.4 %collective-permute-start.11 = (f32[128,128]{1,0:T(8,128)S(1)}, f32[128,128]{1,0:T(8,128)S(1)}, u32[]{:S(2)}, u32[]{:S(2)}) collective-permute-start(f32[128,128]{1,0:T(8,128)S(1)} %get-tuple-element.26.refs_0_), channel_id=1, source_target_pairs={{0,2},{1,3},{2,0},{3,1},{4,6},{5,7},{6,4},{7,5},{8,10},{9,11},{10,... | collective-permute-start | bytes 196616 | tf_op jit(solution)/shard_map/ppermute | solution.py:209
  34.0 0.0 collective-permute-done.6.refs_2_
  34.1 1.0 %score.4 = (f32[128,128]{1,0:T(8,128)S(1)}, f32[128,128]{1,0:T(8,128)S(1)}) custom-call(f32[128,128]{1,0:T(8,128)S(1)} %get-tuple-element.26.refs_0_, bf16[128,768]{1,0:T(8,128)(2,1)S(1)} %project.6.refs_1_, bf16[128,768]{1,0:T(8,128)(2,1)S(1)} %collective-permute-done.6.refs_2_, bf16[768,1024]{1,0:T(8,128)(2,1)S(1)} %get-tuple-element.23.refs_4_.refs_3_.refs_0_, ...), custom_call_target="tpu_custom_call" | custom-call | tf_op jit(solution)/shard_map/score/pallas_call | solution.py:151
  35.1 0.1 collective-permute-start.12
  35.1 0.0 collective-permute-done.9.refs_2_
  35.2 2.1 %collective-permute-start.7 = (f32[128,128]{1,0:T(8,128)S(1)}, f32[128,128]{1,0:T(8,128)S(1)}, u32[]{:S(2)}, u32[]{:S(2)}) collective-permute-start(f32[128,128]{1,0:T(8,128)S(1)} %get-tuple-element.28), channel_id=1, source_target_pairs={{0,4},{4,0},{8,12},{12,8},{1,5},{5,1},{9,13},{13,9},{2,6},{6,2},{1... | collective-permute-start | bytes 196616 | tf_op jit(solution)/shard_map/ppermute | solution.py:206
  37.2 1.0 %score.5 = (f32[128,128]{1,0:T(8,128)S(1)}, f32[128,128]{1,0:T(8,128)S(1)}) custom-call(f32[128,128]{1,0:T(8,128)S(1)} %get-tuple-element.29.refs_0_, bf16[128,768]{1,0:T(8,128)(2,1)S(1)} %project.7.refs_1_, bf16[128,768]{1,0:T(8,128)(2,1)S(1)} %collective-permute-done.9.refs_2_, bf16[768,1024]{1,0:T(8,128)(2,1)S(1)} %get-tuple-element.23.refs_4_.refs_3_.refs_0_, ...), custom_call_target="tpu_custom_call" | custom-call | tf_op jit(solution)/shard_map/score/pallas_call | solution.py:151
  38.3 0.0 collective-permute-done.14.refs_0_
  38.3 1.1 %collective-permute-start.10 = (f32[128,128]{1,0:T(8,128)S(1)}, f32[128,128]{1,0:T(8,128)S(1)}, u32[]{:S(2)}, u32[]{:S(2)}) collective-permute-start(f32[128,128]{1,0:T(8,128)S(1)} %get-tuple-element.31), channel_id=1, source_target_pairs={{0,8},{4,12},{8,0},{12,4},{1,9},{5,13},{9,1},{13,5},{2,10},{6,14},... | collective-permute-start | bytes 196616 | tf_op jit(solution)/shard_map/ppermute | solution.py:206
  39.4 0.0 collective-permute-done.15.refs_1_
  39.4 2.7 %collective-permute-start.13 = (f32[128,128]{1,0:T(8,128)S(1)}, f32[128,128]{1,0:T(8,128)S(1)}, u32[]{:S(2)}, u32[]{:S(2)}) collective-permute-start(f32[128,128]{1,0:T(8,128)S(1)} %get-tuple-element.32), channel_id=1, source_target_pairs={{0,10},{1,11},{2,8},{3,9},{4,14},{5,15},{6,12},{7,13},{8,2},{9,3},... | collective-permute-start | bytes 196616 | tf_op jit(solution)/shard_map/ppermute | solution.py:217
  42.1 0.2 select.2.refs_6_
  42.3 0.0 collective-permute-done.12.refs_4_
  42.3 0.0 collective-permute-done.7.refs_1_
  42.3 0.0 collective-permute-done.11.refs_3_
  42.4 2.2 %collective-permute-done.10.refs_2_ = f32[128,128]{1,0:T(8,128)S(1)} collective-permute-done((f32[128,128]{1,0:T(8,128)S(1)}, f32[128,128]{1,0:T(8,128)S(1)}, u32[]{:S(2)}, u32[]{:S(2)}) %collective-permute-start.10) | collective-permute-done | bytes 65568 | tf_op jit(solution)/shard_map/ppermute | solution.py:206
  44.6 1.2 %collective-permute-done.13.refs_5_ = f32[128,128]{1,0:T(8,128)S(1)} collective-permute-done((f32[128,128]{1,0:T(8,128)S(1)}, f32[128,128]{1,0:T(8,128)S(1)}, u32[]{:S(2)}, u32[]{:S(2)}) %collective-permute-start.13) | collective-permute-done | bytes 65568 | tf_op jit(solution)/shard_map/ppermute | solution.py:217
  45.7 1.0 %select.3 = f32[256,128]{1,0:T(8,128)} custom-call(s32[1,256]{1,0:T(1,128)S(1)} %copy-done.5, f32[128,128]{1,0:T(8,128)S(1)} %get-tuple-element.25.refs_0_, f32[128,128]{1,0:T(8,128)S(1)} %collective-permute-done.7.refs_1_, f32[128,128]{1,0:T(8,128)S(1)} %collective-permute-done.10.refs_2_, f32[128,128]{1,0:T(8,128)S(1)} %collective-permute-done.11.refs_3_, ...), custom_call_target="tpu_custom_call" | custom-call | tf_op jit(solution)/shard_map/select/pallas_call | solution.py:190
  (7 shorter events, 0.0 us)
Async XLA Ops:
  0.0 20.4 %collective-permute-start.4 = (bf16[768,1024]{1,0:T(8,128)(2,1)}, bf16[768,1024]{1,0:T(8,128)(2,1)}, u32[]{:S(2)}, u32[]{:S(2)}) collective-permute-start(bf16[768,1024]{1,0:T(8,128)(2,1)} %slab_ref.1), channel_id=1, source_target_pairs={{0,1},{1,0},{2,3},{3,2},{4,5},{5,4},{6,7},{7,6},{8,9},{9,8},{10,11... | collective-permute-start | bytes 4718600 | tf_op jit(solution)/shard_map/ppermute | solution.py:209
  2.6 11.1 %collective-permute-start = (bf16[128,768]{1,0:T(8,128)(2,1)}, bf16[128,768]{1,0:T(8,128)(2,1)S(1)}, u32[]{:S(2)}, u32[]{:S(2)}) collective-permute-start(bf16[128,768]{1,0:T(8,128)(2,1)} %get-tuple-element.21), channel_id=1, source_target_pairs={{0,12},{4,8},{8,4},{12,0},{1,13},{5,9},{9,5},{13,1},{2,14},{6,10},... | collective-permute-start | bytes 589832 | tf_op jit(solution)/shard_map/ppermute | solution.py:206
  7.3 11.1 %collective-permute-start.5 = (bf16[128,768]{1,0:T(8,128)(2,1)}, bf16[128,768]{1,0:T(8,128)(2,1)S(1)}, u32[]{:S(2)}, u32[]{:S(2)}) collective-permute-start(bf16[128,768]{1,0:T(8,128)(2,1)} %get-tuple-element.27), channel_id=1, source_target_pairs={{0,4},{4,0},{8,12},{12,8},{1,5},{5,1},{9,13},{13,9},{2,6},{6,2},{1... | collective-permute-start | bytes 589832 | tf_op jit(solution)/shard_map/ppermute | solution.py:206
  7.3 17.7 %collective-permute-start.8 = (bf16[128,768]{1,0:T(8,128)(2,1)}, bf16[128,768]{1,0:T(8,128)(2,1)S(1)}, u32[]{:S(2)}, u32[]{:S(2)}) collective-permute-start(bf16[128,768]{1,0:T(8,128)(2,1)} %get-tuple-element.30), channel_id=1, source_target_pairs={{0,8},{4,12},{8,0},{12,4},{1,9},{5,13},{9,1},{13,5},{2,10},{6,14},... | collective-permute-start | bytes 589832 | tf_op jit(solution)/shard_map/ppermute | solution.py:206
  8.0 1.4 %collective-permute-start.1 = (s32[1024]{0:T(1024)}, s32[1024]{0:T(1024)S(1)}, u32[]{:S(2)}, u32[]{:S(2)}) collective-permute-start(s32[1024]{0:T(1024)} %param.8), channel_id=1, source_target_pairs={{0,1},{1,0},{2,3},{3,2},{4,5},{5,4},{6,7},{7,6},{8,9},{9,8},{10,11... | collective-permute-start | bytes 12296 | tf_op jit(solution)/shard_map/ppermute | solution.py:209
  9.3 1.3 %copy-start = (bf16[768,768]{1,0:T(8,128)(2,1)S(1)}, bf16[768,768]{1,0:T(8,128)(2,1)}, u32[]{:S(2)}) copy-start(bf16[768,768]{1,0:T(8,128)(2,1)} %projection_ref.7) | copy-start | bytes 3538948
  10.6 0.9 %copy-start.3 = (bf16[128,768]{1,0:T(8,128)(2,1)S(1)}, bf16[128,768]{1,0:T(8,128)(2,1)}, u32[]{:S(2)}) copy-start(bf16[128,768]{1,0:T(8,128)(2,1)} %get-tuple-element.22.piece_ref) | copy-start | bytes 589828
  11.5 6.9 %copy-start.1 = (bf16[768,768]{1,0:T(8,128)(2,1)S(1)}, bf16[768,768]{1,0:T(8,128)(2,1)}, u32[]{:S(2)}) copy-start(bf16[768,768]{1,0:T(8,128)(2,1)} %projection_ref.7) | copy-start | bytes 3538948
  12.0 8.4 %copy-start.2 = (bf16[768,1024]{1,0:T(8,128)(2,1)S(1)}, bf16[768,1024]{1,0:T(8,128)(2,1)}, u32[]{:S(2)}) copy-start(bf16[768,1024]{1,0:T(8,128)(2,1)} %slab_ref.1) | copy-start | bytes 4718596
  12.0 8.4 %copy-start.4 = (s32[1024]{0:T(1024)S(1)}, s32[1024]{0:T(1024)}, u32[]{:S(2)}) copy-start(s32[1024]{0:T(1024)} %param.8) | copy-start | bytes 12292
  12.0 8.4 %copy-start.5 = (s32[1,256]{1,0:T(1,128)S(1)}, s32[1,256]{1,0:T(1,128)}, u32[]{:S(2)}) copy-start(s32[1,256]{1,0:T(1,128)} %get-tuple-element.20.after_ref.position_ref) | copy-start | bytes 3076
  12.0 14.9 %collective-permute-start.3 = (bf16[128,768]{1,0:T(8,128)(2,1)S(1)}, bf16[128,768]{1,0:T(8,128)(2,1)S(1)}, u32[]{:S(2)}, u32[]{:S(2)}) collective-permute-start(bf16[128,768]{1,0:T(8,128)(2,1)S(1)} %project.5.refs_1_), channel_id=1, source_target_pairs={{0,2},{1,3},{2,0},{3,1},{4,6},{5,7},{6,4},{7,5},{8,10},{9,11},{10,... | collective-permute-start | bytes 589832 | tf_op jit(solution)/shard_map/ppermute | solution.py:209
  14.1 12.7 %collective-permute-start.2 = (bf16[128,768]{1,0:T(8,128)(2,1)S(1)}, bf16[128,768]{1,0:T(8,128)(2,1)S(1)}, u32[]{:S(2)}, u32[]{:S(2)}) collective-permute-start(bf16[128,768]{1,0:T(8,128)(2,1)S(1)} %project.4.refs_0_), channel_id=1, source_target_pairs={{0,2},{1,3},{2,0},{3,1},{4,6},{5,7},{6,4},{7,5},{8,10},{9,11},{10,... | collective-permute-start | bytes 589832 | tf_op jit(solution)/shard_map/ppermute | solution.py:209
  18.9 15.2 %collective-permute-start.6 = (bf16[128,768]{1,0:T(8,128)(2,1)S(1)}, bf16[128,768]{1,0:T(8,128)(2,1)S(1)}, u32[]{:S(2)}, u32[]{:S(2)}) collective-permute-start(bf16[128,768]{1,0:T(8,128)(2,1)S(1)} %project.6.refs_1_), channel_id=1, source_target_pairs={{0,2},{1,3},{2,0},{3,1},{4,6},{5,7},{6,4},{7,5},{8,10},{9,11},{10,... | collective-permute-start | bytes 589832 | tf_op jit(solution)/shard_map/ppermute | solution.py:209
  25.4 9.7 %collective-permute-start.9 = (bf16[128,768]{1,0:T(8,128)(2,1)S(1)}, bf16[128,768]{1,0:T(8,128)(2,1)S(1)}, u32[]{:S(2)}, u32[]{:S(2)}) collective-permute-start(bf16[128,768]{1,0:T(8,128)(2,1)S(1)} %project.7.refs_1_), channel_id=1, source_target_pairs={{0,2},{1,3},{2,0},{3,1},{4,6},{5,7},{6,4},{7,5},{8,10},{9,11},{10,... | collective-permute-start | bytes 589832 | tf_op jit(solution)/shard_map/ppermute | solution.py:209
  28.7 9.6 %collective-permute-start.14 = (f32[128,128]{1,0:T(8,128)S(1)}, f32[128,128]{1,0:T(8,128)S(1)}, u32[]{:S(2)}, u32[]{:S(2)}) collective-permute-start(f32[128,128]{1,0:T(8,128)S(1)} %get-tuple-element.33), channel_id=1, source_target_pairs={{0,12},{4,8},{8,4},{12,0},{1,13},{5,9},{9,5},{13,1},{2,14},{6,10},... | collective-permute-start | bytes 196616 | tf_op jit(solution)/shard_map/ppermute | solution.py:206
  31.3 8.1 %collective-permute-start.15 = (f32[128,128]{1,0:T(8,128)S(1)}, f32[128,128]{1,0:T(8,128)S(1)}, u32[]{:S(2)}, u32[]{:S(2)}) collective-permute-start(f32[128,128]{1,0:T(8,128)S(1)} %get-tuple-element.34), channel_id=1, source_target_pairs={{0,14},{1,15},{2,12},{3,13},{4,10},{5,11},{6,8},{7,9},{8,6},{9,7},... | collective-permute-start | bytes 196616 | tf_op jit(solution)/shard_map/ppermute | solution.py:217
  32.7 9.7 %collective-permute-start.11 = (f32[128,128]{1,0:T(8,128)S(1)}, f32[128,128]{1,0:T(8,128)S(1)}, u32[]{:S(2)}, u32[]{:S(2)}) collective-permute-start(f32[128,128]{1,0:T(8,128)S(1)} %get-tuple-element.26.refs_0_), channel_id=1, source_target_pairs={{0,2},{1,3},{2,0},{3,1},{4,6},{5,7},{6,4},{7,5},{8,10},{9,11},{10,... | collective-permute-start | bytes 196616 | tf_op jit(solution)/shard_map/ppermute | solution.py:209
  35.1 7.3 %collective-permute-start.12 = (f32[128,128]{1,0:T(8,128)S(1)}, f32[128,128]{1,0:T(8,128)S(1)}, u32[]{:S(2)}, u32[]{:S(2)}) collective-permute-start(f32[128,128]{1,0:T(8,128)S(1)} %get-tuple-element.29.refs_0_), channel_id=1, source_target_pairs={{0,6},{1,7},{2,4},{3,5},{4,2},{5,3},{6,0},{7,1},{8,14},{9,15},{10,... | collective-permute-start | bytes 196616 | tf_op jit(solution)/shard_map/ppermute | solution.py:217
  35.2 7.2 %collective-permute-start.7 = (f32[128,128]{1,0:T(8,128)S(1)}, f32[128,128]{1,0:T(8,128)S(1)}, u32[]{:S(2)}, u32[]{:S(2)}) collective-permute-start(f32[128,128]{1,0:T(8,128)S(1)} %get-tuple-element.28), channel_id=1, source_target_pairs={{0,4},{4,0},{8,12},{12,8},{1,5},{5,1},{9,13},{13,9},{2,6},{6,2},{1... | collective-permute-start | bytes 196616 | tf_op jit(solution)/shard_map/ppermute | solution.py:206
  38.3 6.3 %collective-permute-start.10 = (f32[128,128]{1,0:T(8,128)S(1)}, f32[128,128]{1,0:T(8,128)S(1)}, u32[]{:S(2)}, u32[]{:S(2)}) collective-permute-start(f32[128,128]{1,0:T(8,128)S(1)} %get-tuple-element.31), channel_id=1, source_target_pairs={{0,8},{4,12},{8,0},{12,4},{1,9},{5,13},{9,1},{13,5},{2,10},{6,14},... | collective-permute-start | bytes 196616 | tf_op jit(solution)/shard_map/ppermute | solution.py:206
  39.4 6.3 %collective-permute-start.13 = (f32[128,128]{1,0:T(8,128)S(1)}, f32[128,128]{1,0:T(8,128)S(1)}, u32[]{:S(2)}, u32[]{:S(2)}) collective-permute-start(f32[128,128]{1,0:T(8,128)S(1)} %get-tuple-element.32), channel_id=1, source_target_pairs={{0,10},{1,11},{2,8},{3,9},{4,14},{5,15},{6,12},{7,13},{8,2},{9,3},... | collective-permute-start | bytes 196616 | tf_op jit(solution)/shard_map/ppermute | solution.py:217

commit v5 on v4

--- a/solution.py
+++ b/solution.py
@@ -108,26 +108,38 @@
     )(piece, projection, *after)
 
 
-def sort_kernel(after_ref, bins_ref, slab_ref, other_bins_ref, other_hbm, sorted_ref, other_sorted_ref, other_ref, sem):
+def sort_kernel(after_ref, bins_ref, slab_ref, sorted_ref):
+    sorted_ref[...] = sorted_columns(bins_ref[...], slab_ref[...])
+
+
+def sort_slab(after, bins, slab):
+    return pl.pallas_call(
+        sort_kernel,
+        out_shape=jax.ShapeDtypeStruct(slab.shape, jnp.bfloat16),
+        in_specs=[pl.BlockSpec(memory_space=pl.ANY)] + [pl.BlockSpec(memory_space=pltpu.VMEM)] * 2,
+        compiler_params=params(),
+        cost_estimate=us(0),
+        name="sort_slab",
+    )(after, bins.reshape(1, slab.shape[1]), slab)
+
+
+def sort_and_fetch_kernel(bins_ref, slab_ref, other_hbm, sorted_ref, other_ref, sem):
     copy = pltpu.make_async_copy(other_hbm, other_ref, sem)
     copy.start()
     sorted_ref[...] = sorted_columns(bins_ref[...], slab_ref[...])
     copy.wait()
-    other_sorted_ref[...] = sorted_columns(other_bins_ref[...], other_ref[...])
-
-
-def sort_slabs(after, bins, slab, other_bins, other_slab):
-    width = slab.shape[1]
-    vmem, hbm = pl.BlockSpec(memory_space=pltpu.VMEM), pl.BlockSpec(memory_space=pltpu.HBM)
-    return pl.pallas_call(
-        sort_kernel,
+
+
+def sort_and_fetch(bins, slab, other):
+    return pl.pallas_call(
+        sort_and_fetch_kernel,
         out_shape=[jax.ShapeDtypeStruct(slab.shape, jnp.bfloat16)] * 2,
-        in_specs=[pl.BlockSpec(memory_space=pl.ANY), vmem, vmem, vmem, hbm],
-        scratch_shapes=[pltpu.VMEM(slab.shape, slab.dtype), pltpu.SemaphoreType.DMA],
-        compiler_params=params(),
-        cost_estimate=us(0),
-        name="sort_slabs",
-    )(after, bins.reshape(1, width), slab, other_bins.reshape(1, width), other_slab)
+        in_specs=[pl.BlockSpec(memory_space=pltpu.VMEM)] * 2 + [pl.BlockSpec(memory_space=pltpu.HBM)],
+        scratch_shapes=[pltpu.SemaphoreType.DMA],
+        compiler_params=params(),
+        cost_estimate=us(0),
+        name="sort_and_fetch",
+    )(bins.reshape(1, slab.shape[1]), slab, other)
 
 
 def score_kernel(afters, pieces, *refs):
@@ -218,25 +230,30 @@
 
     position, *pieces = prepare(queries, routes, groups, capacity)
     other_slab, other_bins = along_blk(vectors, 1), along_blk(bins, 1)
-    slabs_here = sort_slabs(position, bins, vectors, other_bins, other_slab)
     arrived = {k: along_db(pieces[k], k) for k in (3, 1, 2)}
-    here, partner = {}, {}
-    for k, piece, after in (
-        (0, pieces[0], [other_bins]),
-        (1, arrived[1], []),
-        (3, arrived[3], []),
-        (2, arrived[2], [slabs_here[0]]),
-    ):
+    here, partner, answers = {}, {}, {}
+
+    def cross(k, piece, *after):
         here[k] = project(piece, projection, *after)
         partner[k] = along_blk(here[k], 2)
-    answers, after = {}, []
-    for wave in ((3, 0), (1,), (2,)):
-        found = score(after, [here[k] for k in wave] + [partner[k] for k in wave], slabs_here)
-        for k, mine, theirs in zip(wave, found[: len(wave)], found[len(wave) :]):
-            answers[k] = (along_db(mine, k), along_both(theirs, k, 2)) if k else (mine, along_blk(theirs, 2))
-        after = found[-1:]
-    some = select(position, (3,), answers, [], 3)
-    return select(position, (0, 1, 2), answers, [some], 0)
+
+    def scores(k, *after):
+        mine, theirs = score(after, [here[k], partner[k]], slabs_here)
+        answers[k] = (along_db(mine, k), along_both(theirs, k, 2)) if k else (mine, along_blk(theirs, 2))
+        return theirs
+
+    own_slab, fetched = sort_and_fetch(bins, vectors, other_slab)
+    slabs_here = [own_slab, sort_slab(position, other_bins, fetched)]
+    cross(0, pieces[0], other_bins)
+    cross(1, arrived[1], own_slab)
+    cross(3, arrived[3])
+    done = scores(0)
+    cross(2, arrived[2], done)
+    done = scores(3, done)
+    done = scores(1, done)
+    scores(2, done)
+    far = select(position, (3,), answers, [], 3)
+    return select(position, (0, 1, 2), answers, [far], 0)
 
 
 def binned_max(query_rows, columns):

time: 46.9 us -> 46.1 us (0.983)
    ppermute x6, waiting for transfers between devices: 5.19 us -> 2.83 us  [along_db(): return lax.ppermute(value, 'db', [(i, i ^ distance) for i in range(groups)])]
    ppermute x3, waiting for transfers between devices: 1.16 us -> 3.34 us  [along_both(): return lax.ppermute(value, ('db', 'blk'), pairs)]
    ppermute x7, starting transfers between devices: 7.84 us -> 8.45 us  [along_blk(): return lax.ppermute(value, 'blk', [(i, i ^ distance) for i in range(slabs)])]
    ppermute x3, starting transfers between devices: 4.15 us -> 3.64 us  [along_both(): return lax.ppermute(value, ('db', 'blk'), pairs)]
    pallas_call x1 -> x2, Pallas kernels: 4.55 us -> 4.08 us  [the longest x1 2.05 us: sort_and_fetch(): pl.pallas_call(sort_and_fetch_kernel, out_shape=[jax.ShapeDtypeStruct(sla...]
    pallas_call x3 -> x4, Pallas kernels: 3.83 us -> 4 us  [score(): pl.pallas_call(functools.partial(score_kernel, len(after), len(pieces)),...]
  transfers between devices with their start and end apart: 16 -> 16, of which waited for: 4 -> 5; matrix products, arithmetic and copies ran while one was open for 0% -> 0% of each run, Pallas kernels for 27% -> 27%
where the time goes in v5:
time: 46.1 us; the launch traced here: 45.9 us
  starting transfers between devices  23 us (50%)
  Pallas kernels  13.2 us (29%)
  waiting for transfers between devices  7.33 us (16%)
  local copies, waits for them, and re-layouts  2.21 us (5%)
    ppermute x6, starting transfers between devices, along_db(): return lax.ppermute(value, 'db', [(i, i ^ distance) for i in range(groups)])  10.9 us
    ppermute x7, starting transfers between devices, along_blk(): return lax.ppermute(value, 'blk', [(i, i ^ distance) for i in range(slabs)])  8.45 us
    pallas_call x4, Pallas kernels, score(): pl.pallas_call(functools.partial(score_kernel, len(after), len(pieces)),...  4 us
    ppermute x3, starting transfers between devices, along_both(): return lax.ppermute(value, ('db', 'blk'), pairs)  3.64 us
    ppermute x3, waiting for transfers between devices, along_both(): return lax.ppermute(value, ('db', 'blk'), pairs)  3.34 us
    ppermute x6, waiting for transfers between devices, along_db(): return lax.ppermute(value, 'db', [(i, i ^ distance) for i in range(groups)])  2.83 us
    unnamed x12, local copies, waits for them, and re-layouts  2.21 us
    pallas_call x1, Pallas kernels, prepare(): pl.pallas_call(functools.partial(prepare_kernel, groups, capacity), out_s...  2.18 us
  transfers between devices with their start and end apart: 16, of which 5 were waited for; matrix products, arithmetic and copies ran while one was open for 0% of the time, Pallas kernels for 27%

profile of v5, /device:TPU:0, one launch (start us, length us, event | category | flops | bytes accessed | tf_op | source)
XLA Modules:
  0.0 45.9 jit_solution(782152831141187386)
XLA Ops:
  0.0 0.5 collective-permute-start.2
  0.5 2.2 %prepare.1 = (s32[1,256]{1,0:T(1,128)}, bf16[128,768]{1,0:T(8,128)(2,1)}, bf16[128,768]{1,0:T(8,128)(2,1)}, bf16[128,768]{1,0:T(8,128)(2,1)}, bf16[128,768]{1,0:T(8,128)(2,1)}) custom-call(s32[1,256]{1,0:T(1,128)} %bitcast.5, bf16[256,768]{1,0:T(8,128)(2,1)} %queries_hbm.1), custom_call_target="tpu_custom_call" | custom-call | tf_op jit(solution)/shard_map/prepare/pallas_call | solution.py:84
  2.6 4.7 %collective-permute-start.3 = (bf16[128,768]{1,0:T(8,128)(2,1)}, bf16[128,768]{1,0:T(8,128)(2,1)S(1)}, u32[]{:S(2)}, u32[]{:S(2)}) collective-permute-start(bf16[128,768]{1,0:T(8,128)(2,1)} %get-tuple-element.26), channel_id=1, source_target_pairs={{0,12},{4,8},{8,4},{12,0},{1,13},{5,9},{9,5},{13,1},{2,14},{6,10},... | collective-permute-start | bytes 589832 | tf_op jit(solution)/shard_map/ppermute | solution.py:218
  7.3 0.2 collective-permute-start
  7.5 0.0 collective-permute-start.5
  7.5 1.1 %collective-permute-done.refs_0_ = s32[1024]{0:T(1024)S(1)} collective-permute-done((s32[1024]{0:T(1024)}, s32[1024]{0:T(1024)S(1)}, u32[]{:S(2)}, u32[]{:S(2)}) %collective-permute-start) | collective-permute-done | bytes 4128 | tf_op jit(solution)/shard_map/ppermute | solution.py:221
  8.7 1.3 %copy-done = bf16[768,768]{1,0:T(8,128)(2,1)S(1)} copy-done((bf16[768,768]{1,0:T(8,128)(2,1)S(1)}, bf16[768,768]{1,0:T(8,128)(2,1)}, u32[]{:S(2)}) %copy-start) | copy-done | bytes 1179672
  10.0 0.9 %copy-done.3 = bf16[128,768]{1,0:T(8,128)(2,1)S(1)} copy-done((bf16[128,768]{1,0:T(8,128)(2,1)S(1)}, bf16[128,768]{1,0:T(8,128)(2,1)}, u32[]{:S(2)}) %copy-start.3) | copy-done | bytes 196632
  10.9 0.4 project.4.refs_0_
  11.3 1.6 %collective-permute-start.1 = (bf16[128,768]{1,0:T(8,128)(2,1)S(1)}, bf16[128,768]{1,0:T(8,128)(2,1)S(1)}, u32[]{:S(2)}, u32[]{:S(2)}) collective-permute-start(bf16[128,768]{1,0:T(8,128)(2,1)S(1)} %project.4.refs_0_), channel_id=1, source_target_pairs={{0,2},{1,3},{2,0},{3,1},{4,6},{5,7},{6,4},{7,5},{8,10},{9,11},{10,... | collective-permute-start | bytes 589832 | tf_op jit(solution)/shard_map/ppermute | solution.py:221
  12.9 0.0 collective-permute-start.8
  12.9 0.4 collective-permute-done.3.piece_ref
  13.3 0.0 copy-done.1
  13.3 0.4 project.5.refs_1_
  13.7 1.7 %collective-permute-start.4 = (bf16[128,768]{1,0:T(8,128)(2,1)S(1)}, bf16[128,768]{1,0:T(8,128)(2,1)S(1)}, u32[]{:S(2)}, u32[]{:S(2)}) collective-permute-start(bf16[128,768]{1,0:T(8,128)(2,1)S(1)} %project.5.refs_1_), channel_id=1, source_target_pairs={{0,2},{1,3},{2,0},{3,1},{4,6},{5,7},{6,4},{7,5},{8,10},{9,11},{10,... | collective-permute-start | bytes 589832 | tf_op jit(solution)/shard_map/ppermute | solution.py:221
  15.4 0.0 collective-permute-done.2.other_hbm
  15.4 2.1 %sort_and_fetch.1 = (bf16[768,1024]{1,0:T(8,128)(2,1)S(1)}, bf16[768,1024]{1,0:T(8,128)(2,1)S(1)}) custom-call(s32[1,1024]{1,0:T(1,128)S(1)} %bitcast.4, bf16[768,1024]{1,0:T(8,128)(2,1)S(1)} %copy-done.2, bf16[768,1024]{1,0:T(8,128)(2,1)} %collective-permute-done.2.other_hbm), custom_call_target="tpu_custom_call" | custom-call | tf_op jit(solution)/shard_map/sort_and_fetch/pallas_call | solution.py:134
  17.5 0.8 %collective-permute-done.5.piece_ref = bf16[128,768]{1,0:T(8,128)(2,1)S(1)} collective-permute-done((bf16[128,768]{1,0:T(8,128)(2,1)}, bf16[128,768]{1,0:T(8,128)(2,1)S(1)}, u32[]{:S(2)}, u32[]{:S(2)}) %collective-permute-start.5) | collective-permute-done | bytes 196640 | tf_op jit(solution)/shard_map/ppermute | solution.py:218
  18.3 0.4 project.6.refs_1_
  18.8 1.6 %collective-permute-start.6 = (bf16[128,768]{1,0:T(8,128)(2,1)S(1)}, bf16[128,768]{1,0:T(8,128)(2,1)S(1)}, u32[]{:S(2)}, u32[]{:S(2)}) collective-permute-start(bf16[128,768]{1,0:T(8,128)(2,1)S(1)} %project.6.refs_1_), channel_id=1, source_target_pairs={{0,2},{1,3},{2,0},{3,1},{4,6},{5,7},{6,4},{7,5},{8,10},{9,11},{10,... | collective-permute-start | bytes 589832 | tf_op jit(solution)/shard_map/ppermute | solution.py:221
  20.4 2.0 %sort_slab.1.refs_3_.refs_4_ = bf16[768,1024]{1,0:T(8,128)(2,1)S(1)} custom-call(s32[1,256]{1,0:T(1,128)S(1)} %copy-done.5, s32[1,1024]{1,0:T(1,128)S(1)} %bitcast.3, bf16[768,1024]{1,0:T(8,128)(2,1)S(1)} %get-tuple-element.23.slab_ref), custom_call_target="tpu_custom_call" | custom-call | tf_op jit(solution)/shard_map/sort_slab/pallas_call | solution.py:116
  22.4 0.0 collective-permute-done.1.refs_1_
  22.4 1.0 %score.4 = (f32[128,128]{1,0:T(8,128)S(1)}, f32[128,128]{1,0:T(8,128)S(1)}) custom-call(bf16[128,768]{1,0:T(8,128)(2,1)S(1)} %project.4.refs_0_, bf16[128,768]{1,0:T(8,128)(2,1)S(1)} %collective-permute-done.1.refs_1_, bf16[768,1024]{1,0:T(8,128)(2,1)S(1)} %get-tuple-element.22.refs_2_.refs_3_.refs_0_, bf16[768,1024]{1,0:T(8,128)(2,1)S(1)} %sort_slab.1.refs_3_.refs_4_), custom_call_target="tpu_custom_call" | custom-call | tf_op jit(solution)/shard_map/score/pallas_call | solution.py:163
  23.4 1.5 %collective-permute-done.8.piece_ref = bf16[128,768]{1,0:T(8,128)(2,1)S(1)} collective-permute-done((bf16[128,768]{1,0:T(8,128)(2,1)}, bf16[128,768]{1,0:T(8,128)(2,1)S(1)}, u32[]{:S(2)}, u32[]{:S(2)}) %collective-permute-start.8) | collective-permute-done | bytes 196640 | tf_op jit(solution)/shard_map/ppermute | solution.py:218
  24.9 0.4 project.7.refs_1_
  25.4 1.5 %collective-permute-start.9 = (bf16[128,768]{1,0:T(8,128)(2,1)S(1)}, bf16[128,768]{1,0:T(8,128)(2,1)S(1)}, u32[]{:S(2)}, u32[]{:S(2)}) collective-permute-start(bf16[128,768]{1,0:T(8,128)(2,1)S(1)} %project.7.refs_1_), channel_id=1, source_target_pairs={{0,2},{1,3},{2,0},{3,1},{4,6},{5,7},{6,4},{7,5},{8,10},{9,11},{10,... | collective-permute-start | bytes 589832 | tf_op jit(solution)/shard_map/ppermute | solution.py:221
  26.9 0.0 collective-permute-done.4.refs_2_
  26.9 1.0 %score.5 = (f32[128,128]{1,0:T(8,128)S(1)}, f32[128,128]{1,0:T(8,128)S(1)}) custom-call(f32[128,128]{1,0:T(8,128)S(1)} %get-tuple-element.25.refs_0_, bf16[128,768]{1,0:T(8,128)(2,1)S(1)} %project.5.refs_1_, bf16[128,768]{1,0:T(8,128)(2,1)S(1)} %collective-permute-done.4.refs_2_, bf16[768,1024]{1,0:T(8,128)(2,1)S(1)} %get-tuple-element.22.refs_2_.refs_3_.refs_0_, ...), custom_call_target="tpu_custom_call" | custom-call | tf_op jit(solution)/shard_map/score/pallas_call | solution.py:163
  27.9 2.6 %collective-permute-start.15 = (f32[128,128]{1,0:T(8,128)S(1)}, f32[128,128]{1,0:T(8,128)S(1)}, u32[]{:S(2)}, u32[]{:S(2)}) collective-permute-start(f32[128,128]{1,0:T(8,128)S(1)} %get-tuple-element.27.refs_0_), channel_id=1, source_target_pairs={{0,14},{1,15},{2,12},{3,13},{4,10},{5,11},{6,8},{7,9},{8,6},{9,7},... | collective-permute-start | bytes 196616 | tf_op jit(solution)/shard_map/ppermute | solution.py:229
  30.5 1.4 %collective-permute-start.14 = (f32[128,128]{1,0:T(8,128)S(1)}, f32[128,128]{1,0:T(8,128)S(1)}, u32[]{:S(2)}, u32[]{:S(2)}) collective-permute-start(f32[128,128]{1,0:T(8,128)S(1)} %get-tuple-element.34), channel_id=1, source_target_pairs={{0,12},{4,8},{8,4},{12,0},{1,13},{5,9},{9,5},{13,1},{2,14},{6,10},... | collective-permute-start | bytes 196616 | tf_op jit(solution)/shard_map/ppermute | solution.py:218
  31.8 1.4 %collective-permute-start.11 = (f32[128,128]{1,0:T(8,128)S(1)}, f32[128,128]{1,0:T(8,128)S(1)}, u32[]{:S(2)}, u32[]{:S(2)}) collective-permute-start(f32[128,128]{1,0:T(8,128)S(1)} %get-tuple-element.25.refs_0_), channel_id=1, source_target_pairs={{0,2},{1,3},{2,0},{3,1},{4,6},{5,7},{6,4},{7,5},{8,10},{9,11},{10,... | collective-permute-start | bytes 196616 | tf_op jit(solution)/shard_map/ppermute | solution.py:221
  33.2 0.0 collective-permute-done.6.refs_2_
  33.2 1.0 %score.6 = (f32[128,128]{1,0:T(8,128)S(1)}, f32[128,128]{1,0:T(8,128)S(1)}) custom-call(f32[128,128]{1,0:T(8,128)S(1)} %get-tuple-element.27.refs_0_, bf16[128,768]{1,0:T(8,128)(2,1)S(1)} %project.6.refs_1_, bf16[128,768]{1,0:T(8,128)(2,1)S(1)} %collective-permute-done.6.refs_2_, bf16[768,1024]{1,0:T(8,128)(2,1)S(1)} %get-tuple-element.22.refs_2_.refs_3_.refs_0_, ...), custom_call_target="tpu_custom_call" | custom-call | tf_op jit(solution)/shard_map/score/pallas_call | solution.py:163
  34.2 0.1 collective-permute-start.12
  34.3 0.0 collective-permute-done.9.refs_2_
  34.3 1.0 %score.7 = (f32[128,128]{1,0:T(8,128)S(1)}, f32[128,128]{1,0:T(8,128)S(1)}) custom-call(f32[128,128]{1,0:T(8,128)S(1)} %get-tuple-element.30.refs_0_, bf16[128,768]{1,0:T(8,128)(2,1)S(1)} %project.7.refs_1_, bf16[128,768]{1,0:T(8,128)(2,1)S(1)} %collective-permute-done.9.refs_2_, bf16[768,1024]{1,0:T(8,128)(2,1)S(1)} %get-tuple-element.22.refs_2_.refs_3_.refs_0_, ...), custom_call_target="tpu_custom_call" | custom-call | tf_op jit(solution)/shard_map/score/pallas_call | solution.py:163
  35.3 3.1 %collective-permute-start.10 = (f32[128,128]{1,0:T(8,128)S(1)}, f32[128,128]{1,0:T(8,128)S(1)}, u32[]{:S(2)}, u32[]{:S(2)}) collective-permute-start(f32[128,128]{1,0:T(8,128)S(1)} %get-tuple-element.32), channel_id=1, source_target_pairs={{0,8},{4,12},{8,0},{12,4},{1,9},{5,13},{9,1},{13,5},{2,10},{6,14},... | collective-permute-start | bytes 196616 | tf_op jit(solution)/shard_map/ppermute | solution.py:218
  38.5 0.0 collective-permute-done.15.refs_1_
  38.5 1.0 %collective-permute-start.13 = (f32[128,128]{1,0:T(8,128)S(1)}, f32[128,128]{1,0:T(8,128)S(1)}, u32[]{:S(2)}, u32[]{:S(2)}) collective-permute-start(f32[128,128]{1,0:T(8,128)S(1)} %get-tuple-element.33), channel_id=1, source_target_pairs={{0,10},{1,11},{2,8},{3,9},{4,14},{5,15},{6,12},{7,13},{8,2},{9,3},... | collective-permute-start | bytes 196616 | tf_op jit(solution)/shard_map/ppermute | solution.py:229
  39.5 0.0 collective-permute-done.14.refs_0_
  39.5 1.8 %collective-permute-start.7 = (f32[128,128]{1,0:T(8,128)S(1)}, f32[128,128]{1,0:T(8,128)S(1)}, u32[]{:S(2)}, u32[]{:S(2)}) collective-permute-start(f32[128,128]{1,0:T(8,128)S(1)} %get-tuple-element.29), channel_id=1, source_target_pairs={{0,4},{4,0},{8,12},{12,8},{1,5},{5,1},{9,13},{13,9},{2,6},{6,2},{1... | collective-permute-start | bytes 196616 | tf_op jit(solution)/shard_map/ppermute | solution.py:218
  41.2 0.2 select.2.refs_6_
  41.5 0.0 collective-permute-done.11.refs_3_
  41.5 0.0 collective-permute-done.10.refs_2_
  41.5 3.3 %collective-permute-done.13.refs_5_ = f32[128,128]{1,0:T(8,128)S(1)} collective-permute-done((f32[128,128]{1,0:T(8,128)S(1)}, f32[128,128]{1,0:T(8,128)S(1)}, u32[]{:S(2)}, u32[]{:S(2)}) %collective-permute-start.13) | collective-permute-done | bytes 65568 | tf_op jit(solution)/shard_map/ppermute | solution.py:229
  44.9 0.0 collective-permute-done.12.refs_4_
  44.9 0.0 collective-permute-done.7.refs_1_
  44.9 1.0 %select.3 = f32[256,128]{1,0:T(8,128)} custom-call(s32[1,256]{1,0:T(1,128)S(1)} %copy-done.5, f32[128,128]{1,0:T(8,128)S(1)} %get-tuple-element.24.refs_0_, f32[128,128]{1,0:T(8,128)S(1)} %collective-permute-done.7.refs_1_, f32[128,128]{1,0:T(8,128)S(1)} %collective-permute-done.10.refs_2_, f32[128,128]{1,0:T(8,128)S(1)} %collective-permute-done.11.refs_3_, ...), custom_call_target="tpu_custom_call" | custom-call | tf_op jit(solution)/shard_map/select/pallas_call | solution.py:202
  (9 shorter events, 0.0 us)
Async XLA Ops:
  0.0 15.4 %collective-permute-start.2 = (bf16[768,1024]{1,0:T(8,128)(2,1)}, bf16[768,1024]{1,0:T(8,128)(2,1)}, u32[]{:S(2)}, u32[]{:S(2)}) collective-permute-start(bf16[768,1024]{1,0:T(8,128)(2,1)} %slab_ref.1), channel_id=1, source_target_pairs={{0,1},{1,0},{2,3},{3,2},{4,5},{5,4},{6,7},{7,6},{8,9},{9,8},{10,11... | collective-permute-start | bytes 4718600 | tf_op jit(solution)/shard_map/ppermute | solution.py:221
  2.6 10.7 %collective-permute-start.3 = (bf16[128,768]{1,0:T(8,128)(2,1)}, bf16[128,768]{1,0:T(8,128)(2,1)S(1)}, u32[]{:S(2)}, u32[]{:S(2)}) collective-permute-start(bf16[128,768]{1,0:T(8,128)(2,1)} %get-tuple-element.26), channel_id=1, source_target_pairs={{0,12},{4,8},{8,4},{12,0},{1,13},{5,9},{9,5},{13,1},{2,14},{6,10},... | collective-permute-start | bytes 589832 | tf_op jit(solution)/shard_map/ppermute | solution.py:218
  7.3 1.4 %collective-permute-start = (s32[1024]{0:T(1024)}, s32[1024]{0:T(1024)S(1)}, u32[]{:S(2)}, u32[]{:S(2)}) collective-permute-start(s32[1024]{0:T(1024)} %param.8), channel_id=1, source_target_pairs={{0,1},{1,0},{2,3},{3,2},{4,5},{5,4},{6,7},{7,6},{8,9},{9,8},{10,11... | collective-permute-start | bytes 12296 | tf_op jit(solution)/shard_map/ppermute | solution.py:221
  7.5 10.8 %collective-permute-start.5 = (bf16[128,768]{1,0:T(8,128)(2,1)}, bf16[128,768]{1,0:T(8,128)(2,1)S(1)}, u32[]{:S(2)}, u32[]{:S(2)}) collective-permute-start(bf16[128,768]{1,0:T(8,128)(2,1)} %get-tuple-element.28), channel_id=1, source_target_pairs={{0,4},{4,0},{8,12},{12,8},{1,5},{5,1},{9,13},{13,9},{2,6},{6,2},{1... | collective-permute-start | bytes 589832 | tf_op jit(solution)/shard_map/ppermute | solution.py:218
  8.7 1.3 %copy-start = (bf16[768,768]{1,0:T(8,128)(2,1)S(1)}, bf16[768,768]{1,0:T(8,128)(2,1)}, u32[]{:S(2)}) copy-start(bf16[768,768]{1,0:T(8,128)(2,1)} %projection_ref.7) | copy-start | bytes 3538948
  10.0 0.9 %copy-start.3 = (bf16[128,768]{1,0:T(8,128)(2,1)S(1)}, bf16[128,768]{1,0:T(8,128)(2,1)}, u32[]{:S(2)}) copy-start(bf16[128,768]{1,0:T(8,128)(2,1)} %get-tuple-element.21.piece_ref) | copy-start | bytes 589828
  10.9 2.4 %copy-start.1 = (bf16[768,768]{1,0:T(8,128)(2,1)S(1)}, bf16[768,768]{1,0:T(8,128)(2,1)}, u32[]{:S(2)}) copy-start(bf16[768,768]{1,0:T(8,128)(2,1)} %projection_ref.7) | copy-start | bytes 3538948
  10.9 4.5 %copy-start.2 = (bf16[768,1024]{1,0:T(8,128)(2,1)S(1)}, bf16[768,1024]{1,0:T(8,128)(2,1)}, u32[]{:S(2)}) copy-start(bf16[768,1024]{1,0:T(8,128)(2,1)} %slab_ref.1) | copy-start | bytes 4718596
  10.9 4.6 %copy-start.4 = (s32[1024]{0:T(1024)S(1)}, s32[1024]{0:T(1024)}, u32[]{:S(2)}) copy-start(s32[1024]{0:T(1024)} %param.8) | copy-start | bytes 12292
  11.3 11.1 %collective-permute-start.1 = (bf16[128,768]{1,0:T(8,128)(2,1)S(1)}, bf16[128,768]{1,0:T(8,128)(2,1)S(1)}, u32[]{:S(2)}, u32[]{:S(2)}) collective-permute-start(bf16[128,768]{1,0:T(8,128)(2,1)S(1)} %project.4.refs_0_), channel_id=1, source_target_pairs={{0,2},{1,3},{2,0},{3,1},{4,6},{5,7},{6,4},{7,5},{8,10},{9,11},{10,... | collective-permute-start | bytes 589832 | tf_op jit(solution)/shard_map/ppermute | solution.py:221
  12.9 12.1 %collective-permute-start.8 = (bf16[128,768]{1,0:T(8,128)(2,1)}, bf16[128,768]{1,0:T(8,128)(2,1)S(1)}, u32[]{:S(2)}, u32[]{:S(2)}) collective-permute-start(bf16[128,768]{1,0:T(8,128)(2,1)} %get-tuple-element.31), channel_id=1, source_target_pairs={{0,8},{4,12},{8,0},{12,4},{1,9},{5,13},{9,1},{13,5},{2,10},{6,14},... | collective-permute-start | bytes 589832 | tf_op jit(solution)/shard_map/ppermute | solution.py:218
  13.7 13.1 %collective-permute-start.4 = (bf16[128,768]{1,0:T(8,128)(2,1)S(1)}, bf16[128,768]{1,0:T(8,128)(2,1)S(1)}, u32[]{:S(2)}, u32[]{:S(2)}) collective-permute-start(bf16[128,768]{1,0:T(8,128)(2,1)S(1)} %project.5.refs_1_), channel_id=1, source_target_pairs={{0,2},{1,3},{2,0},{3,1},{4,6},{5,7},{6,4},{7,5},{8,10},{9,11},{10,... | collective-permute-start | bytes 589832 | tf_op jit(solution)/shard_map/ppermute | solution.py:221
  18.3 2.1 %copy-start.5 = (s32[1,256]{1,0:T(1,128)S(1)}, s32[1,256]{1,0:T(1,128)}, u32[]{:S(2)}) copy-start(s32[1,256]{1,0:T(1,128)} %get-tuple-element.20.after_ref.position_ref) | copy-start | bytes 3076
  18.8 14.5 %collective-permute-start.6 = (bf16[128,768]{1,0:T(8,128)(2,1)S(1)}, bf16[128,768]{1,0:T(8,128)(2,1)S(1)}, u32[]{:S(2)}, u32[]{:S(2)}) collective-permute-start(bf16[128,768]{1,0:T(8,128)(2,1)S(1)} %project.6.refs_1_), channel_id=1, source_target_pairs={{0,2},{1,3},{2,0},{3,1},{4,6},{5,7},{6,4},{7,5},{8,10},{9,11},{10,... | collective-permute-start | bytes 589832 | tf_op jit(solution)/shard_map/ppermute | solution.py:221
  25.4 8.9 %collective-permute-start.9 = (bf16[128,768]{1,0:T(8,128)(2,1)S(1)}, bf16[128,768]{1,0:T(8,128)(2,1)S(1)}, u32[]{:S(2)}, u32[]{:S(2)}) collective-permute-start(bf16[128,768]{1,0:T(8,128)(2,1)S(1)} %project.7.refs_1_), channel_id=1, source_target_pairs={{0,2},{1,3},{2,0},{3,1},{4,6},{5,7},{6,4},{7,5},{8,10},{9,11},{10,... | collective-permute-start | bytes 589832 | tf_op jit(solution)/shard_map/ppermute | solution.py:221
  27.9 10.6 %collective-permute-start.15 = (f32[128,128]{1,0:T(8,128)S(1)}, f32[128,128]{1,0:T(8,128)S(1)}, u32[]{:S(2)}, u32[]{:S(2)}) collective-permute-start(f32[128,128]{1,0:T(8,128)S(1)} %get-tuple-element.27.refs_0_), channel_id=1, source_target_pairs={{0,14},{1,15},{2,12},{3,13},{4,10},{5,11},{6,8},{7,9},{8,6},{9,7},... | collective-permute-start | bytes 196616 | tf_op jit(solution)/shard_map/ppermute | solution.py:229
  30.5 9.0 %collective-permute-start.14 = (f32[128,128]{1,0:T(8,128)S(1)}, f32[128,128]{1,0:T(8,128)S(1)}, u32[]{:S(2)}, u32[]{:S(2)}) collective-permute-start(f32[128,128]{1,0:T(8,128)S(1)} %get-tuple-element.34), channel_id=1, source_target_pairs={{0,12},{4,8},{8,4},{12,0},{1,13},{5,9},{9,5},{13,1},{2,14},{6,10},... | collective-permute-start | bytes 196616 | tf_op jit(solution)/shard_map/ppermute | solution.py:218
  31.8 9.7 %collective-permute-start.11 = (f32[128,128]{1,0:T(8,128)S(1)}, f32[128,128]{1,0:T(8,128)S(1)}, u32[]{:S(2)}, u32[]{:S(2)}) collective-permute-start(f32[128,128]{1,0:T(8,128)S(1)} %get-tuple-element.25.refs_0_), channel_id=1, source_target_pairs={{0,2},{1,3},{2,0},{3,1},{4,6},{5,7},{6,4},{7,5},{8,10},{9,11},{10,... | collective-permute-start | bytes 196616 | tf_op jit(solution)/shard_map/ppermute | solution.py:221
  34.2 10.6 %collective-permute-start.12 = (f32[128,128]{1,0:T(8,128)S(1)}, f32[128,128]{1,0:T(8,128)S(1)}, u32[]{:S(2)}, u32[]{:S(2)}) collective-permute-start(f32[128,128]{1,0:T(8,128)S(1)} %get-tuple-element.30.refs_0_), channel_id=1, source_target_pairs={{0,6},{1,7},{2,4},{3,5},{4,2},{5,3},{6,0},{7,1},{8,14},{9,15},{10,... | collective-permute-start | bytes 196616 | tf_op jit(solution)/shard_map/ppermute | solution.py:229
  35.3 6.2 %collective-permute-start.10 = (f32[128,128]{1,0:T(8,128)S(1)}, f32[128,128]{1,0:T(8,128)S(1)}, u32[]{:S(2)}, u32[]{:S(2)}) collective-permute-start(f32[128,128]{1,0:T(8,128)S(1)} %get-tuple-element.32), channel_id=1, source_target_pairs={{0,8},{4,12},{8,0},{12,4},{1,9},{5,13},{9,1},{13,5},{2,10},{6,14},... | collective-permute-start | bytes 196616 | tf_op jit(solution)/shard_map/ppermute | solution.py:218
  38.5 6.4 %collective-permute-start.13 = (f32[128,128]{1,0:T(8,128)S(1)}, f32[128,128]{1,0:T(8,128)S(1)}, u32[]{:S(2)}, u32[]{:S(2)}) collective-permute-start(f32[128,128]{1,0:T(8,128)S(1)} %get-tuple-element.33), channel_id=1, source_target_pairs={{0,10},{1,11},{2,8},{3,9},{4,14},{5,15},{6,12},{7,13},{8,2},{9,3},... | collective-permute-start | bytes 196616 | tf_op jit(solution)/shard_map/ppermute | solution.py:229
  39.5 5.4 %collective-permute-start.7 = (f32[128,128]{1,0:T(8,128)S(1)}, f32[128,128]{1,0:T(8,128)S(1)}, u32[]{:S(2)}, u32[]{:S(2)}) collective-permute-start(f32[128,128]{1,0:T(8,128)S(1)} %get-tuple-element.29), channel_id=1, source_target_pairs={{0,4},{4,0},{8,12},{12,8},{1,5},{5,1},{9,13},{13,9},{2,6},{6,2},{1... | collective-permute-start | bytes 196616 | tf_op jit(solution)/shard_map/ppermute | solution.py:218

commit v6 on v5

--- a/solution.py
+++ b/solution.py
@@ -244,7 +244,7 @@
 
     own_slab, fetched = sort_and_fetch(bins, vectors, other_slab)
     slabs_here = [own_slab, sort_slab(position, other_bins, fetched)]
-    cross(0, pieces[0], other_bins)
+    cross(0, pieces[0], own_slab)
     cross(1, arrived[1], own_slab)
     cross(3, arrived[3])
     done = scores(0)

time: 46.1 us -> 46 us (level)
  starting transfers between devices: 23 us -> 21.9 us
  waiting for transfers between devices: 7.33 us -> 8.41 us
    ppermute x6, waiting for transfers between devices: 2.83 us -> 7.59 us  [along_db(): return lax.ppermute(value, 'db', [(i, i ^ distance) for i in range(groups)])]
    ppermute x3, starting transfers between devices: 3.64 us -> 6.99 us  [along_both(): return lax.ppermute(value, ('db', 'blk'), pairs)]
    ppermute x3, waiting for transfers between devices: 3.34 us -> 0.81 us  [along_both(): return lax.ppermute(value, ('db', 'blk'), pairs)]
    ppermute x7, starting transfers between devices: 8.45 us -> 6.06 us  [along_blk(): return lax.ppermute(value, 'blk', [(i, i ^ distance) for i in range(slabs)])]
    ppermute x6, starting transfers between devices: 10.9 us -> 8.82 us  [along_db(): return lax.ppermute(value, 'db', [(i, i ^ distance) for i in range(groups)])]
    ppermute x7, waiting for transfers between devices: 1.16 us -> 0.02 us  [along_blk(): return lax.ppermute(value, 'blk', [(i, i ^ distance) for i in range(slabs)])]
  transfers between devices with their start and end apart: 16 -> 16, of which waited for: 5 -> 4; matrix products, arithmetic and copies ran while one was open for 0% -> 0% of each run, Pallas kernels for 27% -> 27%
where the time goes in v6:
time: 46 us; the launch traced here: 45.8 us
  starting transfers between devices  21.9 us (48%)
  Pallas kernels  13.2 us (29%)
  waiting for transfers between devices  8.41 us (18%)
  local copies, waits for them, and re-layouts  2.11 us (5%)
    ppermute x6, starting transfers between devices, along_db(): return lax.ppermute(value, 'db', [(i, i ^ distance) for i in range(groups)])  8.82 us
    ppermute x6, waiting for transfers between devices, along_db(): return lax.ppermute(value, 'db', [(i, i ^ distance) for i in range(groups)])  7.59 us
    ppermute x3, starting transfers between devices, along_both(): return lax.ppermute(value, ('db', 'blk'), pairs)  6.99 us
    ppermute x7, starting transfers between devices, along_blk(): return lax.ppermute(value, 'blk', [(i, i ^ distance) for i in range(slabs)])  6.06 us
    pallas_call x4, Pallas kernels, score(): pl.pallas_call(functools.partial(score_kernel, len(after), len(pieces)),...  4.03 us
    pallas_call x1, Pallas kernels, prepare(): pl.pallas_call(functools.partial(prepare_kernel, groups, capacity), out_s...  2.18 us
    unnamed x12, local copies, waits for them, and re-layouts  2.11 us
    pallas_call x1, Pallas kernels, sort_and_fetch(): pl.pallas_call(sort_and_fetch_kernel, out_shape=[jax.ShapeDtypeStruct(sla...  2.05 us
  transfers between devices with their start and end apart: 16, of which 4 were waited for; matrix products, arithmetic and copies ran while one was open for 0% of the time, Pallas kernels for 27%

profile of v6, /device:TPU:0, one launch (start us, length us, event | category | flops | bytes accessed | tf_op | source)
XLA Modules:
  0.0 45.8 jit_solution(15446959813457613545)
XLA Ops:
  0.0 0.5 collective-permute-start
  0.5 2.2 %prepare.1 = (s32[1,256]{1,0:T(1,128)}, bf16[128,768]{1,0:T(8,128)(2,1)}, bf16[128,768]{1,0:T(8,128)(2,1)}, bf16[128,768]{1,0:T(8,128)(2,1)}, bf16[128,768]{1,0:T(8,128)(2,1)}) custom-call(s32[1,256]{1,0:T(1,128)} %bitcast.5, bf16[256,768]{1,0:T(8,128)(2,1)} %queries_hbm.1), custom_call_target="tpu_custom_call" | custom-call | tf_op jit(solution)/shard_map/prepare/pallas_call | solution.py:84
  2.6 4.7 %collective-permute-start.3 = (bf16[128,768]{1,0:T(8,128)(2,1)}, bf16[128,768]{1,0:T(8,128)(2,1)S(1)}, u32[]{:S(2)}, u32[]{:S(2)}) collective-permute-start(bf16[128,768]{1,0:T(8,128)(2,1)} %get-tuple-element.26), channel_id=1, source_target_pairs={{0,12},{4,8},{8,4},{12,0},{1,13},{5,9},{9,5},{13,1},{2,14},{6,10},... | collective-permute-start | bytes 589832 | tf_op jit(solution)/shard_map/ppermute | solution.py:218
  7.3 0.0 collective-permute-start.5
  7.3 0.0 collective-permute-done.other_hbm
  7.3 1.4 %copy-done.1 = bf16[768,1024]{1,0:T(8,128)(2,1)S(1)} copy-done((bf16[768,1024]{1,0:T(8,128)(2,1)S(1)}, bf16[768,1024]{1,0:T(8,128)(2,1)}, u32[]{:S(2)}) %copy-start.1) | copy-done | bytes 1572888
  8.7 0.7 %copy-done.3 = s32[1024]{0:T(1024)S(1)} copy-done((s32[1024]{0:T(1024)S(1)}, s32[1024]{0:T(1024)}, u32[]{:S(2)}) %copy-start.3) | copy-done | bytes 4120
  9.4 2.0 %sort_and_fetch.1 = (bf16[768,1024]{1,0:T(8,128)(2,1)S(1)}, bf16[768,1024]{1,0:T(8,128)(2,1)S(1)}) custom-call(s32[1,1024]{1,0:T(1,128)S(1)} %bitcast.3, bf16[768,1024]{1,0:T(8,128)(2,1)S(1)} %copy-done.1, bf16[768,1024]{1,0:T(8,128)(2,1)} %collective-permute-done.other_hbm), custom_call_target="tpu_custom_call" | custom-call | tf_op jit(solution)/shard_map/sort_and_fetch/pallas_call | solution.py:134
  11.5 0.4 project.4.refs_0_
  11.9 1.6 %collective-permute-start.1 = (bf16[128,768]{1,0:T(8,128)(2,1)S(1)}, bf16[128,768]{1,0:T(8,128)(2,1)S(1)}, u32[]{:S(2)}, u32[]{:S(2)}) collective-permute-start(bf16[128,768]{1,0:T(8,128)(2,1)S(1)} %project.4.refs_0_), channel_id=1, source_target_pairs={{0,2},{1,3},{2,0},{3,1},{4,6},{5,7},{6,4},{7,5},{8,10},{9,11},{10,... | collective-permute-start | bytes 589832 | tf_op jit(solution)/shard_map/ppermute | solution.py:221
  13.5 0.8 %collective-permute-start.8 = (bf16[128,768]{1,0:T(8,128)(2,1)S(1)}, bf16[128,768]{1,0:T(8,128)(2,1)S(1)}, u32[]{:S(2)}, u32[]{:S(2)}) collective-permute-start(bf16[128,768]{1,0:T(8,128)(2,1)S(1)} %copy-done.5), channel_id=1, source_target_pairs={{0,8},{4,12},{8,0},{12,4},{1,9},{5,13},{9,1},{13,5},{2,10},{6,14},... | collective-permute-start | bytes 589832 | tf_op jit(solution)/shard_map/ppermute | solution.py:218
  14.3 0.0 collective-permute-done.3.piece_ref
  14.3 0.4 project.5.refs_1_
  14.7 0.0 copy-start.4
  14.7 0.7 %collective-permute-start.4 = (bf16[128,768]{1,0:T(8,128)(2,1)S(1)}, bf16[128,768]{1,0:T(8,128)(2,1)S(1)}, u32[]{:S(2)}, u32[]{:S(2)}) collective-permute-start(bf16[128,768]{1,0:T(8,128)(2,1)S(1)} %project.5.refs_1_), channel_id=1, source_target_pairs={{0,2},{1,3},{2,0},{3,1},{4,6},{5,7},{6,4},{7,5},{8,10},{9,11},{10,... | collective-permute-start | bytes 589832 | tf_op jit(solution)/shard_map/ppermute | solution.py:221
  15.5 0.0 collective-permute-start.2
  15.5 3.2 %collective-permute-done.5.piece_ref = bf16[128,768]{1,0:T(8,128)(2,1)S(1)} collective-permute-done((bf16[128,768]{1,0:T(8,128)(2,1)}, bf16[128,768]{1,0:T(8,128)(2,1)S(1)}, u32[]{:S(2)}, u32[]{:S(2)}) %collective-permute-start.5) | collective-permute-done | bytes 196640 | tf_op jit(solution)/shard_map/ppermute | solution.py:218
  18.6 0.4 project.6.refs_1_
  19.1 1.3 %collective-permute-start.6 = (bf16[128,768]{1,0:T(8,128)(2,1)S(1)}, bf16[128,768]{1,0:T(8,128)(2,1)S(1)}, u32[]{:S(2)}, u32[]{:S(2)}) collective-permute-start(bf16[128,768]{1,0:T(8,128)(2,1)S(1)} %project.6.refs_1_), channel_id=1, source_target_pairs={{0,2},{1,3},{2,0},{3,1},{4,6},{5,7},{6,4},{7,5},{8,10},{9,11},{10,... | collective-permute-start | bytes 589832 | tf_op jit(solution)/shard_map/ppermute | solution.py:221
  20.4 0.0 collective-permute-done.2
  20.4 2.0 %sort_slab.1.refs_3_.refs_4_ = bf16[768,1024]{1,0:T(8,128)(2,1)S(1)} custom-call(s32[1,256]{1,0:T(1,128)S(1)} %copy-done.4, s32[1,1024]{1,0:T(1,128)S(1)} %bitcast.4, bf16[768,1024]{1,0:T(8,128)(2,1)S(1)} %get-tuple-element.23.slab_ref), custom_call_target="tpu_custom_call" | custom-call | tf_op jit(solution)/shard_map/sort_slab/pallas_call | solution.py:116
  22.4 0.0 collective-permute-done.1.refs_1_
  22.4 1.0 %score.4 = (f32[128,128]{1,0:T(8,128)S(1)}, f32[128,128]{1,0:T(8,128)S(1)}) custom-call(bf16[128,768]{1,0:T(8,128)(2,1)S(1)} %project.4.refs_0_, bf16[128,768]{1,0:T(8,128)(2,1)S(1)} %collective-permute-done.1.refs_1_, bf16[768,1024]{1,0:T(8,128)(2,1)S(1)} %get-tuple-element.22.refs_0_.refs_2_.refs_3_, bf16[768,1024]{1,0:T(8,128)(2,1)S(1)} %sort_slab.1.refs_3_.refs_4_), custom_call_target="tpu_custom_call" | custom-call | tf_op jit(solution)/shard_map/score/pallas_call | solution.py:163
  23.5 1.9 %collective-permute-done.8.piece_ref = bf16[128,768]{1,0:T(8,128)(2,1)S(1)} collective-permute-done((bf16[128,768]{1,0:T(8,128)(2,1)S(1)}, bf16[128,768]{1,0:T(8,128)(2,1)S(1)}, u32[]{:S(2)}, u32[]{:S(2)}) %collective-permute-start.8) | collective-permute-done | bytes 196640 | tf_op jit(solution)/shard_map/ppermute | solution.py:218
  25.4 0.4 project.7.refs_1_
  25.8 1.0 %collective-permute-start.9 = (bf16[128,768]{1,0:T(8,128)(2,1)S(1)}, bf16[128,768]{1,0:T(8,128)(2,1)S(1)}, u32[]{:S(2)}, u32[]{:S(2)}) collective-permute-start(bf16[128,768]{1,0:T(8,128)(2,1)S(1)} %project.7.refs_1_), channel_id=1, source_target_pairs={{0,2},{1,3},{2,0},{3,1},{4,6},{5,7},{6,4},{7,5},{8,10},{9,11},{10,... | collective-permute-start | bytes 589832 | tf_op jit(solution)/shard_map/ppermute | solution.py:221
  26.9 0.0 collective-permute-done.4.refs_2_
  26.9 1.0 %score.5 = (f32[128,128]{1,0:T(8,128)S(1)}, f32[128,128]{1,0:T(8,128)S(1)}) custom-call(f32[128,128]{1,0:T(8,128)S(1)} %get-tuple-element.25.refs_0_, bf16[128,768]{1,0:T(8,128)(2,1)S(1)} %project.5.refs_1_, bf16[128,768]{1,0:T(8,128)(2,1)S(1)} %collective-permute-done.4.refs_2_, bf16[768,1024]{1,0:T(8,128)(2,1)S(1)} %get-tuple-element.22.refs_0_.refs_2_.refs_3_, ...), custom_call_target="tpu_custom_call" | custom-call | tf_op jit(solution)/shard_map/score/pallas_call | solution.py:163
  27.9 2.6 %collective-permute-start.14 = (f32[128,128]{1,0:T(8,128)S(1)}, f32[128,128]{1,0:T(8,128)S(1)}, u32[]{:S(2)}, u32[]{:S(2)}) collective-permute-start(f32[128,128]{1,0:T(8,128)S(1)} %get-tuple-element.34), channel_id=1, source_target_pairs={{0,12},{4,8},{8,4},{12,0},{1,13},{5,9},{9,5},{13,1},{2,14},{6,10},... | collective-permute-start | bytes 196616 | tf_op jit(solution)/shard_map/ppermute | solution.py:218
  30.5 1.8 %collective-permute-start.15 = (f32[128,128]{1,0:T(8,128)S(1)}, f32[128,128]{1,0:T(8,128)S(1)}, u32[]{:S(2)}, u32[]{:S(2)}) collective-permute-start(f32[128,128]{1,0:T(8,128)S(1)} %get-tuple-element.27.refs_0_), channel_id=1, source_target_pairs={{0,14},{1,15},{2,12},{3,13},{4,10},{5,11},{6,8},{7,9},{8,6},{9,7},... | collective-permute-start | bytes 196616 | tf_op jit(solution)/shard_map/ppermute | solution.py:229
  32.3 1.0 %collective-permute-start.11 = (f32[128,128]{1,0:T(8,128)S(1)}, f32[128,128]{1,0:T(8,128)S(1)}, u32[]{:S(2)}, u32[]{:S(2)}) collective-permute-start(f32[128,128]{1,0:T(8,128)S(1)} %get-tuple-element.25.refs_0_), channel_id=1, source_target_pairs={{0,2},{1,3},{2,0},{3,1},{4,6},{5,7},{6,4},{7,5},{8,10},{9,11},{10,... | collective-permute-start | bytes 196616 | tf_op jit(solution)/shard_map/ppermute | solution.py:221
  33.2 0.0 collective-permute-done.6.refs_2_
  33.2 1.0 %score.6 = (f32[128,128]{1,0:T(8,128)S(1)}, f32[128,128]{1,0:T(8,128)S(1)}) custom-call(f32[128,128]{1,0:T(8,128)S(1)} %get-tuple-element.27.refs_0_, bf16[128,768]{1,0:T(8,128)(2,1)S(1)} %project.6.refs_1_, bf16[128,768]{1,0:T(8,128)(2,1)S(1)} %collective-permute-done.6.refs_2_, bf16[768,1024]{1,0:T(8,128)(2,1)S(1)} %get-tuple-element.22.refs_0_.refs_2_.refs_3_, ...), custom_call_target="tpu_custom_call" | custom-call | tf_op jit(solution)/shard_map/score/pallas_call | solution.py:163
  34.2 0.1 collective-permute-start.7
  34.3 0.0 collective-permute-done.9.refs_2_
  34.3 2.5 %collective-permute-start.12 = (f32[128,128]{1,0:T(8,128)S(1)}, f32[128,128]{1,0:T(8,128)S(1)}, u32[]{:S(2)}, u32[]{:S(2)}) collective-permute-start(f32[128,128]{1,0:T(8,128)S(1)} %get-tuple-element.30.refs_0_), channel_id=1, source_target_pairs={{0,6},{1,7},{2,4},{3,5},{4,2},{5,3},{6,0},{7,1},{8,14},{9,15},{10,... | collective-permute-start | bytes 196616 | tf_op jit(solution)/shard_map/ppermute | solution.py:229
  36.8 1.0 %score.7 = (f32[128,128]{1,0:T(8,128)S(1)}, f32[128,128]{1,0:T(8,128)S(1)}) custom-call(f32[128,128]{1,0:T(8,128)S(1)} %get-tuple-element.30.refs_0_, bf16[128,768]{1,0:T(8,128)(2,1)S(1)} %project.7.refs_1_, bf16[128,768]{1,0:T(8,128)(2,1)S(1)} %collective-permute-done.9.refs_2_, bf16[768,1024]{1,0:T(8,128)(2,1)S(1)} %get-tuple-element.22.refs_0_.refs_2_.refs_3_, ...), custom_call_target="tpu_custom_call" | custom-call | tf_op jit(solution)/shard_map/score/pallas_call | solution.py:163
  37.8 0.0 collective-permute-done.14.refs_0_
  37.9 0.7 %collective-permute-start.10 = (f32[128,128]{1,0:T(8,128)S(1)}, f32[128,128]{1,0:T(8,128)S(1)}, u32[]{:S(2)}, u32[]{:S(2)}) collective-permute-start(f32[128,128]{1,0:T(8,128)S(1)} %get-tuple-element.32), channel_id=1, source_target_pairs={{0,8},{4,12},{8,0},{12,4},{1,9},{5,13},{9,1},{13,5},{2,10},{6,14},... | collective-permute-start | bytes 196616 | tf_op jit(solution)/shard_map/ppermute | solution.py:218
  38.6 0.0 collective-permute-done.15.refs_1_
  38.6 2.7 %collective-permute-start.13 = (f32[128,128]{1,0:T(8,128)S(1)}, f32[128,128]{1,0:T(8,128)S(1)}, u32[]{:S(2)}, u32[]{:S(2)}) collective-permute-start(f32[128,128]{1,0:T(8,128)S(1)} %get-tuple-element.33), channel_id=1, source_target_pairs={{0,10},{1,11},{2,8},{3,9},{4,14},{5,15},{6,12},{7,13},{8,2},{9,3},... | collective-permute-start | bytes 196616 | tf_op jit(solution)/shard_map/ppermute | solution.py:229
  41.3 0.2 select.2.refs_6_
  41.5 0.0 collective-permute-done.11.refs_3_
  41.5 0.0 collective-permute-done.7.refs_1_
  41.5 0.0 collective-permute-done.12.refs_4_
  41.5 2.5 %collective-permute-done.10.refs_2_ = f32[128,128]{1,0:T(8,128)S(1)} collective-permute-done((f32[128,128]{1,0:T(8,128)S(1)}, f32[128,128]{1,0:T(8,128)S(1)}, u32[]{:S(2)}, u32[]{:S(2)}) %collective-permute-start.10) | collective-permute-done | bytes 65568 | tf_op jit(solution)/shard_map/ppermute | solution.py:218
  44.0 0.8 %collective-permute-done.13.refs_5_ = f32[128,128]{1,0:T(8,128)S(1)} collective-permute-done((f32[128,128]{1,0:T(8,128)S(1)}, f32[128,128]{1,0:T(8,128)S(1)}, u32[]{:S(2)}, u32[]{:S(2)}) %collective-permute-start.13) | collective-permute-done | bytes 65568 | tf_op jit(solution)/shard_map/ppermute | solution.py:229
  44.8 1.0 %select.3 = f32[256,128]{1,0:T(8,128)} custom-call(s32[1,256]{1,0:T(1,128)S(1)} %copy-done.4, f32[128,128]{1,0:T(8,128)S(1)} %get-tuple-element.24.refs_0_, f32[128,128]{1,0:T(8,128)S(1)} %collective-permute-done.7.refs_1_, f32[128,128]{1,0:T(8,128)S(1)} %collective-permute-done.10.refs_2_, f32[128,128]{1,0:T(8,128)S(1)} %collective-permute-done.11.refs_3_, ...), custom_call_target="tpu_custom_call" | custom-call | tf_op jit(solution)/shard_map/select/pallas_call | solution.py:202
  (9 shorter events, 0.0 us)
Async XLA Ops:
  0.0 7.3 %collective-permute-start = (bf16[768,1024]{1,0:T(8,128)(2,1)}, bf16[768,1024]{1,0:T(8,128)(2,1)}, u32[]{:S(2)}, u32[]{:S(2)}) collective-permute-start(bf16[768,1024]{1,0:T(8,128)(2,1)} %slab_ref.1), channel_id=1, source_target_pairs={{0,1},{1,0},{2,3},{3,2},{4,5},{5,4},{6,7},{7,6},{8,9},{9,8},{10,11... | collective-permute-start | bytes 4718600 | tf_op jit(solution)/shard_map/ppermute | solution.py:221
  2.6 11.7 %collective-permute-start.3 = (bf16[128,768]{1,0:T(8,128)(2,1)}, bf16[128,768]{1,0:T(8,128)(2,1)S(1)}, u32[]{:S(2)}, u32[]{:S(2)}) collective-permute-start(bf16[128,768]{1,0:T(8,128)(2,1)} %get-tuple-element.26), channel_id=1, source_target_pairs={{0,12},{4,8},{8,4},{12,0},{1,13},{5,9},{9,5},{13,1},{2,14},{6,10},... | collective-permute-start | bytes 589832 | tf_op jit(solution)/shard_map/ppermute | solution.py:218
  7.3 11.3 %collective-permute-start.5 = (bf16[128,768]{1,0:T(8,128)(2,1)}, bf16[128,768]{1,0:T(8,128)(2,1)S(1)}, u32[]{:S(2)}, u32[]{:S(2)}) collective-permute-start(bf16[128,768]{1,0:T(8,128)(2,1)} %get-tuple-element.28), channel_id=1, source_target_pairs={{0,4},{4,0},{8,12},{12,8},{1,5},{5,1},{9,13},{13,9},{2,6},{6,2},{1... | collective-permute-start | bytes 589832 | tf_op jit(solution)/shard_map/ppermute | solution.py:218
  7.3 1.4 %copy-start.1 = (bf16[768,1024]{1,0:T(8,128)(2,1)S(1)}, bf16[768,1024]{1,0:T(8,128)(2,1)}, u32[]{:S(2)}) copy-start(bf16[768,1024]{1,0:T(8,128)(2,1)} %slab_ref.1) | copy-start | bytes 4718596
  8.7 0.7 %copy-start.3 = (s32[1024]{0:T(1024)S(1)}, s32[1024]{0:T(1024)}, u32[]{:S(2)}) copy-start(s32[1024]{0:T(1024)} %param.8) | copy-start | bytes 12292
  9.4 2.1 %copy-start = (bf16[768,768]{1,0:T(8,128)(2,1)S(1)}, bf16[768,768]{1,0:T(8,128)(2,1)}, u32[]{:S(2)}) copy-start(bf16[768,768]{1,0:T(8,128)(2,1)} %projection_ref.7) | copy-start | bytes 3538948
  9.4 2.1 %copy-start.2 = (bf16[128,768]{1,0:T(8,128)(2,1)S(1)}, bf16[128,768]{1,0:T(8,128)(2,1)}, u32[]{:S(2)}) copy-start(bf16[128,768]{1,0:T(8,128)(2,1)} %get-tuple-element.21.piece_ref) | copy-start | bytes 589828
  11.5 2.0 %copy-start.5 = (bf16[128,768]{1,0:T(8,128)(2,1)S(1)}, bf16[128,768]{1,0:T(8,128)(2,1)}, u32[]{:S(2)}) copy-start(bf16[128,768]{1,0:T(8,128)(2,1)} %get-tuple-element.31) | copy-start | bytes 589828
  11.9 10.5 %collective-permute-start.1 = (bf16[128,768]{1,0:T(8,128)(2,1)S(1)}, bf16[128,768]{1,0:T(8,128)(2,1)S(1)}, u32[]{:S(2)}, u32[]{:S(2)}) collective-permute-start(bf16[128,768]{1,0:T(8,128)(2,1)S(1)} %project.4.refs_0_), channel_id=1, source_target_pairs={{0,2},{1,3},{2,0},{3,1},{4,6},{5,7},{6,4},{7,5},{8,10},{9,11},{10,... | collective-permute-start | bytes 589832 | tf_op jit(solution)/shard_map/ppermute | solution.py:221
  13.5 11.9 %collective-permute-start.8 = (bf16[128,768]{1,0:T(8,128)(2,1)S(1)}, bf16[128,768]{1,0:T(8,128)(2,1)S(1)}, u32[]{:S(2)}, u32[]{:S(2)}) collective-permute-start(bf16[128,768]{1,0:T(8,128)(2,1)S(1)} %copy-done.5), channel_id=1, source_target_pairs={{0,8},{4,12},{8,0},{12,4},{1,9},{5,13},{9,1},{13,5},{2,10},{6,14},... | collective-permute-start | bytes 589832 | tf_op jit(solution)/shard_map/ppermute | solution.py:218
  14.7 5.7 %copy-start.4 = (s32[1,256]{1,0:T(1,128)S(1)}, s32[1,256]{1,0:T(1,128)}, u32[]{:S(2)}) copy-start(s32[1,256]{1,0:T(1,128)} %get-tuple-element.20.after_ref.position_ref) | copy-start | bytes 3076
  14.7 12.1 %collective-permute-start.4 = (bf16[128,768]{1,0:T(8,128)(2,1)S(1)}, bf16[128,768]{1,0:T(8,128)(2,1)S(1)}, u32[]{:S(2)}, u32[]{:S(2)}) collective-permute-start(bf16[128,768]{1,0:T(8,128)(2,1)S(1)} %project.5.refs_1_), channel_id=1, source_target_pairs={{0,2},{1,3},{2,0},{3,1},{4,6},{5,7},{6,4},{7,5},{8,10},{9,11},{10,... | collective-permute-start | bytes 589832 | tf_op jit(solution)/shard_map/ppermute | solution.py:221
  15.5 4.9 %collective-permute-start.2 = (s32[1024]{0:T(1024)S(1)}, s32[1024]{0:T(1024)S(1)}, u32[]{:S(2)}, u32[]{:S(2)}) collective-permute-start(s32[1024]{0:T(1024)S(1)} %copy-done.3), channel_id=1, source_target_pairs={{0,1},{1,0},{2,3},{3,2},{4,5},{5,4},{6,7},{7,6},{8,9},{9,8},{10,11... | collective-permute-start | bytes 12296 | tf_op jit(solution)/shard_map/ppermute | solution.py:221
  19.1 14.2 %collective-permute-start.6 = (bf16[128,768]{1,0:T(8,128)(2,1)S(1)}, bf16[128,768]{1,0:T(8,128)(2,1)S(1)}, u32[]{:S(2)}, u32[]{:S(2)}) collective-permute-start(bf16[128,768]{1,0:T(8,128)(2,1)S(1)} %project.6.refs_1_), channel_id=1, source_target_pairs={{0,2},{1,3},{2,0},{3,1},{4,6},{5,7},{6,4},{7,5},{8,10},{9,11},{10,... | collective-permute-start | bytes 589832 | tf_op jit(solution)/shard_map/ppermute | solution.py:221
  25.8 8.5 %collective-permute-start.9 = (bf16[128,768]{1,0:T(8,128)(2,1)S(1)}, bf16[128,768]{1,0:T(8,128)(2,1)S(1)}, u32[]{:S(2)}, u32[]{:S(2)}) collective-permute-start(bf16[128,768]{1,0:T(8,128)(2,1)S(1)} %project.7.refs_1_), channel_id=1, source_target_pairs={{0,2},{1,3},{2,0},{3,1},{4,6},{5,7},{6,4},{7,5},{8,10},{9,11},{10,... | collective-permute-start | bytes 589832 | tf_op jit(solution)/shard_map/ppermute | solution.py:221
  27.9 10.0 %collective-permute-start.14 = (f32[128,128]{1,0:T(8,128)S(1)}, f32[128,128]{1,0:T(8,128)S(1)}, u32[]{:S(2)}, u32[]{:S(2)}) collective-permute-start(f32[128,128]{1,0:T(8,128)S(1)} %get-tuple-element.34), channel_id=1, source_target_pairs={{0,12},{4,8},{8,4},{12,0},{1,13},{5,9},{9,5},{13,1},{2,14},{6,10},... | collective-permute-start | bytes 196616 | tf_op jit(solution)/shard_map/ppermute | solution.py:218
  30.5 8.1 %collective-permute-start.15 = (f32[128,128]{1,0:T(8,128)S(1)}, f32[128,128]{1,0:T(8,128)S(1)}, u32[]{:S(2)}, u32[]{:S(2)}) collective-permute-start(f32[128,128]{1,0:T(8,128)S(1)} %get-tuple-element.27.refs_0_), channel_id=1, source_target_pairs={{0,14},{1,15},{2,12},{3,13},{4,10},{5,11},{6,8},{7,9},{8,6},{9,7},... | collective-permute-start | bytes 196616 | tf_op jit(solution)/shard_map/ppermute | solution.py:229
  32.3 9.2 %collective-permute-start.11 = (f32[128,128]{1,0:T(8,128)S(1)}, f32[128,128]{1,0:T(8,128)S(1)}, u32[]{:S(2)}, u32[]{:S(2)}) collective-permute-start(f32[128,128]{1,0:T(8,128)S(1)} %get-tuple-element.25.refs_0_), channel_id=1, source_target_pairs={{0,2},{1,3},{2,0},{3,1},{4,6},{5,7},{6,4},{7,5},{8,10},{9,11},{10,... | collective-permute-start | bytes 196616 | tf_op jit(solution)/shard_map/ppermute | solution.py:221
  34.2 7.3 %collective-permute-start.7 = (f32[128,128]{1,0:T(8,128)S(1)}, f32[128,128]{1,0:T(8,128)S(1)}, u32[]{:S(2)}, u32[]{:S(2)}) collective-permute-start(f32[128,128]{1,0:T(8,128)S(1)} %get-tuple-element.29), channel_id=1, source_target_pairs={{0,4},{4,0},{8,12},{12,8},{1,5},{5,1},{9,13},{13,9},{2,6},{6,2},{1... | collective-permute-start | bytes 196616 | tf_op jit(solution)/shard_map/ppermute | solution.py:218
  34.3 7.2 %collective-permute-start.12 = (f32[128,128]{1,0:T(8,128)S(1)}, f32[128,128]{1,0:T(8,128)S(1)}, u32[]{:S(2)}, u32[]{:S(2)}) collective-permute-start(f32[128,128]{1,0:T(8,128)S(1)} %get-tuple-element.30.refs_0_), channel_id=1, source_target_pairs={{0,6},{1,7},{2,4},{3,5},{4,2},{5,3},{6,0},{7,1},{8,14},{9,15},{10,... | collective-permute-start | bytes 196616 | tf_op jit(solution)/shard_map/ppermute | solution.py:229
  37.9 6.2 %collective-permute-start.10 = (f32[128,128]{1,0:T(8,128)S(1)}, f32[128,128]{1,0:T(8,128)S(1)}, u32[]{:S(2)}, u32[]{:S(2)}) collective-permute-start(f32[128,128]{1,0:T(8,128)S(1)} %get-tuple-element.32), channel_id=1, source_target_pairs={{0,8},{4,12},{8,0},{12,4},{1,9},{5,13},{9,1},{13,5},{2,10},{6,14},... | collective-permute-start | bytes 196616 | tf_op jit(solution)/shard_map/ppermute | solution.py:218
  38.6 6.3 %collective-permute-start.13 = (f32[128,128]{1,0:T(8,128)S(1)}, f32[128,128]{1,0:T(8,128)S(1)}, u32[]{:S(2)}, u32[]{:S(2)}) collective-permute-start(f32[128,128]{1,0:T(8,128)S(1)} %get-tuple-element.33), channel_id=1, source_target_pairs={{0,10},{1,11},{2,8},{3,9},{4,14},{5,15},{6,12},{7,13},{8,2},{9,3},... | collective-permute-start | bytes 196616 | tf_op jit(solution)/shard_map/ppermute | solution.py:229
